TPU v7x, 512 devices: a whole 4x4x16 slice. The times are simulated.
512 devices in a mesh: dp: 8 (over z_lo), seq: 8 (over z_hi, y), head: 8 (over x, core).
Axes of the slice: x: 4, y: 4, z: 16 (z_hi: 2, z_lo: 8; z = z_hi * 8 + z_lo), core: 2. Of those that a mesh axis runs over, the one named last changes fastest.
Arguments:
- queries: bfloat16 [65536, 4096], P(('dp', 'seq', 'head')), parts along dimension 0, may hold values from -5 to 5
- stored_key_rows: bfloat16 [65536, 512], P(('dp', 'seq', 'head')), parts along dimension 0, may hold values from -5 to 5
- stored_value_rows: bfloat16 [65536, 512], P(('dp', 'seq', 'head')), parts along dimension 0, may hold values from -6 to 6
- grad_out: bfloat16 [65536, 4096], P(('dp', 'seq', 'head')), parts along dimension 0, may hold values from -6 to 6
- segment_ids: int32 [65536], P('dp'), parts along dimension 0, may hold values from 0 to 47, never falling along the last dimension, each value on 1 to 256 neighbouring positions
- stored_block_order: int32 [128], P('dp'), parts along dimension 0, may hold values from 0 to 15, each once
Outputs:
- attended: bfloat16 [65536, 4096], P(('dp', 'seq', 'head')), parts along dimension 0
- grad_query: bfloat16 [65536, 4096], P(('dp', 'seq', 'head')), parts along dimension 0
- key_gradient: bfloat16 [65536, 512], P(('dp', 'seq', 'head')), parts along dimension 0
- value_gradient: bfloat16 [65536, 512], P(('dp', 'seq', 'head')), parts along dimension 0
There are 8 independent parts, one for each index of `dp`. A program takes and returns all parts, laid end to end along the dimension named above; each array names one. Nothing has to cross between parts.
Inputs may be any that keep to these rules, and one draw needn't show every extreme that they name: `segment_ids`: indexed by sequence position, not by stored row; never falls; each document holds at most 256 positions, one exactly 256. Stored block j, rows j * 512 to j * 512 + 511, holds sequence block stored_block_order[j]; each block once.
All inputs are finite; a program needn't handle non-finite values.
Results may differ from a plain program's by a relative error of at most 0.019.
Values may be sent and summed in bfloat16 or wider, within the bound.
No kernel may reach another device: no remote copies, remote signals or barrier semaphores. Data moves between devices by JAX's collectives and lax.ppermute only.
A program may use at most 64 MiB of HBM per device.

v0:
```python
import math

import jax
import jax.numpy as jnp
from jax import lax
from jax.sharding import PartitionSpec as P

HEAD_SIZE = 128
QUERY_HEADS = 32
KEY_VALUE_HEADS = 4


def block_inverse(stored_block_order):
    count_of_blocks = stored_block_order.shape[0]
    slots = jnp.arange(count_of_blocks, dtype=jnp.int32)
    match = stored_block_order[:, None] == slots[None, :]
    return jnp.sum(jnp.where(match, slots[:, None], 0), axis=0)


def attend_block(block_id, query_block, grad_block, kv_blocks, own_slot, prior_slot, documents):
    rows_per_block, head_count, head_width = query_block.shape
    tile = rows_per_block // 2
    score_scale = 1.0 / math.sqrt(head_width)
    own_rows = lax.dynamic_index_in_dim(kv_blocks, own_slot, 0, keepdims=False)
    prior_rows = lax.dynamic_index_in_dim(kv_blocks, prior_slot, 0, keepdims=False)[
        rows_per_block - tile :
    ]
    extended = jnp.concatenate([prior_rows, own_rows], axis=0)
    prior_block = jnp.maximum(block_id - 1, 0)
    own_doc = lax.dynamic_index_in_dim(documents, block_id, 0, keepdims=False)
    prior_doc = lax.dynamic_index_in_dim(documents, prior_block, 0, keepdims=False)[
        rows_per_block - tile :
    ]
    prior_doc = jnp.where(block_id >= 1, prior_doc, -1)
    extended_doc = jnp.concatenate([prior_doc, own_doc], axis=0)
    extended_pos = (
        block_id * rows_per_block - tile + jnp.arange(rows_per_block + tile, dtype=jnp.int32)
    )
    band = jnp.stack([extended[tile * i : tile * (i + 2)] for i in range(2)], axis=0)
    band_doc = jnp.stack([extended_doc[tile * i : tile * (i + 2)] for i in range(2)], axis=0)
    band_pos = jnp.stack([extended_pos[tile * i : tile * (i + 2)] for i in range(2)], axis=0)
    key_band = band[:, :, :head_width]
    value_band = band[:, :, head_width:]
    query_tiles = query_block.reshape(2, tile, head_count, head_width)
    grad_tiles = grad_block.reshape(2, tile, head_count, head_width)
    query_pos = (block_id * rows_per_block + jnp.arange(rows_per_block, dtype=jnp.int32)).reshape(
        2, tile
    )
    query_doc = own_doc.reshape(2, tile)
    usable = (band_pos[:, None, :] <= query_pos[:, :, None]) & (
        band_doc[:, None, :] == query_doc[:, :, None]
    )
    usable = usable[:, None]
    scores = (
        jnp.einsum("tqhd,tkd->thqk", query_tiles, key_band, preferred_element_type=jnp.float32)
        * score_scale
    )
    masked = jnp.where(usable, scores, -jnp.inf)
    row_max = jnp.max(masked, axis=3)
    log_total = row_max + jnp.log(jnp.sum(jnp.exp(masked - row_max[..., None]), axis=3))
    weights = jnp.exp(jnp.where(usable, scores - log_total[..., None], -jnp.inf))
    weights16 = weights.astype(jnp.bfloat16)
    output = jnp.einsum(
        "thqk,tkd->tqhd", weights16, value_band, preferred_element_type=jnp.float32
    ).astype(jnp.bfloat16)
    delta = jnp.einsum("tqhd,tqhd->thq", grad_tiles, output, preferred_element_type=jnp.float32)
    dprob = jnp.einsum("tqhd,tkd->thqk", grad_tiles, value_band, preferred_element_type=jnp.float32)
    dscore = (weights * (dprob - delta[..., None]) * score_scale).astype(jnp.bfloat16)
    grad_rows = jnp.einsum(
        "thqk,tkd->tqhd", dscore, key_band, preferred_element_type=jnp.float32
    ).astype(jnp.bfloat16)
    grad_keys = jnp.einsum(
        "thqk,tqhd->tkd", dscore, query_tiles, preferred_element_type=jnp.float32
    )
    grad_values = jnp.einsum(
        "thqk,tqhd->tkd", weights16, grad_tiles, preferred_element_type=jnp.float32
    )
    band_grads = jnp.concatenate([grad_keys, grad_values], axis=2).reshape(
        2, 2, tile, 2 * head_width
    )
    prior_grad = band_grads[0, 0]
    own_grad = jnp.concatenate([band_grads[0, 1] + band_grads[1, 0], band_grads[1, 1]], axis=0)
    return (
        output.reshape(rows_per_block, head_count, head_width),
        grad_rows.reshape(rows_per_block, head_count, head_width),
        prior_grad,
        own_grad,
    )


def local(queries, stored_key_rows, stored_value_rows, grad_out, segment_ids, stored_block_order):
    number_of_heads = lax.axis_size("head")
    device_local_rows = queries.shape[0]
    per_dev = QUERY_HEADS // number_of_heads
    head_copies = number_of_heads // KEY_VALUE_HEADS
    count_of_blocks = stored_block_order.shape[0]
    rows_per_block = segment_ids.shape[0] // count_of_blocks
    tile = rows_per_block // 2
    seq_rank = lax.axis_index("seq")
    query_local, grad_local = (
        lax.all_to_all(queries, "head", split_axis=1, concat_axis=0, tiled=True),
        lax.all_to_all(grad_out, "head", split_axis=1, concat_axis=0, tiled=True),
    )
    key_value_pair = jnp.stack(
        [
            stored_key_rows.reshape(device_local_rows, KEY_VALUE_HEADS, HEAD_SIZE),
            stored_value_rows.reshape(device_local_rows, KEY_VALUE_HEADS, HEAD_SIZE),
        ],
        axis=2,
    )
    repeated = jnp.broadcast_to(
        key_value_pair[:, :, None], (device_local_rows, KEY_VALUE_HEADS, head_copies, 2, HEAD_SIZE)
    )
    repeated = repeated.reshape(device_local_rows, number_of_heads * 2 * HEAD_SIZE)
    kv_local = lax.all_to_all(repeated, "head", split_axis=1, concat_axis=0, tiled=True)
    kv_all = lax.all_gather(kv_local, "seq", axis=0, tiled=True)
    inverse_order = block_inverse(stored_block_order)
    kv_blocks = kv_all.reshape(count_of_blocks, rows_per_block, 2 * HEAD_SIZE)
    documents = segment_ids.reshape(count_of_blocks, rows_per_block)
    local_width = per_dev * HEAD_SIZE
    query_view = query_local.reshape(2, rows_per_block, per_dev, HEAD_SIZE)
    grad_view = grad_local.reshape(2, rows_per_block, per_dev, HEAD_SIZE)
    mine = lax.dynamic_slice_in_dim(stored_block_order, 2 * seq_rank, 2, 0)
    targets = mine - 1
    outputs = []
    gradients = []
    prior_grads = []
    own_grads = []
    for which_block in range(2):
        own_slot = 2 * seq_rank + which_block
        block_id = mine[which_block]
        prior_slot = jnp.take(inverse_order, jnp.maximum(targets[which_block], 0), axis=0)
        output_block, grad_block, prior_grad, own_grad = attend_block(
            block_id,
            query_view[which_block],
            grad_view[which_block],
            kv_blocks,
            own_slot,
            prior_slot,
            documents,
        )
        outputs.append(output_block)
        gradients.append(grad_block)
        prior_grads.append(prior_grad)
        own_grads.append(own_grad)
    attended_local = jnp.stack(outputs, axis=0).reshape(2 * rows_per_block, local_width)
    grad_query_local = jnp.stack(gradients, axis=0).reshape(2 * rows_per_block, local_width)
    own_first = (
        own_grads[0]
        .at[rows_per_block - tile :]
        .add(jnp.where(targets[1] == mine[0], prior_grads[1], 0.0))
    )
    own_second = (
        own_grads[1]
        .at[rows_per_block - tile :]
        .add(jnp.where(targets[0] == mine[1], prior_grads[0], 0.0))
    )
    own_total = jnp.stack([own_first, own_second], axis=0)
    send_mask = jnp.stack(
        [(targets[0] >= 0) & (targets[0] != mine[1]), (targets[1] >= 0) & (targets[1] != mine[0])]
    )
    full_rows = jnp.zeros((count_of_blocks, rows_per_block, 2 * HEAD_SIZE), jnp.bfloat16)
    full_rows = lax.dynamic_update_slice_in_dim(
        full_rows, own_total.astype(jnp.bfloat16), 2 * seq_rank, 0
    )
    for which_block in range(2):
        target_slot = jnp.take(inverse_order, jnp.maximum(targets[which_block], 0), axis=0)
        corner = (target_slot, jnp.int32(rows_per_block - tile), jnp.int32(0))
        existing = lax.dynamic_slice(full_rows, corner, (1, tile, 2 * HEAD_SIZE))
        piece = jnp.where(
            send_mask[which_block], prior_grads[which_block].astype(jnp.bfloat16)[None], existing
        )
        full_rows = lax.dynamic_update_slice(full_rows, piece, corner)
    flat_rows = full_rows.reshape(count_of_blocks * rows_per_block, 2 * HEAD_SIZE).astype(
        jnp.float32
    )
    shares = lax.psum_scatter(
        flat_rows.astype(jnp.bfloat16), "seq", scatter_dimension=0, tiled=True
    ).astype(jnp.float32)
    returned_result = lax.all_to_all(
        shares.astype(jnp.bfloat16), "head", split_axis=0, concat_axis=1, tiled=True
    ).astype(shares.dtype)
    combined_result = jnp.sum(
        returned_result.reshape(device_local_rows, KEY_VALUE_HEADS, head_copies, 2, HEAD_SIZE),
        axis=2,
    )
    key_gradient = (
        combined_result[:, :, 0]
        .reshape(device_local_rows, KEY_VALUE_HEADS * HEAD_SIZE)
        .astype(jnp.bfloat16)
    )
    value_gradient = (
        combined_result[:, :, 1]
        .reshape(device_local_rows, KEY_VALUE_HEADS * HEAD_SIZE)
        .astype(jnp.bfloat16)
    )
    attended, grad_query = (
        lax.all_to_all(attended_local, "head", split_axis=0, concat_axis=1, tiled=True),
        lax.all_to_all(grad_query_local, "head", split_axis=0, concat_axis=1, tiled=True),
    )
    return (attended, grad_query, key_gradient, value_gradient)


def solution(mesh):
    return jax.shard_map(
        local,
        mesh=mesh,
        in_specs=(
            P(("dp", "seq", "head"), None),
            P(("dp", "seq", "head"), None),
            P(("dp", "seq", "head"), None),
            P(("dp", "seq", "head"), None),
            P("dp"),
            P("dp"),
        ),
        out_specs=(
            P(("dp", "seq", "head"), None),
            P(("dp", "seq", "head"), None),
            P(("dp", "seq", "head"), None),
            P(("dp", "seq", "head"), None),
        ),
        check_vma=False,
    )
```

profile of v0, /device:TPU:1, one launch (start us, length us, event | category | flops | bytes accessed | tf_op | source)
XLA Modules:
  0.0 489.6 jit_solution(3927054780133933813)
XLA Ops:
  10.3 19.3 %all_to_all.102 = bf16[128,8,256]{2,0,1:T(8,128)(2,1)} all-to-all(bf16[128,8,256]{2,0,1:T(8,128)(2,1)S(1)} %all_to_all.76), channel_id=1, replica_groups=mesh['dp'=8,'seq'=8,'head'=8] {'head'}, dimensions={1} | all-to-all | bytes 1048576 | tf_op jit(solution)/shard_map/all_to_all | solution.py:115
  29.7 1.1 copy.293
  30.7 4.5 all-to-all-start.1
  54.8 1.1 copy.292
  55.9 4.8 all-to-all-start.3
  60.8 1.0 compare_and_fusion.1
  61.8 1.0 compare_and_fusion
  63.1 1.1 copy.223
  64.5 11.4 %all-to-all-done.3 = bf16[128,8,512]{2,0,1:T(8,128)(2,1)S(1)} async-done(((bf16[128,8,512]{2,0,1:T(8,128)(2,1)}), bf16[128,8,512]{2,0,1:T(8,128)(2,1)S(1)}, u32[]{:S(2)}, u32[]{:S(2)}) %all-to-all-start.3) | async-done | bytes 1048608 | tf_op jit(solution)/shard_map/all_to_all | solution.py:102
  76.2 1.1 copy.225
  77.7 129.6 %all-gather.2.cloned.1.call-done = bf16[8192,256]{1,0:T(8,128)(2,1)} async-done(((bf16[1024,256]{1,0:T(8,128)(2,1)}), bf16[8192,256]{1,0:T(8,128)(2,1)}) %all-gather.2.cloned.1.call-update) | async-done | bytes 4194320 | tf_op jit(solution)/shard_map/all_gather | solution.py:116
  207.2 1.1 constant_dynamic-slice_fusion.3
  208.3 1.1 dynamic-slice_bitcast_fusion.1
  211.2 2.4 bitcast_convert_fusion
  213.5 2.1 convolution_bitcast_fusion
  215.7 1.6 copy.266
  218.0 3.8 fusion.2
  222.7 1.0 pad_maximum_fusion.3
  223.7 1.6 copy.287
  226.1 2.0 fusion.10
  229.0 2.6 bitcast_convert_fusion.1
  231.6 2.1 convolution_bitcast_fusion.2
  233.8 2.5 copy.256
  236.3 2.7 multiply_reduce_fusion.1
  239.0 1.1 copy.257
  240.0 3.9 fusion.5
  244.0 1.3 copy-done.2
  247.2 2.5 copy.286
  249.7 1.1 fusion.21
  251.8 1.1 bitcast_dynamic-update-slice_fusion.1
  252.9 2.4 broadcast_in_dim.92
  256.1 1.7 fusion.31
  257.8 1.6 fusion.28
  259.4 1.3 copy.208
  260.8 1.3 copy.204
  263.0 1.2 all_to_all.83
  264.2 5.3 %all-to-all-start.2 = ((bf16[8,128,512]{2,1,0:T(8,128)(2,1)}), bf16[8,128,512]{2,1,0:T(8,128)(2,1)S(1)}, u32[]{:S(2)}, u32[]{:S(2)}) async-start(bf16[8,128,512]{2,1,0:T(8,128)(2,1)} %all_to_all.83), calls=%async_computation.2 | async-start | bytes 2097152 | tf_op jit(solution)/shard_map/all_to_all | solution.py:198
  269.6 2.3 fusion.15
  271.8 1.3 copy.219
  273.1 2.2 fusion.14
  276.9 7.8 %all-to-all-done.2 = bf16[8,128,512]{2,1,0:T(8,128)(2,1)S(1)} async-done(((bf16[8,128,512]{2,1,0:T(8,128)(2,1)}), bf16[8,128,512]{2,1,0:T(8,128)(2,1)S(1)}, u32[]{:S(2)}, u32[]{:S(2)}) %all-to-all-start.2) | async-done | bytes 1048608 | tf_op jit(solution)/shard_map/all_to_all | solution.py:198
  284.8 18.6 %all_to_all.103 = bf16[8,128,512]{2,1,0:T(8,128)(2,1)S(1)} all-to-all(bf16[8,128,512]{2,1,0:T(8,128)(2,1)S(1)} %all_to_all.90), channel_id=1, replica_groups=mesh['dp'=8,'seq'=8,'head'=8] {'head'}, dimensions={0} | all-to-all | bytes 2097152 | tf_op jit(solution)/shard_map/all_to_all | solution.py:199
  303.4 159.4 %reduce-scatter.2.cloned.1.call-done = bf16[1024,256]{1,0:T(8,128)(2,1)} async-done(((bf16[8192,256]{1,0:T(8,128)(2,1)}), bf16[1024,256]{1,0:T(8,128)(2,1)}) %reduce-scatter.2.cloned.1.call-update) | async-done | bytes 524304 | tf_op jit(solution)/shard_map/reduce_scatter | solution.py:177
  462.8 6.1 %all-to-all-start.5 = ((bf16[8,128,256]{2,1,0:T(8,128)(2,1)}), bf16[8,128,256]{2,1,0:T(8,128)(2,1)}, u32[]{:S(2)}, u32[]{:S(2)}) async-start(bf16[8,128,256]{2,1,0:T(8,128)(2,1)} %bitcast.258), calls=%async_computation.6 | async-start | bytes 1048576 | tf_op jit(solution)/shard_map/all_to_all | solution.py:180
  469.5 1.3 copy.240
  471.5 1.3 copy.241
  472.8 5.6 %all-to-all-done.5 = bf16[8,128,256]{2,1,0:T(8,128)(2,1)} async-done(((bf16[8,128,256]{2,1,0:T(8,128)(2,1)}), bf16[8,128,256]{2,1,0:T(8,128)(2,1)}, u32[]{:S(2)}, u32[]{:S(2)}) %all-to-all-start.5) | async-done | bytes 524320 | tf_op jit(solution)/shard_map/all_to_all | solution.py:180
  478.4 1.2 convert_element_type.102
  (110 shorter events, 22.7 us)
Async XLA Ops:
  7.2 22.5 %copy-start.10 = (bf16[128,4096]{1,0:T(8,128)(2,1)S(1)}, bf16[128,4096]{1,0:T(8,128)(2,1)}, u32[]{:S(2)}) copy-start(bf16[128,4096]{1,0:T(8,128)(2,1)} %param.10) | copy-start | bytes 3145732
  7.2 200.0 %all-gather.2.cloned.1.call-start = ((), (), s32[]{:S(2)}) async-start(), calls=%async_computation.7 | async-start | bytes 4718592 | tf_op jit(solution)/shard_map/all_gather | solution.py:116
  9.4 25.9 %copy-start.18 = (s32[16]{0:T(128)S(1)}, s32[16]{0:T(128)}, u32[]{:S(2)}) copy-start(s32[16]{0:T(128)} %param.15) | copy-start | bytes 196
  9.4 32.4 %copy-start.17 = (s32[8192]{0:T(1024)S(1)}, s32[8192]{0:T(1024)}, u32[]{:S(2)}) copy-start(s32[8192]{0:T(1024)} %param.14) | copy-start | bytes 98308
  9.4 45.4 %copy-start.11 = (bf16[128,4096]{1,0:T(8,128)(2,1)S(1)}, bf16[128,4096]{1,0:T(8,128)(2,1)}, u32[]{:S(2)}) copy-start(bf16[128,4096]{1,0:T(8,128)(2,1)} %param.13) | copy-start | bytes 3145732
  30.7 25.2 %all-to-all-start.1 = ((bf16[128,8,512]{2,0,1:T(8,128)(2,1)}), bf16[128,8,512]{2,0,1:T(8,128)(2,1)S(1)}, u32[]{:S(2)}, u32[]{:S(2)}) async-start(bf16[128,8,512]{2,0,1:T(8,128)(2,1)} %bitcast.226), calls=%async_computation.1 | async-start | bytes 2097152 | tf_op jit(solution)/shard_map/all_to_all | solution.py:101
  55.9 20.0 %all-to-all-start.3 = ((bf16[128,8,512]{2,0,1:T(8,128)(2,1)}), bf16[128,8,512]{2,0,1:T(8,128)(2,1)S(1)}, u32[]{:S(2)}, u32[]{:S(2)}) async-start(bf16[128,8,512]{2,0,1:T(8,128)(2,1)} %bitcast.225), calls=%async_computation.3 | async-start | bytes 2097152 | tf_op jit(solution)/shard_map/all_to_all | solution.py:102
  60.7 402.0 %reduce-scatter.2.cloned.1.call-start = ((), (), s32[]{:S(2)}) async-start(), calls=%async_computation.8 | async-start | bytes 4718592 | tf_op jit(solution)/shard_map/reduce_scatter | solution.py:177
  76.0 133.4 %copy-start.9 = (pred[2,256,512]{1,2,0:T(8,128)(4,1)S(1)}, pred[2,256,512]{1,2,0:T(8,128)(4,1)}, u32[]{:S(2)}) copy-start(pred[2,256,512]{1,2,0:T(8,128)(4,1)} %compare_and_fusion) | copy-start | bytes 786436
  76.2 134.0 %copy-start.3 = (bf16[2,256,4,128]{3,2,1,0:T(4,128)(2,1)}, bf16[2,256,4,128]{3,2,1,0:T(4,128)(2,1)S(1)}, u32[]{:S(2)}) copy-start(bf16[2,256,4,128]{3,2,1,0:T(4,128)(2,1)S(1)} %reshape_squeeze.16) | copy-start | bytes 1572868
  77.6 135.9 %copy-start.13 = (bf16[2,256,4,128]{1,3,2,0:T(8,128)(2,1)}, bf16[2,256,4,128]{1,3,2,0:T(8,128)(2,1)S(1)}, u32[]{:S(2)}) copy-start(bf16[2,256,4,128]{1,3,2,0:T(8,128)(2,1)S(1)} %copy.232) | copy-start | bytes 1572868
  208.3 9.7 %copy-start.5 = (bf16[1,512,256]{2,1,0:T(8,128)(2,1)}, bf16[1,512,256]{2,1,0:T(8,128)(2,1)S(1)}, u32[]{:S(2)}) copy-start(bf16[1,512,256]{2,1,0:T(8,128)(2,1)S(1)} %get-tuple-element.75) | copy-start | bytes 786436
  209.4 8.6 %copy-start.6 = (bf16[1,512,256]{2,1,0:T(8,128)(2,1)}, bf16[1,512,256]{2,1,0:T(8,128)(2,1)S(1)}, u32[]{:S(2)}) copy-start(bf16[1,512,256]{2,1,0:T(8,128)(2,1)S(1)} %fusion.23) | copy-start | bytes 786436
  210.2 3.3 copy-start
  218.0 4.7 copy-start.15
  225.3 2.8 copy-start.7
  226.1 3.0 copy-start.8
  228.1 3.5 copy-start.1
  229.0 2.6 copy-start.12
  240.0 5.3 %copy-start.4 = (bf16[2,256,4,128]{1,3,2,0:T(8,128)(2,1)S(1)}, bf16[2,256,4,128]{1,3,2,0:T(8,128)(2,1)}, u32[]{:S(2)}) copy-start(bf16[2,256,4,128]{1,3,2,0:T(8,128)(2,1)} %copy.223) | copy-start | bytes 1572868
  240.0 6.1 %copy-start.16 = (f32[2,512,128]{1,2,0:T(8,128)S(1)}, f32[2,512,128]{1,2,0:T(8,128)}, u32[]{:S(2)}) copy-start(f32[2,512,128]{1,2,0:T(8,128)} %convolution_bitcast_fusion.2) | copy-start | bytes 1572868
  244.0 1.4 copy-start.2
  245.3 5.5 %copy-start.14 = (bf16[256,256]{1,0:T(8,128)(2,1)S(1)}, bf16[256,256]{1,0:T(8,128)(2,1)}, u32[]{:S(2)}) copy-start(bf16[256,256]{1,0:T(8,128)(2,1)} %get-tuple-element.80) | copy-start | bytes 393220
  264.2 20.5 %all-to-all-start.2 = ((bf16[8,128,512]{2,1,0:T(8,128)(2,1)}), bf16[8,128,512]{2,1,0:T(8,128)(2,1)S(1)}, u32[]{:S(2)}, u32[]{:S(2)}) async-start(bf16[8,128,512]{2,1,0:T(8,128)(2,1)} %all_to_all.83), calls=%async_computation.2 | async-start | bytes 2097152 | tf_op jit(solution)/shard_map/all_to_all | solution.py:198
  462.8 15.6 %all-to-all-start.5 = ((bf16[8,128,256]{2,1,0:T(8,128)(2,1)}), bf16[8,128,256]{2,1,0:T(8,128)(2,1)}, u32[]{:S(2)}, u32[]{:S(2)}) async-start(bf16[8,128,256]{2,1,0:T(8,128)(2,1)} %bitcast.258), calls=%async_computation.6 | async-start | bytes 1048576 | tf_op jit(solution)/shard_map/all_to_all | solution.py:180
Sparse Core Ops, SparseCore 0:
  29.8 177.3 all-gather.1
  259.6 203.1 reduce-scatter.1
where the time goes:
time: 491 us; the launch traced here: 490 us
  waiting for transfers between devices  314 us (64%)
  local copies, waits for them, and re-layouts  40.8 us (8%)
  blocking collectives  37.9 us (8%)
  between operations  31.4 us (6%)
  matrix products  25.8 us (5%)
  starting transfers between devices  20.8 us (4%)
  other arithmetic  19.1 us (4%)
    reduce_scatter x1, waiting for transfers between devices, local(): lax.psum_scatter(flat_rows.astype(jnp.bfloat16), 'seq', scatter_dimension...  159 us
    all_gather x1, waiting for transfers between devices, local(): kv_all = lax.all_gather(kv_local, 'seq', axis=0, tiled=True)  130 us
    all_to_all x1, blocking collectives, local(): lax.all_to_all(repeated, 'head', split_axis=1, concat_axis=0, tiled=True)  19.3 us
    all_to_all x1, blocking collectives, local(): lax.all_to_all(grad_query_local, 'head', split_axis=0, concat_axis=1, til...  18.6 us
    all_to_all x1, waiting for transfers between devices, local(): lax.all_to_all(grad_out, 'head', split_axis=1, concat_axis=0, tiled=True)  11.4 us
  transfers between devices with their start and end apart: 6, of which 5 were waited for; matrix products, arithmetic and copies ran while one was open for 5% of the time, Pallas kernels for 0%

commit v1 on v0

v1 whole, which is shorter than its diff:
```python
import functools
import math

import jax
import jax.numpy as jnp
from jax import lax
from jax.experimental import pallas as pl
from jax.experimental.pallas import tpu as pltpu
from jax.sharding import PartitionSpec as P

HEAD_SIZE = 128
QUERY_HEADS = 32
KEY_VALUE_HEADS = 4
GROUP = QUERY_HEADS // KEY_VALUE_HEADS
CHUNK = 128
WINDOW = 3 * CHUNK
KV_WIDTH = KEY_VALUE_HEADS * HEAD_SIZE
AXES = ("seq", "head")


def attend_kernel(
    info_ref,
    segments_ref,
    query_ref,
    grad_ref,
    key_far_ref,
    value_far_ref,
    key_near_ref,
    value_near_ref,
    key_own_ref,
    value_own_ref,
    out_ref,
    grad_query_ref,
    far_key_ref,
    far_value_ref,
    near_key_ref,
    near_value_ref,
    own_key_ref,
    own_value_ref,
    bias_ref,
):
    @pl.when(pl.program_id(0) == 0)
    def _():
        chunk = info_ref[0]
        own_row = segments_ref[pl.ds(chunk, 1), :]
        query_doc = jnp.broadcast_to(own_row, (CHUNK, CHUNK))
        for back in (2, 1, 0):
            at = chunk - back
            row = segments_ref[pl.ds(jnp.maximum(at, 0), 1), :]
            row = jnp.where(at >= 0, row, -1)
            key_doc = jnp.broadcast_to(row, (CHUNK, CHUNK)).T
            usable = key_doc == query_doc
            if back == 0:
                usable &= lax.broadcasted_iota(jnp.int32, (CHUNK, CHUNK), 0) <= (
                    lax.broadcasted_iota(jnp.int32, (CHUNK, CHUNK), 1)
                )
            tile = jnp.where(usable, 0.0, -jnp.inf).astype(jnp.float32)
            rows = pl.ds((2 - back) * CHUNK, CHUNK)
            bias_ref[rows, 0:CHUNK] = tile
            bias_ref[rows, CHUNK : 2 * CHUNK] = tile

    scale = 1.0 / math.sqrt(HEAD_SIZE)
    keys = jnp.concatenate([key_far_ref[...], key_near_ref[...], key_own_ref[...]], axis=0)
    values = jnp.concatenate([value_far_ref[...], value_near_ref[...], value_own_ref[...]], axis=0)
    keys_t = keys.T
    values_t = values.T
    last = (((1,), (1,)), ((), ()))
    plain = (((1,), (0,)), ((), ()))
    weight_parts, dscore_parts, query_parts, grad_parts = [], [], [], []
    for pair in range(GROUP // 2):
        heads = (2 * pair, 2 * pair + 1)
        queries = jnp.concatenate(
            [query_ref[:, a * HEAD_SIZE : (a + 1) * HEAD_SIZE] for a in heads], axis=0
        )
        grads = jnp.concatenate(
            [grad_ref[:, a * HEAD_SIZE : (a + 1) * HEAD_SIZE] for a in heads], axis=0
        )
        scores = lax.dot_general(keys, queries, last, preferred_element_type=jnp.float32)
        scores = scores + bias_ref[...]
        top = jnp.max(scores, axis=0, keepdims=True)
        raised = jnp.exp2((scores - top) * (scale * math.log2(math.e)))
        weights = raised * (1.0 / jnp.sum(raised, axis=0, keepdims=True))
        weights16 = weights.astype(jnp.bfloat16)
        dprob = lax.dot_general(values, grads, last, preferred_element_type=jnp.float32)
        product = weights * dprob
        delta = jnp.sum(product, axis=0, keepdims=True)
        dscore = ((product - weights * delta) * scale).astype(jnp.bfloat16)
        output_t = lax.dot_general(values_t, weights16, plain, preferred_element_type=jnp.float32)
        grad_query_t = lax.dot_general(keys_t, dscore, plain, preferred_element_type=jnp.float32)
        for i, a in enumerate(heads):
            columns = slice(a * HEAD_SIZE, (a + 1) * HEAD_SIZE)
            part = slice(i * CHUNK, (i + 1) * CHUNK)
            out_ref[:, columns] = output_t[:, part].T.astype(jnp.bfloat16)
            grad_query_ref[:, columns] = grad_query_t[:, part].T.astype(jnp.bfloat16)
        weight_parts.append(weights16)
        dscore_parts.append(dscore)
        query_parts.append(queries)
        grad_parts.append(grads)
    grad_keys = lax.dot_general(
        jnp.concatenate(dscore_parts, axis=1),
        jnp.concatenate(query_parts, axis=0),
        plain,
        preferred_element_type=jnp.float32,
    )
    grad_values = lax.dot_general(
        jnp.concatenate(weight_parts, axis=1),
        jnp.concatenate(grad_parts, axis=0),
        plain,
        preferred_element_type=jnp.float32,
    )
    far_key_ref[...] = grad_keys[:CHUNK].astype(jnp.bfloat16)
    near_key_ref[...] = grad_keys[CHUNK : 2 * CHUNK].astype(jnp.bfloat16)
    own_key_ref[...] = grad_keys[2 * CHUNK :]
    far_value_ref[...] = grad_values[:CHUNK].astype(jnp.bfloat16)
    near_value_ref[...] = grad_values[CHUNK : 2 * CHUNK].astype(jnp.bfloat16)
    own_value_ref[...] = grad_values[2 * CHUNK :]


def attend(chunk, segments, queries, grads, far, near, own):
    rows = queries.shape[0]
    wide = pl.BlockSpec((rows, GROUP * HEAD_SIZE), lambda g, info: (0, g))
    narrow = pl.BlockSpec((rows, HEAD_SIZE), lambda g, info: (0, g))
    half = jax.ShapeDtypeStruct((rows, KV_WIDTH), jnp.bfloat16)
    full = jax.ShapeDtypeStruct((rows, KV_WIDTH), jnp.float32)
    products = 6 * 2 * rows * QUERY_HEADS * WINDOW * HEAD_SIZE
    return pl.pallas_call(
        attend_kernel,
        grid_spec=pltpu.PrefetchScalarGridSpec(
            num_scalar_prefetch=1,
            grid=(KEY_VALUE_HEADS,),
            in_specs=[
                pl.BlockSpec(segments.shape, lambda g, info: (0, 0)),
                wide,
                wide,
                narrow,
                narrow,
                narrow,
                narrow,
                narrow,
                narrow,
            ],
            out_specs=[wide, wide] + [narrow] * 6,
            scratch_shapes=[pltpu.VMEM((WINDOW, 2 * CHUNK), jnp.float32)],
        ),
        out_shape=[
            jax.ShapeDtypeStruct(queries.shape, jnp.bfloat16),
            jax.ShapeDtypeStruct(queries.shape, jnp.bfloat16),
            half,
            half,
            half,
            half,
            full,
            full,
        ],
        compiler_params=pltpu.CompilerParams(vmem_limit_bytes=48 * 1024 * 1024),
        cost_estimate=pl.CostEstimate(
            flops=products,
            bytes_accessed=8 * rows * QUERY_HEADS * HEAD_SIZE,
            transcendentals=rows * QUERY_HEADS * WINDOW,
        ),
    )(chunk, segments, queries, grads, *far, *near, *own)


def within_block(moves):
    return [
        (s * 8 + b * 4 + source, s * 8 + b * 4 + target)
        for s in range(8)
        for b in range(2)
        for source, target in moves
    ]


def to_seq(value, mask):
    if mask == 0:
        return value
    return lax.ppermute(value, "seq", [(s, s ^ mask) for s in range(8)])


def to_plane(value, mask):
    if mask == 0:
        return value
    return lax.ppermute(
        value,
        AXES,
        [(s * 8 + h, (s ^ (mask >> 1)) * 8 + (h ^ ((mask & 1) * 4))) for s in range(8) for h in range(8)],
    )


def pick(stack, index):
    return lax.dynamic_index_in_dim(stack, index, 0, keepdims=False)


def local(queries, keys, values, grads, segment_ids, order):
    s = lax.axis_index("seq")
    h = lax.axis_index("head")
    z, y = s // 4, s % 4
    block, c = h // 4, h % 4
    count = order.shape[0]
    slots = jnp.arange(count, dtype=jnp.int32)
    step = order[:, None] - order[None, :]
    before = jnp.sum(jnp.where((step == 1) | (step == 1 - count), slots[None, :], 0), axis=1)
    after = jnp.sum(jnp.where((step == -1) | (step == count - 1), slots[None, :], 0), axis=1)
    mine = 2 * s + block
    before_mine = pick(before, mine)
    after_mine = pick(after, mine)

    near_in = [lax.ppermute(t, AXES, within_block([(0, 1), (1, 2), (2, 3)])) for t in (keys, values)]
    far_in = [lax.ppermute(t, AXES, within_block([(0, 2), (1, 3)])) for t in (keys, values)]

    moved = lax.ppermute(values, AXES, within_block([(2, 0), (3, 1)]))
    quarter = jnp.where(c >= 2, keys, moved).reshape(4, CHUNK // 4, KV_WIDTH)
    pieces = [pick(quarter, y ^ m) for m in range(4)]
    held = jnp.stack([to_seq(pieces[m % 4], m) for m in range(8)], axis=0)
    arrived = []
    for mask in range(8):
        target = 2 * (s ^ (mask >> 1)) + (block ^ (mask & 1))
        arrived.append(to_plane(pick(held, (pick(before, target) >> 1) ^ s), mask))
    arrived = jnp.stack(arrived, axis=0).reshape(4, 2, CHUNK // 4, KV_WIDTH)
    arrived = lax.dynamic_index_in_dim(arrived, (before_mine & 1) ^ block, 1, keepdims=False)
    quarter = jnp.concatenate([pick(arrived, m ^ y) for m in range(4)], axis=0)
    straight = lax.ppermute(quarter, AXES, within_block([(2, 0), (3, 1)]))
    to_first = lax.ppermute(quarter, AXES, within_block([(1, 0)]))
    across = lax.ppermute(quarter, AXES, within_block([(3, 0)]))
    far = (jnp.where(c < 2, straight, far_in[0]), jnp.where(c < 2, quarter, far_in[1]))
    near = (jnp.where(c == 0, across, near_in[0]), jnp.where(c == 0, to_first, near_in[1]))

    chunk = (pick(order, mine) * 4 + c).reshape(1)
    attended, grad_query, far_key, far_value, near_key, near_value, own_key, own_value = attend(
        chunk, segment_ids.reshape(-1, CHUNK), queries, grads, far, near, (keys, values)
    )

    straight = lax.ppermute(far_key, AXES, within_block([(0, 2), (1, 3)]))
    to_second = lax.ppermute(near_value, AXES, within_block([(0, 1)]))
    across = lax.ppermute(near_key, AXES, within_block([(0, 3)]))
    near_back = [
        lax.ppermute(t, AXES, within_block([(1, 0), (2, 1), (3, 2)])) for t in (near_key, near_value)
    ]
    far_back = [lax.ppermute(t, AXES, within_block([(2, 0), (3, 1)])) for t in (far_key, far_value)]
    quarter = jnp.where(c < 2, far_value, straight).astype(jnp.float32)
    quarter = quarter + jnp.where(c == 1, to_second, jnp.where(c == 3, across, 0)).astype(jnp.float32)
    quarter = quarter.astype(jnp.bfloat16).reshape(4, CHUNK // 4, KV_WIDTH)
    pieces = [pick(quarter, y ^ m) for m in range(4)]
    held = jnp.stack([to_plane(pieces[mask >> 1], mask) for mask in range(8)], axis=0)
    arrived = []
    for m in range(8):
        target = pick(after, 2 * (s ^ m) + block)
        index = ((((target >> 1) ^ s) & 3) << 1) | ((target & 1) ^ block)
        arrived.append(to_seq(pick(held, index), m))
    arrived = jnp.stack(arrived, axis=0).reshape(2, 4, CHUNK // 4, KV_WIDTH)
    arrived = pick(arrived, (after_mine >> 3) ^ z)
    quarter = jnp.concatenate([pick(arrived, m ^ y) for m in range(4)], axis=0)
    moved = lax.ppermute(quarter, AXES, within_block([(0, 2), (1, 3)]))

    wide = functools.partial(jnp.asarray, dtype=jnp.float32)
    key_gradient = own_key + wide(near_back[0]) + wide(far_back[0]) + wide(jnp.where(c >= 2, quarter, 0))
    value_gradient = own_value + wide(near_back[1]) + wide(far_back[1]) + wide(jnp.where(c >= 2, moved, 0))
    return (
        attended,
        grad_query,
        key_gradient.astype(jnp.bfloat16),
        value_gradient.astype(jnp.bfloat16),
    )


def solution(mesh):
    rows = P(("dp", "seq", "head"), None)
    return jax.shard_map(
        local,
        mesh=mesh,
        in_specs=(rows, rows, rows, rows, P("dp"), P("dp")),
        out_specs=(rows, rows, rows, rows),
        check_vma=False,
    )
```

time: 491 us -> 300 us (0.61)
  the two profiles are of different devices: /device:TPU:1 before, /device:TPU:6 now
where the time goes in v1:
time: 300 us; the launch traced here: 298 us
  starting transfers between devices  159 us (53%)
  waiting for transfers between devices  104 us (35%)
  between operations  19 us (6%)
  Pallas kernels  11.2 us (4%)
    ppermute x14, starting transfers between devices, to_seq(): return lax.ppermute(value, 'seq', [(s, s ^ mask) for s in range(8)])  74.4 us
    ppermute x14, waiting for transfers between devices, to_seq(): return lax.ppermute(value, 'seq', [(s, s ^ mask) for s in range(8)])  63 us
    ppermute x14, starting transfers between devices, to_plane(): lax.ppermute(value, AXES, [(s * 8 + h, (s ^ mask >> 1) * 8 + (h ^ (mask &...  55.8 us
    ppermute x14, waiting for transfers between devices, to_plane(): lax.ppermute(value, AXES, [(s * 8 + h, (s ^ mask >> 1) * 8 + (h ^ (mask &...  22.2 us
    pallas_call x1, Pallas kernels, attend(): pl.pallas_call(attend_kernel, grid_spec=pltpu.PrefetchScalarGridSpec(num_...  11.2 us
    ppermute x2, starting transfers between devices, local(): lax.ppermute(t, AXES, within_block([(0, 1), (1, 2), (2, 3)]))  7.23 us
    ppermute x1, waiting for transfers between devices, local(): straight = lax.ppermute(far_key, AXES, within_block([(0, 2), (1, 3)]))  6.92 us
  transfers between devices with their start and end apart: 44, of which 17 were waited for; matrix products, arithmetic and copies ran while one was open for 1% of the time, Pallas kernels for 0%

profile of v1, /device:TPU:6, one launch (start us, length us, event | category | flops | bytes accessed | tf_op | source)
XLA Modules:
  0.0 298.4 jit_solution(13823653763677269366)
XLA Ops:
  0.6 2.7 collective-permute-start
  3.4 3.0 %collective-permute-done = bf16[128,512]{1,0:T(8,128)(2,1)S(1)} collective-permute-done((bf16[128,512]{1,0:T(8,128)(2,1)}, bf16[128,512]{1,0:T(8,128)(2,1)S(1)}, u32[]{:S(2)}, u32[]{:S(2)}) %collective-permute-start) | collective-permute-done | bytes 131104 | tf_op jit(solution)/shard_map/ppermute | solution.py:210
  7.4 3.5 %collective-permute-start.1 = (bf16[32,512]{1,0:T(8,128)(2,1)S(1)}, bf16[32,512]{1,0:T(8,128)(2,1)S(1)}, u32[]{:S(2)}, u32[]{:S(2)}) collective-permute-start(bf16[32,512]{1,0:T(8,128)(2,1)S(1)} %get-tuple-element.57), channel_id=1, source_target_pairs={{0,8},{8,0},{16,24},{24,16},{32,40},{40,32},{48,56},{56,48},{1,9},... | collective-permute-start | bytes 98312 | tf_op jit(solution)/shard_map/ppermute | solution.py:176
  17.1 17.3 %collective-permute-start.7 = (bf16[32,512]{1,0:T(8,128)(2,1)S(1)}, bf16[32,512]{1,0:T(8,128)(2,1)S(1)}, u32[]{:S(2)}, u32[]{:S(2)}) collective-permute-start(bf16[32,512]{1,0:T(8,128)(2,1)S(1)} %get-tuple-element.55), channel_id=1, source_target_pairs={{0,56},{8,48},{16,40},{24,32},{32,24},{40,16},{48,8},{56,0},{1,57}... | collective-permute-start | bytes 98312 | tf_op jit(solution)/shard_map/ppermute | solution.py:176
  34.4 3.0 collective-permute-start.3
  39.3 4.4 %collective-permute-start.2 = (bf16[32,512]{1,0:T(8,128)(2,1)S(1)}, bf16[32,512]{1,0:T(8,128)(2,1)S(1)}, u32[]{:S(2)}, u32[]{:S(2)}) collective-permute-start(bf16[32,512]{1,0:T(8,128)(2,1)S(1)} %get-tuple-element.56), channel_id=1, source_target_pairs={{0,16},{8,24},{16,0},{24,8},{32,48},{40,56},{48,32},{56,40},{1,17}... | collective-permute-start | bytes 98312 | tf_op jit(solution)/shard_map/ppermute | solution.py:176
  43.7 12.2 %collective-permute-start.5 = (bf16[32,512]{1,0:T(8,128)(2,1)S(1)}, bf16[32,512]{1,0:T(8,128)(2,1)S(1)}, u32[]{:S(2)}, u32[]{:S(2)}) collective-permute-start(bf16[32,512]{1,0:T(8,128)(2,1)S(1)} %get-tuple-element.57), channel_id=1, source_target_pairs={{0,40},{8,32},{16,56},{24,48},{32,8},{40,0},{48,24},{56,16},{1,41}... | collective-permute-start | bytes 98312 | tf_op jit(solution)/shard_map/ppermute | solution.py:176
  55.9 4.4 %collective-permute-start.4 = (bf16[32,512]{1,0:T(8,128)(2,1)S(1)}, bf16[32,512]{1,0:T(8,128)(2,1)S(1)}, u32[]{:S(2)}, u32[]{:S(2)}) collective-permute-start(bf16[32,512]{1,0:T(8,128)(2,1)S(1)} %get-tuple-element.53), channel_id=1, source_target_pairs={{0,32},{8,40},{16,48},{24,56},{32,0},{40,8},{48,16},{56,24},{1,33}... | collective-permute-start | bytes 98312 | tf_op jit(solution)/shard_map/ppermute | solution.py:176
  60.4 10.1 %collective-permute-done.4 = bf16[32,512]{1,0:T(8,128)(2,1)S(1)} collective-permute-done((bf16[32,512]{1,0:T(8,128)(2,1)S(1)}, bf16[32,512]{1,0:T(8,128)(2,1)S(1)}, u32[]{:S(2)}, u32[]{:S(2)}) %collective-permute-start.4) | collective-permute-done | bytes 32800 | tf_op jit(solution)/shard_map/ppermute | solution.py:176
  70.6 3.2 %collective-permute-start.8 = (bf16[32,512]{1,0:T(8,128)(2,1)S(1)}, bf16[32,512]{1,0:T(8,128)(2,1)S(1)}, u32[]{:S(2)}, u32[]{:S(2)}) collective-permute-start(bf16[32,512]{1,0:T(8,128)(2,1)S(1)} %get-tuple-element.44), channel_id=1, source_target_pairs={{0,4},{1,5},{2,6},{3,7},{4,0},{5,1},{6,2},{7,3},{8,12},{9,13},{10,... | collective-permute-start | bytes 98312 | tf_op jit(solution)/shard_map/ppermute | solution.py:182
  77.7 6.4 %collective-permute-start.14 = (bf16[32,512]{1,0:T(8,128)(2,1)S(1)}, bf16[32,512]{1,0:T(8,128)(2,1)S(1)}, u32[]{:S(2)}, u32[]{:S(2)}) collective-permute-start(bf16[32,512]{1,0:T(8,128)(2,1)S(1)} %get-tuple-element.38), channel_id=1, source_target_pairs={{0,28},{1,29},{2,30},{3,31},{4,24},{5,25},{6,26},{7,27},{8,20},{9,... | collective-permute-start | bytes 98312 | tf_op jit(solution)/shard_map/ppermute | solution.py:182
  84.1 2.5 collective-permute-start.13
  86.6 3.4 %collective-permute-start.9 = (bf16[32,512]{1,0:T(8,128)(2,1)S(1)}, bf16[32,512]{1,0:T(8,128)(2,1)S(1)}, u32[]{:S(2)}, u32[]{:S(2)}) collective-permute-start(bf16[32,512]{1,0:T(8,128)(2,1)S(1)} %get-tuple-element.43), channel_id=1, source_target_pairs={{0,8},{1,9},{2,10},{3,11},{4,12},{5,13},{6,14},{7,15},{8,0},{9,1},... | collective-permute-start | bytes 98312 | tf_op jit(solution)/shard_map/ppermute | solution.py:182
  90.1 2.4 collective-permute-done.9
  92.4 4.0 %collective-permute-start.10 = (bf16[32,512]{1,0:T(8,128)(2,1)S(1)}, bf16[32,512]{1,0:T(8,128)(2,1)S(1)}, u32[]{:S(2)}, u32[]{:S(2)}) collective-permute-start(bf16[32,512]{1,0:T(8,128)(2,1)S(1)} %get-tuple-element.42), channel_id=1, source_target_pairs={{0,12},{1,13},{2,14},{3,15},{4,8},{5,9},{6,10},{7,11},{8,4},{9,5},... | collective-permute-start | bytes 98312 | tf_op jit(solution)/shard_map/ppermute | solution.py:182
  96.4 4.2 %collective-permute-done.10 = bf16[32,512]{1,0:T(8,128)(2,1)S(1)} collective-permute-done((bf16[32,512]{1,0:T(8,128)(2,1)S(1)}, bf16[32,512]{1,0:T(8,128)(2,1)S(1)}, u32[]{:S(2)}, u32[]{:S(2)}) %collective-permute-start.10) | collective-permute-done | bytes 32800 | tf_op jit(solution)/shard_map/ppermute | solution.py:182
  100.6 4.7 %collective-permute-start.11 = (bf16[32,512]{1,0:T(8,128)(2,1)S(1)}, bf16[32,512]{1,0:T(8,128)(2,1)S(1)}, u32[]{:S(2)}, u32[]{:S(2)}) collective-permute-start(bf16[32,512]{1,0:T(8,128)(2,1)S(1)} %get-tuple-element.41), channel_id=1, source_target_pairs={{0,16},{1,17},{2,18},{3,19},{4,20},{5,21},{6,22},{7,23},{8,24},{9,... | collective-permute-start | bytes 98312 | tf_op jit(solution)/shard_map/ppermute | solution.py:182
  105.3 2.6 collective-permute-done.11
  107.9 5.5 %collective-permute-start.12 = (bf16[32,512]{1,0:T(8,128)(2,1)S(1)}, bf16[32,512]{1,0:T(8,128)(2,1)S(1)}, u32[]{:S(2)}, u32[]{:S(2)}) collective-permute-start(bf16[32,512]{1,0:T(8,128)(2,1)S(1)} %get-tuple-element.40), channel_id=1, source_target_pairs={{0,20},{1,21},{2,22},{3,23},{4,16},{5,17},{6,18},{7,19},{8,28},{9,... | collective-permute-start | bytes 98312 | tf_op jit(solution)/shard_map/ppermute | solution.py:182
  113.5 4.1 %collective-permute-done.12 = bf16[32,512]{1,0:T(8,128)(2,1)S(1)} collective-permute-done((bf16[32,512]{1,0:T(8,128)(2,1)S(1)}, bf16[32,512]{1,0:T(8,128)(2,1)S(1)}, u32[]{:S(2)}, u32[]{:S(2)}) %collective-permute-start.12) | collective-permute-done | bytes 32800 | tf_op jit(solution)/shard_map/ppermute | solution.py:182
  119.9 5.3 %collective-permute-start.21 = (bf16[128,512]{1,0:T(8,128)(2,1)S(1)}, bf16[128,512]{1,0:T(8,128)(2,1)S(1)}, u32[]{:S(2)}, u32[]{:S(2)}) collective-permute-start(bf16[128,512]{1,0:T(8,128)(2,1)S(1)} %copy-done.3), channel_id=1, source_target_pairs={{0,1},{1,2},{2,3},{4,5},{5,6},{6,7},{8,9},{9,10},{10,11},{12,13},{... | collective-permute-start | bytes 393224 | tf_op jit(solution)/shard_map/ppermute | solution.py:207
  127.1 4.9 %collective-permute-start.15 = (bf16[128,512]{1,0:T(8,128)(2,1)S(1)}, bf16[128,512]{1,0:T(8,128)(2,1)S(1)}, u32[]{:S(2)}, u32[]{:S(2)}) collective-permute-start(bf16[128,512]{1,0:T(8,128)(2,1)S(1)} %get-tuple-element.52), channel_id=1, source_target_pairs={{2,0},{3,1},{6,4},{7,5},{10,8},{11,9},{14,12},{15,13},{18,16},{19,... | collective-permute-start | bytes 393224 | tf_op jit(solution)/shard_map/ppermute | solution.py:221
  132.1 3.6 %collective-permute-done.15 = bf16[128,512]{1,0:T(8,128)(2,1)S(1)} collective-permute-done((bf16[128,512]{1,0:T(8,128)(2,1)S(1)}, bf16[128,512]{1,0:T(8,128)(2,1)S(1)}, u32[]{:S(2)}, u32[]{:S(2)}) %collective-permute-start.15) | collective-permute-done | bytes 131104 | tf_op jit(solution)/shard_map/ppermute | solution.py:221
  136.5 11.2 %shard_map.93 = (bf16[128,4096]{1,0:T(8,128)(2,1)}, bf16[128,4096]{1,0:T(8,128)(2,1)}, bf16[128,512]{1,0:T(8,128)(2,1)S(1)}, bf16[128,512]{1,0:T(8,128)(2,1)S(1)...) custom-call(s32[1]{0:T(128)} %bitcast.1.info_ref, ...), custom_call_target="tpu_custom_call" | custom-call | flops 2415919104 | bytes 4194304 | tf_op jit(solution)/shard_map/pallas_call | solution.py:126
  150.4 6.9 %collective-permute-done.24 = bf16[128,512]{1,0:T(8,128)(2,1)S(1)} collective-permute-done((bf16[128,512]{1,0:T(8,128)(2,1)S(1)}, bf16[128,512]{1,0:T(8,128)(2,1)S(1)}, u32[]{:S(2)}, u32[]{:S(2)}) %collective-permute-start.24) | collective-permute-done | bytes 131104 | tf_op jit(solution)/shard_map/ppermute | solution.py:232
  157.4 4.2 %collective-permute-start.27 = (bf16[32,512]{1,0:T(8,128)(2,1)S(1)}, bf16[32,512]{1,0:T(8,128)(2,1)S(1)}, u32[]{:S(2)}, u32[]{:S(2)}) collective-permute-start(bf16[32,512]{1,0:T(8,128)(2,1)S(1)} %get-tuple-element.50), channel_id=1, source_target_pairs={{0,4},{1,5},{2,6},{3,7},{4,0},{5,1},{6,2},{7,3},{8,12},{9,13},{10,... | collective-permute-start | bytes 98312 | tf_op jit(solution)/shard_map/ppermute | solution.py:182
  171.9 5.2 %collective-permute-start.33 = (bf16[32,512]{1,0:T(8,128)(2,1)S(1)}, bf16[32,512]{1,0:T(8,128)(2,1)S(1)}, u32[]{:S(2)}, u32[]{:S(2)}) collective-permute-start(bf16[32,512]{1,0:T(8,128)(2,1)S(1)} %get-tuple-element.46), channel_id=1, source_target_pairs={{0,28},{1,29},{2,30},{3,31},{4,24},{5,25},{6,26},{7,27},{8,20},{9,... | collective-permute-start | bytes 98312 | tf_op jit(solution)/shard_map/ppermute | solution.py:182
  177.1 2.5 collective-permute-start.32
  179.6 5.2 %collective-permute-start.31 = (bf16[32,512]{1,0:T(8,128)(2,1)S(1)}, bf16[32,512]{1,0:T(8,128)(2,1)S(1)}, u32[]{:S(2)}, u32[]{:S(2)}) collective-permute-start(bf16[32,512]{1,0:T(8,128)(2,1)S(1)} %get-tuple-element.48), channel_id=1, source_target_pairs={{0,20},{1,21},{2,22},{3,23},{4,16},{5,17},{6,18},{7,19},{8,28},{9,... | collective-permute-start | bytes 98312 | tf_op jit(solution)/shard_map/ppermute | solution.py:182
  184.9 3.9 %collective-permute-start.30 = (bf16[32,512]{1,0:T(8,128)(2,1)S(1)}, bf16[32,512]{1,0:T(8,128)(2,1)S(1)}, u32[]{:S(2)}, u32[]{:S(2)}) collective-permute-start(bf16[32,512]{1,0:T(8,128)(2,1)S(1)} %get-tuple-element.48), channel_id=1, source_target_pairs={{0,16},{1,17},{2,18},{3,19},{4,20},{5,21},{6,22},{7,23},{8,24},{9,... | collective-permute-start | bytes 98312 | tf_op jit(solution)/shard_map/ppermute | solution.py:182
  188.7 2.2 collective-permute-start.28
  191.0 3.6 %collective-permute-done.28 = bf16[32,512]{1,0:T(8,128)(2,1)S(1)} collective-permute-done((bf16[32,512]{1,0:T(8,128)(2,1)S(1)}, bf16[32,512]{1,0:T(8,128)(2,1)S(1)}, u32[]{:S(2)}, u32[]{:S(2)}) %collective-permute-start.28) | collective-permute-done | bytes 32800 | tf_op jit(solution)/shard_map/ppermute | solution.py:182
  194.5 2.9 collective-permute-start.29
  197.4 5.3 %collective-permute-done.29 = bf16[32,512]{1,0:T(8,128)(2,1)S(1)} collective-permute-done((bf16[32,512]{1,0:T(8,128)(2,1)S(1)}, bf16[32,512]{1,0:T(8,128)(2,1)S(1)}, u32[]{:S(2)}, u32[]{:S(2)}) %collective-permute-start.29) | collective-permute-done | bytes 32800 | tf_op jit(solution)/shard_map/ppermute | solution.py:182
  202.9 2.2 collective-permute-start.34
  212.3 5.7 %collective-permute-start.35 = (bf16[32,512]{1,0:T(8,128)(2,1)S(1)}, bf16[32,512]{1,0:T(8,128)(2,1)S(1)}, u32[]{:S(2)}, u32[]{:S(2)}) collective-permute-start(bf16[32,512]{1,0:T(8,128)(2,1)S(1)} %get-tuple-element.31), channel_id=1, source_target_pairs={{0,16},{8,24},{16,0},{24,8},{32,48},{40,56},{48,32},{56,40},{1,17}... | collective-permute-start | bytes 98312 | tf_op jit(solution)/shard_map/ppermute | solution.py:176
  218.0 2.0 collective-permute-done.35
  220.0 3.8 %collective-permute-start.36 = (bf16[32,512]{1,0:T(8,128)(2,1)S(1)}, bf16[32,512]{1,0:T(8,128)(2,1)S(1)}, u32[]{:S(2)}, u32[]{:S(2)}) collective-permute-start(bf16[32,512]{1,0:T(8,128)(2,1)S(1)} %get-tuple-element.30), channel_id=1, source_target_pairs={{0,24},{8,16},{16,8},{24,0},{32,56},{40,48},{48,40},{56,32},{1,25}... | collective-permute-start | bytes 98312 | tf_op jit(solution)/shard_map/ppermute | solution.py:176
  223.8 3.2 %collective-permute-done.36 = bf16[32,512]{1,0:T(8,128)(2,1)S(1)} collective-permute-done((bf16[32,512]{1,0:T(8,128)(2,1)S(1)}, bf16[32,512]{1,0:T(8,128)(2,1)S(1)}, u32[]{:S(2)}, u32[]{:S(2)}) %collective-permute-start.36) | collective-permute-done | bytes 32800 | tf_op jit(solution)/shard_map/ppermute | solution.py:176
  227.0 3.7 %collective-permute-start.37 = (bf16[32,512]{1,0:T(8,128)(2,1)S(1)}, bf16[32,512]{1,0:T(8,128)(2,1)S(1)}, u32[]{:S(2)}, u32[]{:S(2)}) collective-permute-start(bf16[32,512]{1,0:T(8,128)(2,1)S(1)} %get-tuple-element.29), channel_id=1, source_target_pairs={{0,32},{8,40},{16,48},{24,56},{32,0},{40,8},{48,16},{56,24},{1,33}... | collective-permute-start | bytes 98312 | tf_op jit(solution)/shard_map/ppermute | solution.py:176
  230.7 10.8 %collective-permute-done.37 = bf16[32,512]{1,0:T(8,128)(2,1)S(1)} collective-permute-done((bf16[32,512]{1,0:T(8,128)(2,1)S(1)}, bf16[32,512]{1,0:T(8,128)(2,1)S(1)}, u32[]{:S(2)}, u32[]{:S(2)}) %collective-permute-start.37) | collective-permute-done | bytes 32800 | tf_op jit(solution)/shard_map/ppermute | solution.py:176
  241.5 3.9 %collective-permute-start.38 = (bf16[32,512]{1,0:T(8,128)(2,1)S(1)}, bf16[32,512]{1,0:T(8,128)(2,1)S(1)}, u32[]{:S(2)}, u32[]{:S(2)}) collective-permute-start(bf16[32,512]{1,0:T(8,128)(2,1)S(1)} %get-tuple-element.28), channel_id=1, source_target_pairs={{0,40},{8,32},{16,56},{24,48},{32,8},{40,0},{48,24},{56,16},{1,41}... | collective-permute-start | bytes 98312 | tf_op jit(solution)/shard_map/ppermute | solution.py:176
  245.5 11.5 %collective-permute-done.38 = bf16[32,512]{1,0:T(8,128)(2,1)S(1)} collective-permute-done((bf16[32,512]{1,0:T(8,128)(2,1)S(1)}, bf16[32,512]{1,0:T(8,128)(2,1)S(1)}, u32[]{:S(2)}, u32[]{:S(2)}) %collective-permute-start.38) | collective-permute-done | bytes 32800 | tf_op jit(solution)/shard_map/ppermute | solution.py:176
  257.0 4.0 %collective-permute-start.39 = (bf16[32,512]{1,0:T(8,128)(2,1)S(1)}, bf16[32,512]{1,0:T(8,128)(2,1)S(1)}, u32[]{:S(2)}, u32[]{:S(2)}) collective-permute-start(bf16[32,512]{1,0:T(8,128)(2,1)S(1)} %get-tuple-element.27), channel_id=1, source_target_pairs={{0,48},{8,56},{16,32},{24,40},{32,16},{40,24},{48,0},{56,8},{1,49}... | collective-permute-start | bytes 98312 | tf_op jit(solution)/shard_map/ppermute | solution.py:176
  260.9 13.0 %collective-permute-done.39 = bf16[32,512]{1,0:T(8,128)(2,1)S(1)} collective-permute-done((bf16[32,512]{1,0:T(8,128)(2,1)S(1)}, bf16[32,512]{1,0:T(8,128)(2,1)S(1)}, u32[]{:S(2)}, u32[]{:S(2)}) %collective-permute-start.39) | collective-permute-done | bytes 32800 | tf_op jit(solution)/shard_map/ppermute | solution.py:176
  274.0 4.3 %collective-permute-start.40 = (bf16[32,512]{1,0:T(8,128)(2,1)S(1)}, bf16[32,512]{1,0:T(8,128)(2,1)S(1)}, u32[]{:S(2)}, u32[]{:S(2)}) collective-permute-start(bf16[32,512]{1,0:T(8,128)(2,1)S(1)} %get-tuple-element.26), channel_id=1, source_target_pairs={{0,56},{8,48},{16,40},{24,32},{32,24},{40,16},{48,8},{56,0},{1,57}... | collective-permute-start | bytes 98312 | tf_op jit(solution)/shard_map/ppermute | solution.py:176
  278.3 12.4 %collective-permute-done.40 = bf16[32,512]{1,0:T(8,128)(2,1)S(1)} collective-permute-done((bf16[32,512]{1,0:T(8,128)(2,1)S(1)}, bf16[32,512]{1,0:T(8,128)(2,1)S(1)}, u32[]{:S(2)}, u32[]{:S(2)}) %collective-permute-start.40) | collective-permute-done | bytes 32800 | tf_op jit(solution)/shard_map/ppermute | solution.py:176
  292.8 4.8 %collective-permute-done.43 = bf16[128,512]{1,0:T(8,128)(2,1)S(1)} collective-permute-done((bf16[128,512]{1,0:T(8,128)(2,1)S(1)}, bf16[128,512]{1,0:T(8,128)(2,1)S(1)}, u32[]{:S(2)}, u32[]{:S(2)}) %collective-permute-start.43) | collective-permute-done | bytes 131104 | tf_op jit(solution)/shard_map/ppermute | solution.py:252
  (99 shorter events, 23.4 us)
Async XLA Ops:
  0.6 5.8 %collective-permute-start = (bf16[128,512]{1,0:T(8,128)(2,1)}, bf16[128,512]{1,0:T(8,128)(2,1)S(1)}, u32[]{:S(2)}, u32[]{:S(2)}) collective-permute-start(bf16[128,512]{1,0:T(8,128)(2,1)} %value_own_ref.1), channel_id=1, source_target_pairs={{2,0},{3,1},{6,4},{7,5},{10,8},{11,9},{14,12},{15,13},{18,16},{19,... | collective-permute-start | bytes 393224 | tf_op jit(solution)/shard_map/ppermute | solution.py:210
  7.4 3.5 %copy-start.5 = (s32[16]{0:T(128)S(1)}, s32[16]{0:T(128)}, u32[]{:S(2)}) copy-start(s32[16]{0:T(128)} %param.11) | copy-start | bytes 196
  7.4 36.3 %collective-permute-start.1 = (bf16[32,512]{1,0:T(8,128)(2,1)S(1)}, bf16[32,512]{1,0:T(8,128)(2,1)S(1)}, u32[]{:S(2)}, u32[]{:S(2)}) collective-permute-start(bf16[32,512]{1,0:T(8,128)(2,1)S(1)} %get-tuple-element.57), channel_id=1, source_target_pairs={{0,8},{8,0},{16,24},{24,16},{32,40},{40,32},{48,56},{56,48},{1,9},... | collective-permute-start | bytes 98312 | tf_op jit(solution)/shard_map/ppermute | solution.py:176
  17.1 53.4 %collective-permute-start.7 = (bf16[32,512]{1,0:T(8,128)(2,1)S(1)}, bf16[32,512]{1,0:T(8,128)(2,1)S(1)}, u32[]{:S(2)}, u32[]{:S(2)}) collective-permute-start(bf16[32,512]{1,0:T(8,128)(2,1)S(1)} %get-tuple-element.55), channel_id=1, source_target_pairs={{0,56},{8,48},{16,40},{24,32},{32,24},{40,16},{48,8},{56,0},{1,57}... | collective-permute-start | bytes 98312 | tf_op jit(solution)/shard_map/ppermute | solution.py:176
  34.4 26.0 %collective-permute-start.3 = (bf16[32,512]{1,0:T(8,128)(2,1)S(1)}, bf16[32,512]{1,0:T(8,128)(2,1)S(1)}, u32[]{:S(2)}, u32[]{:S(2)}) collective-permute-start(bf16[32,512]{1,0:T(8,128)(2,1)S(1)} %get-tuple-element.55), channel_id=1, source_target_pairs={{0,24},{8,16},{16,8},{24,0},{32,56},{40,48},{48,40},{56,32},{1,25}... | collective-permute-start | bytes 98312 | tf_op jit(solution)/shard_map/ppermute | solution.py:176
  37.4 33.1 %collective-permute-start.6 = (bf16[32,512]{1,0:T(8,128)(2,1)S(1)}, bf16[32,512]{1,0:T(8,128)(2,1)S(1)}, u32[]{:S(2)}, u32[]{:S(2)}) collective-permute-start(bf16[32,512]{1,0:T(8,128)(2,1)S(1)} %get-tuple-element.56), channel_id=1, source_target_pairs={{0,48},{8,56},{16,32},{24,40},{32,16},{40,24},{48,0},{56,8},{1,49}... | collective-permute-start | bytes 98312 | tf_op jit(solution)/shard_map/ppermute | solution.py:176
  39.3 16.6 %collective-permute-start.2 = (bf16[32,512]{1,0:T(8,128)(2,1)S(1)}, bf16[32,512]{1,0:T(8,128)(2,1)S(1)}, u32[]{:S(2)}, u32[]{:S(2)}) collective-permute-start(bf16[32,512]{1,0:T(8,128)(2,1)S(1)} %get-tuple-element.56), channel_id=1, source_target_pairs={{0,16},{8,24},{16,0},{24,8},{32,48},{40,56},{48,32},{56,40},{1,17}... | collective-permute-start | bytes 98312 | tf_op jit(solution)/shard_map/ppermute | solution.py:176
  43.7 26.8 %collective-permute-start.5 = (bf16[32,512]{1,0:T(8,128)(2,1)S(1)}, bf16[32,512]{1,0:T(8,128)(2,1)S(1)}, u32[]{:S(2)}, u32[]{:S(2)}) collective-permute-start(bf16[32,512]{1,0:T(8,128)(2,1)S(1)} %get-tuple-element.57), channel_id=1, source_target_pairs={{0,40},{8,32},{16,56},{24,48},{32,8},{40,0},{48,24},{56,16},{1,41}... | collective-permute-start | bytes 98312 | tf_op jit(solution)/shard_map/ppermute | solution.py:176
  55.9 14.5 %collective-permute-start.4 = (bf16[32,512]{1,0:T(8,128)(2,1)S(1)}, bf16[32,512]{1,0:T(8,128)(2,1)S(1)}, u32[]{:S(2)}, u32[]{:S(2)}) collective-permute-start(bf16[32,512]{1,0:T(8,128)(2,1)S(1)} %get-tuple-element.53), channel_id=1, source_target_pairs={{0,32},{8,40},{16,48},{24,56},{32,0},{40,8},{48,16},{56,24},{1,33}... | collective-permute-start | bytes 98312 | tf_op jit(solution)/shard_map/ppermute | solution.py:176
  70.5 5.2 %copy-start.3 = (bf16[128,512]{1,0:T(8,128)(2,1)S(1)}, bf16[128,512]{1,0:T(8,128)(2,1)}, u32[]{:S(2)}) copy-start(bf16[128,512]{1,0:T(8,128)(2,1)} %value_own_ref.1) | copy-start | bytes 393220
  70.6 16.0 %collective-permute-start.8 = (bf16[32,512]{1,0:T(8,128)(2,1)S(1)}, bf16[32,512]{1,0:T(8,128)(2,1)S(1)}, u32[]{:S(2)}, u32[]{:S(2)}) collective-permute-start(bf16[32,512]{1,0:T(8,128)(2,1)S(1)} %get-tuple-element.44), channel_id=1, source_target_pairs={{0,4},{1,5},{2,6},{3,7},{4,0},{5,1},{6,2},{7,3},{8,12},{9,13},{10,... | collective-permute-start | bytes 98312 | tf_op jit(solution)/shard_map/ppermute | solution.py:182
  73.8 53.4 %collective-permute-start.19 = (bf16[128,512]{1,0:T(8,128)(2,1)S(1)}, bf16[128,512]{1,0:T(8,128)(2,1)S(1)}, u32[]{:S(2)}, u32[]{:S(2)}) collective-permute-start(bf16[128,512]{1,0:T(8,128)(2,1)S(1)} %copy-done), channel_id=1, source_target_pairs={{0,1},{1,2},{2,3},{4,5},{5,6},{6,7},{8,9},{9,10},{10,11},{12,13},{... | collective-permute-start | bytes 393224 | tf_op jit(solution)/shard_map/ppermute | solution.py:207
  75.7 42.0 %collective-permute-start.17 = (bf16[128,512]{1,0:T(8,128)(2,1)S(1)}, bf16[128,512]{1,0:T(8,128)(2,1)S(1)}, u32[]{:S(2)}, u32[]{:S(2)}) collective-permute-start(bf16[128,512]{1,0:T(8,128)(2,1)S(1)} %copy-done.3), channel_id=1, source_target_pairs={{0,2},{1,3},{4,6},{5,7},{8,10},{9,11},{12,14},{13,15},{16,18},{17,... | collective-permute-start | bytes 393224 | tf_op jit(solution)/shard_map/ppermute | solution.py:208
  77.7 40.0 %collective-permute-start.14 = (bf16[32,512]{1,0:T(8,128)(2,1)S(1)}, bf16[32,512]{1,0:T(8,128)(2,1)S(1)}, u32[]{:S(2)}, u32[]{:S(2)}) collective-permute-start(bf16[32,512]{1,0:T(8,128)(2,1)S(1)} %get-tuple-element.38), channel_id=1, source_target_pairs={{0,28},{1,29},{2,30},{3,31},{4,24},{5,25},{6,26},{7,27},{8,20},{9,... | collective-permute-start | bytes 98312 | tf_op jit(solution)/shard_map/ppermute | solution.py:182
  84.1 33.6 %collective-permute-start.13 = (bf16[32,512]{1,0:T(8,128)(2,1)S(1)}, bf16[32,512]{1,0:T(8,128)(2,1)S(1)}, u32[]{:S(2)}, u32[]{:S(2)}) collective-permute-start(bf16[32,512]{1,0:T(8,128)(2,1)S(1)} %get-tuple-element.39), channel_id=1, source_target_pairs={{0,24},{1,25},{2,26},{3,27},{4,28},{5,29},{6,30},{7,31},{8,16},{9,... | collective-permute-start | bytes 98312 | tf_op jit(solution)/shard_map/ppermute | solution.py:182
  86.6 5.8 %collective-permute-start.9 = (bf16[32,512]{1,0:T(8,128)(2,1)S(1)}, bf16[32,512]{1,0:T(8,128)(2,1)S(1)}, u32[]{:S(2)}, u32[]{:S(2)}) collective-permute-start(bf16[32,512]{1,0:T(8,128)(2,1)S(1)} %get-tuple-element.43), channel_id=1, source_target_pairs={{0,8},{1,9},{2,10},{3,11},{4,12},{5,13},{6,14},{7,15},{8,0},{9,1},... | collective-permute-start | bytes 98312 | tf_op jit(solution)/shard_map/ppermute | solution.py:182
  92.4 8.2 %collective-permute-start.10 = (bf16[32,512]{1,0:T(8,128)(2,1)S(1)}, bf16[32,512]{1,0:T(8,128)(2,1)S(1)}, u32[]{:S(2)}, u32[]{:S(2)}) collective-permute-start(bf16[32,512]{1,0:T(8,128)(2,1)S(1)} %get-tuple-element.42), channel_id=1, source_target_pairs={{0,12},{1,13},{2,14},{3,15},{4,8},{5,9},{6,10},{7,11},{8,4},{9,5},... | collective-permute-start | bytes 98312 | tf_op jit(solution)/shard_map/ppermute | solution.py:182
  100.6 7.3 %collective-permute-start.11 = (bf16[32,512]{1,0:T(8,128)(2,1)S(1)}, bf16[32,512]{1,0:T(8,128)(2,1)S(1)}, u32[]{:S(2)}, u32[]{:S(2)}) collective-permute-start(bf16[32,512]{1,0:T(8,128)(2,1)S(1)} %get-tuple-element.41), channel_id=1, source_target_pairs={{0,16},{1,17},{2,18},{3,19},{4,20},{5,21},{6,22},{7,23},{8,24},{9,... | collective-permute-start | bytes 98312 | tf_op jit(solution)/shard_map/ppermute | solution.py:182
  107.9 9.7 %collective-permute-start.12 = (bf16[32,512]{1,0:T(8,128)(2,1)S(1)}, bf16[32,512]{1,0:T(8,128)(2,1)S(1)}, u32[]{:S(2)}, u32[]{:S(2)}) collective-permute-start(bf16[32,512]{1,0:T(8,128)(2,1)S(1)} %get-tuple-element.40), channel_id=1, source_target_pairs={{0,20},{1,21},{2,22},{3,23},{4,16},{5,17},{6,18},{7,19},{8,28},{9,... | collective-permute-start | bytes 98312 | tf_op jit(solution)/shard_map/ppermute | solution.py:182
  117.6 18.1 %copy-start.1 = (bf16[128,4096]{1,0:T(8,128)(2,1)S(1)}, bf16[128,4096]{1,0:T(8,128)(2,1)}, u32[]{:S(2)}) copy-start(bf16[128,4096]{1,0:T(8,128)(2,1)} %query_ref.1) | copy-start | bytes 3145732
  117.6 18.1 %copy-start.2 = (bf16[128,4096]{1,0:T(8,128)(2,1)S(1)}, bf16[128,4096]{1,0:T(8,128)(2,1)}, u32[]{:S(2)}) copy-start(bf16[128,4096]{1,0:T(8,128)(2,1)} %grad_ref.1) | copy-start | bytes 3145732
  117.8 14.3 %collective-permute-start.18 = (bf16[128,512]{1,0:T(8,128)(2,1)S(1)}, bf16[128,512]{1,0:T(8,128)(2,1)S(1)}, u32[]{:S(2)}, u32[]{:S(2)}) collective-permute-start(bf16[128,512]{1,0:T(8,128)(2,1)S(1)} %get-tuple-element.52), channel_id=1, source_target_pairs={{3,0},{7,4},{11,8},{15,12},{19,16},{23,20},{27,24},{31,28},{35,32}... | collective-permute-start | bytes 393224 | tf_op jit(solution)/shard_map/ppermute | solution.py:223
  118.6 13.5 %collective-permute-start.16 = (bf16[128,512]{1,0:T(8,128)(2,1)S(1)}, bf16[128,512]{1,0:T(8,128)(2,1)S(1)}, u32[]{:S(2)}, u32[]{:S(2)}) collective-permute-start(bf16[128,512]{1,0:T(8,128)(2,1)S(1)} %copy-done), channel_id=1, source_target_pairs={{0,2},{1,3},{4,6},{5,7},{8,10},{9,11},{12,14},{13,15},{16,18},{17,... | collective-permute-start | bytes 393224 | tf_op jit(solution)/shard_map/ppermute | solution.py:208
  119.9 12.2 %collective-permute-start.21 = (bf16[128,512]{1,0:T(8,128)(2,1)S(1)}, bf16[128,512]{1,0:T(8,128)(2,1)S(1)}, u32[]{:S(2)}, u32[]{:S(2)}) collective-permute-start(bf16[128,512]{1,0:T(8,128)(2,1)S(1)} %copy-done.3), channel_id=1, source_target_pairs={{0,1},{1,2},{2,3},{4,5},{5,6},{6,7},{8,9},{9,10},{10,11},{12,13},{... | collective-permute-start | bytes 393224 | tf_op jit(solution)/shard_map/ppermute | solution.py:207
  126.4 5.6 %collective-permute-start.20 = (bf16[128,512]{1,0:T(8,128)(2,1)S(1)}, bf16[128,512]{1,0:T(8,128)(2,1)S(1)}, u32[]{:S(2)}, u32[]{:S(2)}) collective-permute-start(bf16[128,512]{1,0:T(8,128)(2,1)S(1)} %get-tuple-element.52), channel_id=1, source_target_pairs={{1,0},{5,4},{9,8},{13,12},{17,16},{21,20},{25,24},{29,28},{33,32},... | collective-permute-start | bytes 393224 | tf_op jit(solution)/shard_map/ppermute | solution.py:222
  127.1 8.6 %collective-permute-start.15 = (bf16[128,512]{1,0:T(8,128)(2,1)S(1)}, bf16[128,512]{1,0:T(8,128)(2,1)S(1)}, u32[]{:S(2)}, u32[]{:S(2)}) collective-permute-start(bf16[128,512]{1,0:T(8,128)(2,1)S(1)} %get-tuple-element.52), channel_id=1, source_target_pairs={{2,0},{3,1},{6,4},{7,5},{10,8},{11,9},{14,12},{15,13},{18,16},{19,... | collective-permute-start | bytes 393224 | tf_op jit(solution)/shard_map/ppermute | solution.py:221
  147.8 2.7 collective-permute-start.26
  148.4 8.9 %collective-permute-start.24 = (bf16[128,512]{1,0:T(8,128)(2,1)S(1)}, bf16[128,512]{1,0:T(8,128)(2,1)S(1)}, u32[]{:S(2)}, u32[]{:S(2)}) collective-permute-start(bf16[128,512]{1,0:T(8,128)(2,1)S(1)} %get-tuple-element.16), channel_id=1, source_target_pairs={{0,2},{1,3},{4,6},{5,7},{8,10},{9,11},{12,14},{13,15},{16,18},{17,... | collective-permute-start | bytes 393224 | tf_op jit(solution)/shard_map/ppermute | solution.py:232
  149.7 7.6 %collective-permute-start.25 = (bf16[128,512]{1,0:T(8,128)(2,1)S(1)}, bf16[128,512]{1,0:T(8,128)(2,1)S(1)}, u32[]{:S(2)}, u32[]{:S(2)}) collective-permute-start(bf16[128,512]{1,0:T(8,128)(2,1)S(1)} %get-tuple-element.18), channel_id=1, source_target_pairs={{0,1},{4,5},{8,9},{12,13},{16,17},{20,21},{24,25},{28,29},{32,33},... | collective-permute-start | bytes 393224 | tf_op jit(solution)/shard_map/ppermute | solution.py:233
  157.4 31.3 %collective-permute-start.27 = (bf16[32,512]{1,0:T(8,128)(2,1)S(1)}, bf16[32,512]{1,0:T(8,128)(2,1)S(1)}, u32[]{:S(2)}, u32[]{:S(2)}) collective-permute-start(bf16[32,512]{1,0:T(8,128)(2,1)S(1)} %get-tuple-element.50), channel_id=1, source_target_pairs={{0,4},{1,5},{2,6},{3,7},{4,0},{5,1},{6,2},{7,3},{8,12},{9,13},{10,... | collective-permute-start | bytes 98312 | tf_op jit(solution)/shard_map/ppermute | solution.py:182
  171.9 30.9 %collective-permute-start.33 = (bf16[32,512]{1,0:T(8,128)(2,1)S(1)}, bf16[32,512]{1,0:T(8,128)(2,1)S(1)}, u32[]{:S(2)}, u32[]{:S(2)}) collective-permute-start(bf16[32,512]{1,0:T(8,128)(2,1)S(1)} %get-tuple-element.46), channel_id=1, source_target_pairs={{0,28},{1,29},{2,30},{3,31},{4,24},{5,25},{6,26},{7,27},{8,20},{9,... | collective-permute-start | bytes 98312 | tf_op jit(solution)/shard_map/ppermute | solution.py:182
  177.1 25.7 %collective-permute-start.32 = (bf16[32,512]{1,0:T(8,128)(2,1)S(1)}, bf16[32,512]{1,0:T(8,128)(2,1)S(1)}, u32[]{:S(2)}, u32[]{:S(2)}) collective-permute-start(bf16[32,512]{1,0:T(8,128)(2,1)S(1)} %get-tuple-element.46), channel_id=1, source_target_pairs={{0,24},{1,25},{2,26},{3,27},{4,28},{5,29},{6,30},{7,31},{8,16},{9,... | collective-permute-start | bytes 98312 | tf_op jit(solution)/shard_map/ppermute | solution.py:182
  179.6 23.2 %collective-permute-start.31 = (bf16[32,512]{1,0:T(8,128)(2,1)S(1)}, bf16[32,512]{1,0:T(8,128)(2,1)S(1)}, u32[]{:S(2)}, u32[]{:S(2)}) collective-permute-start(bf16[32,512]{1,0:T(8,128)(2,1)S(1)} %get-tuple-element.48), channel_id=1, source_target_pairs={{0,20},{1,21},{2,22},{3,23},{4,16},{5,17},{6,18},{7,19},{8,28},{9,... | collective-permute-start | bytes 98312 | tf_op jit(solution)/shard_map/ppermute | solution.py:182
  184.9 17.9 %collective-permute-start.30 = (bf16[32,512]{1,0:T(8,128)(2,1)S(1)}, bf16[32,512]{1,0:T(8,128)(2,1)S(1)}, u32[]{:S(2)}, u32[]{:S(2)}) collective-permute-start(bf16[32,512]{1,0:T(8,128)(2,1)S(1)} %get-tuple-element.48), channel_id=1, source_target_pairs={{0,16},{1,17},{2,18},{3,19},{4,20},{5,21},{6,22},{7,23},{8,24},{9,... | collective-permute-start | bytes 98312 | tf_op jit(solution)/shard_map/ppermute | solution.py:182
  188.7 5.8 %collective-permute-start.28 = (bf16[32,512]{1,0:T(8,128)(2,1)S(1)}, bf16[32,512]{1,0:T(8,128)(2,1)S(1)}, u32[]{:S(2)}, u32[]{:S(2)}) collective-permute-start(bf16[32,512]{1,0:T(8,128)(2,1)S(1)} %get-tuple-element.49), channel_id=1, source_target_pairs={{0,8},{1,9},{2,10},{3,11},{4,12},{5,13},{6,14},{7,15},{8,0},{9,1},... | collective-permute-start | bytes 98312 | tf_op jit(solution)/shard_map/ppermute | solution.py:182
  194.5 8.2 %collective-permute-start.29 = (bf16[32,512]{1,0:T(8,128)(2,1)S(1)}, bf16[32,512]{1,0:T(8,128)(2,1)S(1)}, u32[]{:S(2)}, u32[]{:S(2)}) collective-permute-start(bf16[32,512]{1,0:T(8,128)(2,1)S(1)} %get-tuple-element.49), channel_id=1, source_target_pairs={{0,12},{1,13},{2,14},{3,15},{4,8},{5,9},{6,10},{7,11},{8,4},{9,5},... | collective-permute-start | bytes 98312 | tf_op jit(solution)/shard_map/ppermute | solution.py:182
  202.9 9.4 %collective-permute-start.34 = (bf16[32,512]{1,0:T(8,128)(2,1)S(1)}, bf16[32,512]{1,0:T(8,128)(2,1)S(1)}, u32[]{:S(2)}, u32[]{:S(2)}) collective-permute-start(bf16[32,512]{1,0:T(8,128)(2,1)S(1)} %get-tuple-element.32), channel_id=1, source_target_pairs={{0,8},{8,0},{16,24},{24,16},{32,40},{40,32},{48,56},{56,48},{1,9},... | collective-permute-start | bytes 98312 | tf_op jit(solution)/shard_map/ppermute | solution.py:176
  205.8 86.3 %collective-permute-start.22 = (bf16[128,512]{1,0:T(8,128)(2,1)S(1)}, bf16[128,512]{1,0:T(8,128)(2,1)S(1)}, u32[]{:S(2)}, u32[]{:S(2)}) collective-permute-start(bf16[128,512]{1,0:T(8,128)(2,1)S(1)} %get-tuple-element.15), channel_id=1, source_target_pairs={{1,0},{2,1},{3,2},{5,4},{6,5},{7,6},{9,8},{10,9},{11,10},{13,12},{... | collective-permute-start | bytes 393224 | tf_op jit(solution)/shard_map/ppermute | solution.py:236
  207.7 84.4 %collective-permute-start.23 = (bf16[128,512]{1,0:T(8,128)(2,1)S(1)}, bf16[128,512]{1,0:T(8,128)(2,1)S(1)}, u32[]{:S(2)}, u32[]{:S(2)}) collective-permute-start(bf16[128,512]{1,0:T(8,128)(2,1)S(1)} %get-tuple-element.16), channel_id=1, source_target_pairs={{2,0},{3,1},{6,4},{7,5},{10,8},{11,9},{14,12},{15,13},{18,16},{19,... | collective-permute-start | bytes 393224 | tf_op jit(solution)/shard_map/ppermute | solution.py:238
  209.0 83.8 %collective-permute-start.42 = (bf16[128,512]{1,0:T(8,128)(2,1)S(1)}, bf16[128,512]{1,0:T(8,128)(2,1)S(1)}, u32[]{:S(2)}, u32[]{:S(2)}) collective-permute-start(bf16[128,512]{1,0:T(8,128)(2,1)S(1)} %get-tuple-element.17), channel_id=1, source_target_pairs={{2,0},{3,1},{6,4},{7,5},{10,8},{11,9},{14,12},{15,13},{18,16},{19,... | collective-permute-start | bytes 393224 | tf_op jit(solution)/shard_map/ppermute | solution.py:238
  210.3 82.5 %collective-permute-start.41 = (bf16[128,512]{1,0:T(8,128)(2,1)S(1)}, bf16[128,512]{1,0:T(8,128)(2,1)S(1)}, u32[]{:S(2)}, u32[]{:S(2)}) collective-permute-start(bf16[128,512]{1,0:T(8,128)(2,1)S(1)} %get-tuple-element.18), channel_id=1, source_target_pairs={{1,0},{2,1},{3,2},{5,4},{6,5},{7,6},{9,8},{10,9},{11,10},{13,12},{... | collective-permute-start | bytes 393224 | tf_op jit(solution)/shard_map/ppermute | solution.py:236
  212.3 7.7 %collective-permute-start.35 = (bf16[32,512]{1,0:T(8,128)(2,1)S(1)}, bf16[32,512]{1,0:T(8,128)(2,1)S(1)}, u32[]{:S(2)}, u32[]{:S(2)}) collective-permute-start(bf16[32,512]{1,0:T(8,128)(2,1)S(1)} %get-tuple-element.31), channel_id=1, source_target_pairs={{0,16},{8,24},{16,0},{24,8},{32,48},{40,56},{48,32},{56,40},{1,17}... | collective-permute-start | bytes 98312 | tf_op jit(solution)/shard_map/ppermute | solution.py:176
  220.0 7.0 %collective-permute-start.36 = (bf16[32,512]{1,0:T(8,128)(2,1)S(1)}, bf16[32,512]{1,0:T(8,128)(2,1)S(1)}, u32[]{:S(2)}, u32[]{:S(2)}) collective-permute-start(bf16[32,512]{1,0:T(8,128)(2,1)S(1)} %get-tuple-element.30), channel_id=1, source_target_pairs={{0,24},{8,16},{16,8},{24,0},{32,56},{40,48},{48,40},{56,32},{1,25}... | collective-permute-start | bytes 98312 | tf_op jit(solution)/shard_map/ppermute | solution.py:176
  227.0 14.5 %collective-permute-start.37 = (bf16[32,512]{1,0:T(8,128)(2,1)S(1)}, bf16[32,512]{1,0:T(8,128)(2,1)S(1)}, u32[]{:S(2)}, u32[]{:S(2)}) collective-permute-start(bf16[32,512]{1,0:T(8,128)(2,1)S(1)} %get-tuple-element.29), channel_id=1, source_target_pairs={{0,32},{8,40},{16,48},{24,56},{32,0},{40,8},{48,16},{56,24},{1,33}... | collective-permute-start | bytes 98312 | tf_op jit(solution)/shard_map/ppermute | solution.py:176
  241.5 15.4 %collective-permute-start.38 = (bf16[32,512]{1,0:T(8,128)(2,1)S(1)}, bf16[32,512]{1,0:T(8,128)(2,1)S(1)}, u32[]{:S(2)}, u32[]{:S(2)}) collective-permute-start(bf16[32,512]{1,0:T(8,128)(2,1)S(1)} %get-tuple-element.28), channel_id=1, source_target_pairs={{0,40},{8,32},{16,56},{24,48},{32,8},{40,0},{48,24},{56,16},{1,41}... | collective-permute-start | bytes 98312 | tf_op jit(solution)/shard_map/ppermute | solution.py:176
  257.0 17.0 %collective-permute-start.39 = (bf16[32,512]{1,0:T(8,128)(2,1)S(1)}, bf16[32,512]{1,0:T(8,128)(2,1)S(1)}, u32[]{:S(2)}, u32[]{:S(2)}) collective-permute-start(bf16[32,512]{1,0:T(8,128)(2,1)S(1)} %get-tuple-element.27), channel_id=1, source_target_pairs={{0,48},{8,56},{16,32},{24,40},{32,16},{40,24},{48,0},{56,8},{1,49}... | collective-permute-start | bytes 98312 | tf_op jit(solution)/shard_map/ppermute | solution.py:176
  274.0 16.8 %collective-permute-start.40 = (bf16[32,512]{1,0:T(8,128)(2,1)S(1)}, bf16[32,512]{1,0:T(8,128)(2,1)S(1)}, u32[]{:S(2)}, u32[]{:S(2)}) collective-permute-start(bf16[32,512]{1,0:T(8,128)(2,1)S(1)} %get-tuple-element.26), channel_id=1, source_target_pairs={{0,56},{8,48},{16,40},{24,32},{32,24},{40,16},{48,8},{56,0},{1,57}... | collective-permute-start | bytes 98312 | tf_op jit(solution)/shard_map/ppermute | solution.py:176
  290.8 6.9 %collective-permute-start.43 = (bf16[128,512]{1,0:T(8,128)(2,1)S(1)}, bf16[128,512]{1,0:T(8,128)(2,1)S(1)}, u32[]{:S(2)}, u32[]{:S(2)}) collective-permute-start(bf16[128,512]{1,0:T(8,128)(2,1)S(1)} %pad_maximum_fusion.1), channel_id=1, source_target_pairs={{0,2},{1,3},{4,6},{5,7},{8,10},{9,11},{12,14},{13,15},{16,18},{17,... | collective-permute-start | bytes 393224 | tf_op jit(solution)/shard_map/ppermute | solution.py:252
  (2 other events, 4.0 us)

commit v2 on v1

v2 whole, which is shorter than its diff:
```python
import math

import jax
import jax.numpy as jnp
from jax import lax
from jax.experimental import pallas as pl
from jax.experimental.pallas import tpu as pltpu
from jax.sharding import PartitionSpec as P

HEAD_SIZE = 128
QUERY_HEADS = 32
KEY_VALUE_HEADS = 4
GROUP = QUERY_HEADS // KEY_VALUE_HEADS
CHUNK = 128
WINDOW = 3 * CHUNK
KV_WIDTH = KEY_VALUE_HEADS * HEAD_SIZE
BLOCK_AXES = ("x", "core")
SEQ_AXES = ("z", "y")
PLANE_AXES = ("y", "b")


def attend_kernel(
    info_ref,
    segments_ref,
    query_ref,
    grad_ref,
    far_ref,
    near_ref,
    own_ref,
    out_ref,
    grad_query_ref,
    far_grad_ref,
    near_grad_ref,
    own_grad_ref,
    bias_ref,
):
    @pl.when(pl.program_id(0) == 0)
    def _():
        chunk = info_ref[0]
        own_row = segments_ref[pl.ds(chunk, 1), :]
        query_doc = jnp.broadcast_to(own_row, (CHUNK, CHUNK))
        for back in (2, 1, 0):
            at = chunk - back
            row = segments_ref[pl.ds(jnp.maximum(at, 0), 1), :]
            row = jnp.where(at >= 0, row, -1)
            key_doc = jnp.broadcast_to(row, (CHUNK, CHUNK)).T
            usable = key_doc == query_doc
            if back == 0:
                usable &= lax.broadcasted_iota(jnp.int32, (CHUNK, CHUNK), 0) <= (
                    lax.broadcasted_iota(jnp.int32, (CHUNK, CHUNK), 1)
                )
            tile = jnp.where(usable, 0.0, -jnp.inf).astype(jnp.float32)
            rows = pl.ds((2 - back) * CHUNK, CHUNK)
            bias_ref[rows, 0:CHUNK] = tile
            bias_ref[rows, CHUNK : 2 * CHUNK] = tile

    scale = 1.0 / math.sqrt(HEAD_SIZE)
    keys = jnp.concatenate([far_ref[0], near_ref[0], own_ref[0]], axis=0)
    values = jnp.concatenate([far_ref[1], near_ref[1], own_ref[1]], axis=0)
    keys_t = keys.T
    values_t = values.T
    last = (((1,), (1,)), ((), ()))
    plain = (((1,), (0,)), ((), ()))
    weight_parts, dscore_parts, query_parts, grad_parts = [], [], [], []
    for pair in range(GROUP // 2):
        heads = (2 * pair, 2 * pair + 1)
        queries = jnp.concatenate(
            [query_ref[:, a * HEAD_SIZE : (a + 1) * HEAD_SIZE] for a in heads], axis=0
        )
        grads = jnp.concatenate(
            [grad_ref[:, a * HEAD_SIZE : (a + 1) * HEAD_SIZE] for a in heads], axis=0
        )
        scores = lax.dot_general(keys, queries, last, preferred_element_type=jnp.float32)
        scores = scores + bias_ref[...]
        top = jnp.max(scores, axis=0, keepdims=True)
        raised = jnp.exp2((scores - top) * (scale * math.log2(math.e)))
        weights = raised * (1.0 / jnp.sum(raised, axis=0, keepdims=True))
        weights16 = weights.astype(jnp.bfloat16)
        dprob = lax.dot_general(values, grads, last, preferred_element_type=jnp.float32)
        product = weights * dprob
        delta = jnp.sum(product, axis=0, keepdims=True)
        dscore = ((product - weights * delta) * scale).astype(jnp.bfloat16)
        output_t = lax.dot_general(values_t, weights16, plain, preferred_element_type=jnp.float32)
        grad_query_t = lax.dot_general(keys_t, dscore, plain, preferred_element_type=jnp.float32)
        for i, a in enumerate(heads):
            columns = slice(a * HEAD_SIZE, (a + 1) * HEAD_SIZE)
            part = slice(i * CHUNK, (i + 1) * CHUNK)
            out_ref[:, columns] = output_t[:, part].astype(jnp.bfloat16).T
            grad_query_ref[:, columns] = grad_query_t[:, part].astype(jnp.bfloat16).T
        weight_parts.append(weights16)
        dscore_parts.append(dscore)
        query_parts.append(queries)
        grad_parts.append(grads)
    grad_keys = lax.dot_general(
        jnp.concatenate(dscore_parts, axis=1),
        jnp.concatenate(query_parts, axis=0),
        plain,
        preferred_element_type=jnp.float32,
    )
    grad_values = lax.dot_general(
        jnp.concatenate(weight_parts, axis=1),
        jnp.concatenate(grad_parts, axis=0),
        plain,
        preferred_element_type=jnp.float32,
    )
    for i, total in enumerate((grad_keys, grad_values)):
        far_grad_ref[i] = total[:CHUNK].astype(jnp.bfloat16)
        near_grad_ref[i] = total[CHUNK : 2 * CHUNK].astype(jnp.bfloat16)
        own_grad_ref[i] = total[2 * CHUNK :]


def attend(chunk, segments, queries, grads, far, near, own):
    rows = queries.shape[0]
    wide = pl.BlockSpec((rows, GROUP * HEAD_SIZE), lambda g, info: (0, g))
    pair = pl.BlockSpec((2, rows, HEAD_SIZE), lambda g, info: (0, 0, g))
    half = jax.ShapeDtypeStruct((2, rows, KV_WIDTH), jnp.bfloat16)
    full = jax.ShapeDtypeStruct((2, rows, KV_WIDTH), jnp.float32)
    return pl.pallas_call(
        attend_kernel,
        grid_spec=pltpu.PrefetchScalarGridSpec(
            num_scalar_prefetch=1,
            grid=(KEY_VALUE_HEADS,),
            in_specs=[
                pl.BlockSpec(segments.shape, lambda g, info: (0, 0)),
                wide,
                wide,
                pair,
                pair,
                pair,
            ],
            out_specs=[wide, wide, pair, pair, pair],
            scratch_shapes=[pltpu.VMEM((WINDOW, 2 * CHUNK), jnp.float32)],
        ),
        out_shape=[
            jax.ShapeDtypeStruct(queries.shape, jnp.bfloat16),
            jax.ShapeDtypeStruct(queries.shape, jnp.bfloat16),
            half,
            half,
            full,
        ],
        compiler_params=pltpu.CompilerParams(vmem_limit_bytes=48 * 1024 * 1024),
        cost_estimate=pl.CostEstimate(
            flops=6 * 2 * rows * QUERY_HEADS * WINDOW * HEAD_SIZE,
            bytes_accessed=8 * rows * QUERY_HEADS * HEAD_SIZE,
            transcendentals=rows * QUERY_HEADS * WINDOW,
        ),
    )(chunk, segments, queries, grads, far, near, own)


def move(value, moves):
    return lax.ppermute(value, BLOCK_AXES, moves)


def exchange(pieces, axes):
    return lax.all_to_all(pieces, axes, 0, 0)


def pick(stack, index):
    return lax.dynamic_index_in_dim(stack, index, 0, keepdims=False)


def local(queries, keys, values, grads, segment_ids, order):
    s = lax.axis_index(SEQ_AXES)
    z = lax.axis_index("z")
    block = lax.axis_index("b")
    c = lax.axis_index(BLOCK_AXES)
    count = order.shape[0]
    slots = jnp.arange(count, dtype=jnp.int32)
    step = order[:, None] - order[None, :]
    before = jnp.sum(jnp.where((step == 1) | (step == 1 - count), slots[None, :], 0), axis=1)
    after = jnp.sum(jnp.where((step == -1) | (step == count - 1), slots[None, :], 0), axis=1)
    mine = 2 * s + block
    part = (4, CHUNK // 4, KV_WIDTH)

    moved = move(values, [(2, 0), (3, 1)])
    own = jnp.stack([keys, values], axis=0)
    near_in = move(own, [(0, 1), (1, 2), (2, 3)])
    far_in = move(own, [(0, 2), (1, 3)])
    quarter = jnp.where(c >= 2, keys, moved).reshape(part)
    held = exchange(jnp.concatenate([quarter, quarter], axis=0), SEQ_AXES)
    sources = lax.dynamic_slice_in_dim(before, 8 * z, 8) >> 1
    arrived = exchange(jnp.stack([pick(held, sources[i]) for i in range(8)], axis=0), PLANE_AXES)
    arrived = arrived.reshape(4, 2, *part[1:])
    quarter = lax.dynamic_index_in_dim(arrived, pick(before, mine) & 1, 1, keepdims=False)
    quarter = quarter.reshape(CHUNK, KV_WIDTH)
    straight = move(quarter, [(2, 0), (3, 1)])
    to_first = move(quarter, [(1, 0)])
    across = move(quarter, [(3, 0)])
    far = jnp.where(c < 2, jnp.stack([straight, quarter], axis=0), far_in)
    near = jnp.where(c == 0, jnp.stack([across, to_first], axis=0), near_in)

    chunk = (pick(order, mine) * 4 + c).reshape(1)
    attended, grad_query, far_grad, near_grad, own_grad = attend(
        chunk, segment_ids.reshape(-1, CHUNK), queries, grads, far, near, own
    )

    straight = move(far_grad[0], [(0, 2), (1, 3)])
    to_second = move(near_grad[1], [(0, 1)])
    across = move(near_grad[0], [(0, 3)])
    near_back = move(near_grad, [(1, 0), (2, 1), (3, 2)])
    far_back = move(far_grad, [(2, 0), (3, 1)])
    quarter = jnp.where(c < 2, far_grad[1], straight).astype(jnp.float32)
    quarter = quarter + jnp.where(c == 1, to_second, jnp.where(c == 3, across, 0)).astype(jnp.float32)
    quarter = quarter.astype(jnp.bfloat16).reshape(part)
    held = exchange(jnp.repeat(quarter, 2, axis=0), PLANE_AXES)
    targets = lax.dynamic_slice_in_dim(after.reshape(8, 2), block, 1, 1)[:, 0] & 7
    arrived = exchange(jnp.stack([pick(held, targets[i]) for i in range(8)], axis=0), SEQ_AXES)
    quarter = pick(arrived.reshape(2, *part), pick(after, mine) >> 3).reshape(CHUNK, KV_WIDTH)
    moved = move(quarter, [(0, 2), (1, 3)])

    total = own_grad + near_back.astype(jnp.float32) + far_back.astype(jnp.float32)
    late = jnp.where(c >= 2, jnp.stack([quarter, moved], axis=0), 0)
    total = (total + late.astype(jnp.float32)).astype(jnp.bfloat16)
    return attended, grad_query, total[0], total[1]


def solution(mesh):
    names = ("dp", "z", "y", "b", "x", "core")
    fine = jax.sharding.Mesh(mesh.devices.reshape(-1, 2, 4, 2, 2, 2), names)
    rows = P(names, None)
    return jax.shard_map(
        local,
        mesh=fine,
        in_specs=(rows, rows, rows, rows, P("dp"), P("dp")),
        out_specs=(rows, rows, rows, rows),
        check_vma=False,
    )
```

time: 300 us -> 169 us (0.56)
  the two profiles are of different devices: /device:TPU:6 before, /device:TPU:38 now
where the time goes in v2:
time: 169 us; the launch traced here: 167 us
  starting transfers between devices  57.9 us (34%)
  waiting for transfers between devices  47.2 us (28%)
  between operations  33.1 us (20%)
  local copies, waits for them, and re-layouts  15.8 us (9%)
  Pallas kernels  11.1 us (7%)
  other arithmetic  2.31 us (1%)
    all_to_all x4, starting transfers between devices, exchange(): return lax.all_to_all(pieces, axes, 0, 0)  38.7 us
    all_to_all x4, waiting for transfers between devices, exchange(): return lax.all_to_all(pieces, axes, 0, 0)  27.9 us
    ppermute x12, waiting for transfers between devices, move(): return lax.ppermute(value, BLOCK_AXES, moves)  19.2 us
    ppermute x12, starting transfers between devices, move(): return lax.ppermute(value, BLOCK_AXES, moves)  19.2 us
    pallas_call x1, Pallas kernels, attend(): pl.pallas_call(attend_kernel, grid_spec=pltpu.PrefetchScalarGridSpec(num_...  11.1 us
    unnamed x26, local copies, waits for them, and re-layouts  9.99 us
  transfers between devices with their start and end apart: 16, of which 8 were waited for; matrix products, arithmetic and copies ran while one was open for 2% of the time, Pallas kernels for 0%

profile of v2, /device:TPU:38, one launch (start us, length us, event | category | flops | bytes accessed | tf_op | source)
XLA Modules:
  0.0 167.4 jit_solution(4248598594745520701)
XLA Ops:
  0.6 2.7 %collective-permute-start = (bf16[128,512]{1,0:T(8,128)(2,1)}, bf16[128,512]{1,0:T(8,128)(2,1)S(1)}, u32[]{:S(2)}, u32[]{:S(2)}) collective-permute-start(bf16[128,512]{1,0:T(8,128)(2,1)} %param.8), channel_id=1, source_target_pairs={{2,0},{3,1},{6,4},{7,5},{10,8},{11,9},{14,12},{15,13},{18,16},{19,... | collective-permute-start | bytes 393224 | tf_op jit(solution)/shard_map/ppermute | solution.py:151
  3.4 3.0 %collective-permute-done = bf16[128,512]{1,0:T(8,128)(2,1)S(1)} collective-permute-done((bf16[128,512]{1,0:T(8,128)(2,1)}, bf16[128,512]{1,0:T(8,128)(2,1)S(1)}, u32[]{:S(2)}, u32[]{:S(2)}) %collective-permute-start) | collective-permute-done | bytes 131104 | tf_op jit(solution)/shard_map/ppermute | solution.py:151
  6.4 0.9 broadcast_select_fusion
  7.3 0.7 pad_maximum_fusion
  8.1 16.8 %all-to-all-start = ((bf16[8,32,512]{2,1,0:T(8,128)(2,1)}), bf16[8,32,512]{2,1,0:T(8,128)(2,1)S(1)}, u32[]{:S(2)}, u32[]{:S(2)}) async-start(bf16[8,32,512]{2,1,0:T(8,128)(2,1)} %pad_maximum_fusion), calls=%async_computation | async-start | bytes 524288 | tf_op jit(solution)/shard_map/all_to_all | solution.py:155
  24.9 0.7 copy-done.5
  25.8 0.7 fusion.4
  41.8 6.5 %all-to-all-done = bf16[8,32,512]{2,1,0:T(8,128)(2,1)S(1)} async-done(((bf16[8,32,512]{2,1,0:T(8,128)(2,1)}), bf16[8,32,512]{2,1,0:T(8,128)(2,1)S(1)}, u32[]{:S(2)}, u32[]{:S(2)}) %all-to-all-start) | async-done | bytes 262176 | tf_op jit(solution)/shard_map/all_to_all | solution.py:155
  48.4 0.6 constant_dynamic-update-slice_fusion.7
  49.0 0.6 constant_dynamic-update-slice_fusion.6
  49.6 0.6 constant_dynamic-update-slice_fusion.5
  50.2 0.6 constant_dynamic-update-slice_fusion.4
  50.8 0.6 constant_dynamic-update-slice_fusion.3
  51.5 0.6 constant_dynamic-update-slice_fusion.2
  52.1 0.6 constant_dynamic-update-slice_fusion.1
  52.7 0.6 constant_dynamic-update-slice_fusion
  53.3 5.3 %all-to-all-start.1 = ((bf16[8,32,512]{2,1,0:T(8,128)(2,1)}), bf16[8,32,512]{2,1,0:T(8,128)(2,1)S(1)}, u32[]{:S(2)}, u32[]{:S(2)}) async-start(bf16[8,32,512]{2,1,0:T(8,128)(2,1)} %constant_dynamic-update-slice_fusion), calls=%async_computation.1 | async-start | bytes 524288 | tf_op jit(solution)/shard_map/all_to_all | solution.py:155
  58.7 2.1 %collective-permute-start.5 = (bf16[2,128,512]{2,1,0:T(8,128)(2,1)S(1)}, bf16[2,128,512]{2,1,0:T(8,128)(2,1)S(1)}, u32[]{:S(2)}, u32[]{:S(2)}) collective-permute-start(bf16[2,128,512]{2,1,0:T(8,128)(2,1)S(1)} %pad_maximum_fusion.1.own_ref), channel_id=1, source_target_pairs={{0,1},{1,2},{2,3},{4,5},{5,6},{6,7},{8,9},{9,10},{10,11},{12,13},{... | collective-permute-start | bytes 786440 | tf_op jit(solution)/shard_map/ppermute | solution.py:151
  62.0 2.7 %all-to-all-done.1 = bf16[8,32,512]{2,1,0:T(8,128)(2,1)S(1)} async-done(((bf16[8,32,512]{2,1,0:T(8,128)(2,1)}), bf16[8,32,512]{2,1,0:T(8,128)(2,1)S(1)}, u32[]{:S(2)}, u32[]{:S(2)}) %all-to-all-start.1) | async-done | bytes 262176 | tf_op jit(solution)/shard_map/all_to_all | solution.py:155
  64.7 0.7 collective-permute-start.3
  65.4 0.7 collective-permute-start.4
  66.1 1.3 collective-permute-start.2
  68.6 4.6 %collective-permute-start.1 = (bf16[128,512]{1,0:T(8,128)(2,1)S(1)}, bf16[128,512]{1,0:T(8,128)(2,1)S(1)}, u32[]{:S(2)}, u32[]{:S(2)}) collective-permute-start(bf16[128,512]{1,0:T(8,128)(2,1)S(1)} %bitcast.60), channel_id=1, source_target_pairs={{2,0},{3,1},{6,4},{7,5},{10,8},{11,9},{14,12},{15,13},{18,16},{19,... | collective-permute-start | bytes 393224 | tf_op jit(solution)/shard_map/ppermute | solution.py:151
  73.4 2.0 %collective-permute-done.2 = bf16[2,128,512]{2,1,0:T(8,128)(2,1)S(1)} collective-permute-done((bf16[2,128,512]{2,1,0:T(8,128)(2,1)S(1)}, bf16[2,128,512]{2,1,0:T(8,128)(2,1)S(1)}, u32[]{:S(2)}, u32[]{:S(2)}) %collective-permute-start.2) | collective-permute-done | bytes 262176 | tf_op jit(solution)/shard_map/ppermute | solution.py:151
  75.9 0.7 copy-done.2
  76.6 11.1 %shard_map.93 = (bf16[128,4096]{1,0:T(8,128)(2,1)}, bf16[128,4096]{1,0:T(8,128)(2,1)}, bf16[2,128,512]{2,1,0:T(8,128)(2,1)S(1)}, bf16[2,128,512]{2,1,0:T(8,128)(2,1)S(1)}, f32[2,128,512]{2,1,0:T(8,128)S(1)}) custom-call(s32[1]{0:T(128)} %bitcast.1.info_ref, s32[64,128]{1,0:T(8,128)S(1)} %bitcast.50, bf16[128,4096]{1,0:T(8,128)(2,1)S(1)} %copy-done, ...), custom_call_target="tpu_custom_call" | custom-call | flops 2415919104 | bytes 4194304 | tf_op jit(solution)/shard_map/pallas_call | solution.py:118
  87.7 0.7 collective-permute-start.10
  88.3 0.7 collective-permute-start.9
  89.0 1.3 collective-permute-start.8
  90.4 8.2 %collective-permute-done.8 = bf16[128,512]{1,0:T(8,128)(2,1)S(1)} collective-permute-done((bf16[128,512]{1,0:T(8,128)(2,1)S(1)}, bf16[128,512]{1,0:T(8,128)(2,1)S(1)}, u32[]{:S(2)}, u32[]{:S(2)}) %collective-permute-start.8) | collective-permute-done | bytes 131104 | tf_op jit(solution)/shard_map/ppermute | solution.py:151
  98.7 0.7 broadcast_in_dim.36
  99.4 6.6 %all-to-all-start.2 = ((bf16[8,32,512]{2,1,0:T(8,128)(2,1)}), bf16[8,32,512]{2,1,0:T(8,128)(2,1)S(1)}, u32[]{:S(2)}, u32[]{:S(2)}) async-start(bf16[8,32,512]{2,1,0:T(8,128)(2,1)} %bitcast.26), calls=%async_computation.2 | async-start | bytes 524288 | tf_op jit(solution)/shard_map/all_to_all | solution.py:155
  106.1 0.6 fusion.3
  121.6 0.6 constant_dynamic-update-slice_fusion.15
  122.3 0.6 constant_dynamic-update-slice_fusion.14
  122.9 0.6 constant_dynamic-update-slice_fusion.13
  123.5 0.6 constant_dynamic-update-slice_fusion.12
  124.1 0.6 constant_dynamic-update-slice_fusion.11
  124.7 0.6 constant_dynamic-update-slice_fusion.10
  125.3 0.6 constant_dynamic-update-slice_fusion.9
  125.9 0.6 constant_dynamic-update-slice_fusion.8
  126.5 10.0 %all-to-all-start.3 = ((bf16[8,32,512]{2,1,0:T(8,128)(2,1)}), bf16[8,32,512]{2,1,0:T(8,128)(2,1)S(1)}, u32[]{:S(2)}, u32[]{:S(2)}) async-start(bf16[8,32,512]{2,1,0:T(8,128)(2,1)} %constant_dynamic-update-slice_fusion.8), calls=%async_computation.3 | async-start | bytes 524288 | tf_op jit(solution)/shard_map/all_to_all | solution.py:155
  136.5 1.9 %collective-permute-start.6 = (bf16[2,128,512]{2,1,0:T(8,128)(2,1)S(1)}, bf16[2,128,512]{2,1,0:T(8,128)(2,1)S(1)}, u32[]{:S(2)}, u32[]{:S(2)}) collective-permute-start(bf16[2,128,512]{2,1,0:T(8,128)(2,1)S(1)} %get-tuple-element.12), channel_id=1, source_target_pairs={{1,0},{2,1},{3,2},{5,4},{6,5},{7,6},{9,8},{10,9},{11,10},{13,12},{... | collective-permute-start | bytes 786440 | tf_op jit(solution)/shard_map/ppermute | solution.py:151
  138.4 1.3 collective-permute-start.7
  141.0 18.6 %all-to-all-done.3 = bf16[8,32,512]{2,1,0:T(8,128)(2,1)S(1)} async-done(((bf16[8,32,512]{2,1,0:T(8,128)(2,1)}), bf16[8,32,512]{2,1,0:T(8,128)(2,1)S(1)}, u32[]{:S(2)}, u32[]{:S(2)}) %all-to-all-start.3) | async-done | bytes 262176 | tf_op jit(solution)/shard_map/all_to_all | solution.py:155
  159.7 1.3 collective-permute-start.11
  161.0 5.5 %collective-permute-done.11 = bf16[128,512]{1,0:T(8,128)(2,1)S(1)} collective-permute-done((bf16[128,512]{1,0:T(8,128)(2,1)S(1)}, bf16[128,512]{1,0:T(8,128)(2,1)S(1)}, u32[]{:S(2)}, u32[]{:S(2)}) %collective-permute-start.11) | collective-permute-done | bytes 131104 | tf_op jit(solution)/shard_map/ppermute | solution.py:151
  166.7 0.7 slice_bitcast_fusion
  (35 shorter events, 3.0 us)
Async XLA Ops:
  0.6 5.8 %collective-permute-start = (bf16[128,512]{1,0:T(8,128)(2,1)}, bf16[128,512]{1,0:T(8,128)(2,1)S(1)}, u32[]{:S(2)}, u32[]{:S(2)}) collective-permute-start(bf16[128,512]{1,0:T(8,128)(2,1)} %param.8), channel_id=1, source_target_pairs={{2,0},{3,1},{6,4},{7,5},{10,8},{11,9},{14,12},{15,13},{18,16},{19,... | collective-permute-start | bytes 393224 | tf_op jit(solution)/shard_map/ppermute | solution.py:151
  8.1 40.3 %all-to-all-start = ((bf16[8,32,512]{2,1,0:T(8,128)(2,1)}), bf16[8,32,512]{2,1,0:T(8,128)(2,1)S(1)}, u32[]{:S(2)}, u32[]{:S(2)}) async-start(bf16[8,32,512]{2,1,0:T(8,128)(2,1)} %pad_maximum_fusion), calls=%async_computation | async-start | bytes 524288 | tf_op jit(solution)/shard_map/all_to_all | solution.py:155
  24.9 0.7 copy-start.5
  53.3 5.3 %copy-start.3 = (bf16[128,512]{1,0:T(8,128)(2,1)S(1)}, bf16[128,512]{1,0:T(8,128)(2,1)}, u32[]{:S(2)}) copy-start(bf16[128,512]{1,0:T(8,128)(2,1)} %param.7) | copy-start | bytes 393220
  53.3 5.3 %copy-start.4 = (bf16[128,512]{1,0:T(8,128)(2,1)S(1)}, bf16[128,512]{1,0:T(8,128)(2,1)}, u32[]{:S(2)}) copy-start(bf16[128,512]{1,0:T(8,128)(2,1)} %param.8) | copy-start | bytes 393220
  53.3 11.4 %all-to-all-start.1 = ((bf16[8,32,512]{2,1,0:T(8,128)(2,1)}), bf16[8,32,512]{2,1,0:T(8,128)(2,1)S(1)}, u32[]{:S(2)}, u32[]{:S(2)}) async-start(bf16[8,32,512]{2,1,0:T(8,128)(2,1)} %constant_dynamic-update-slice_fusion), calls=%async_computation.1 | async-start | bytes 524288 | tf_op jit(solution)/shard_map/all_to_all | solution.py:155
  58.6 17.2 %copy-start.1 = (bf16[128,4096]{1,0:T(8,128)(2,1)S(1)}, bf16[128,4096]{1,0:T(8,128)(2,1)}, u32[]{:S(2)}) copy-start(bf16[128,4096]{1,0:T(8,128)(2,1)} %grad_ref.1) | copy-start | bytes 3145732
  58.7 17.2 %copy-start = (bf16[128,4096]{1,0:T(8,128)(2,1)S(1)}, bf16[128,4096]{1,0:T(8,128)(2,1)}, u32[]{:S(2)}) copy-start(bf16[128,4096]{1,0:T(8,128)(2,1)} %query_ref.1) | copy-start | bytes 3145732
  58.7 14.6 %collective-permute-start.5 = (bf16[2,128,512]{2,1,0:T(8,128)(2,1)S(1)}, bf16[2,128,512]{2,1,0:T(8,128)(2,1)S(1)}, u32[]{:S(2)}, u32[]{:S(2)}) collective-permute-start(bf16[2,128,512]{2,1,0:T(8,128)(2,1)S(1)} %pad_maximum_fusion.1.own_ref), channel_id=1, source_target_pairs={{0,1},{1,2},{2,3},{4,5},{5,6},{6,7},{8,9},{9,10},{10,11},{12,13},{... | collective-permute-start | bytes 786440 | tf_op jit(solution)/shard_map/ppermute | solution.py:151
  64.7 8.6 %collective-permute-start.3 = (bf16[128,512]{1,0:T(8,128)(2,1)S(1)}, bf16[128,512]{1,0:T(8,128)(2,1)S(1)}, u32[]{:S(2)}, u32[]{:S(2)}) collective-permute-start(bf16[128,512]{1,0:T(8,128)(2,1)S(1)} %bitcast.58), channel_id=1, source_target_pairs={{3,0},{7,4},{11,8},{15,12},{19,16},{23,20},{27,24},{31,28},{35,32}... | collective-permute-start | bytes 393224 | tf_op jit(solution)/shard_map/ppermute | solution.py:151
  65.4 7.9 %collective-permute-start.4 = (bf16[128,512]{1,0:T(8,128)(2,1)S(1)}, bf16[128,512]{1,0:T(8,128)(2,1)S(1)}, u32[]{:S(2)}, u32[]{:S(2)}) collective-permute-start(bf16[128,512]{1,0:T(8,128)(2,1)S(1)} %bitcast.59), channel_id=1, source_target_pairs={{1,0},{5,4},{9,8},{13,12},{17,16},{21,20},{25,24},{29,28},{33,32},... | collective-permute-start | bytes 393224 | tf_op jit(solution)/shard_map/ppermute | solution.py:151
  66.1 9.3 %collective-permute-start.2 = (bf16[2,128,512]{2,1,0:T(8,128)(2,1)S(1)}, bf16[2,128,512]{2,1,0:T(8,128)(2,1)S(1)}, u32[]{:S(2)}, u32[]{:S(2)}) collective-permute-start(bf16[2,128,512]{2,1,0:T(8,128)(2,1)S(1)} %pad_maximum_fusion.1.own_ref), channel_id=1, source_target_pairs={{0,2},{1,3},{4,6},{5,7},{8,10},{9,11},{12,14},{13,15},{16,18},{17,... | collective-permute-start | bytes 786440 | tf_op jit(solution)/shard_map/ppermute | solution.py:151
  68.6 7.2 %collective-permute-start.1 = (bf16[128,512]{1,0:T(8,128)(2,1)S(1)}, bf16[128,512]{1,0:T(8,128)(2,1)S(1)}, u32[]{:S(2)}, u32[]{:S(2)}) collective-permute-start(bf16[128,512]{1,0:T(8,128)(2,1)S(1)} %bitcast.60), channel_id=1, source_target_pairs={{2,0},{3,1},{6,4},{7,5},{10,8},{11,9},{14,12},{15,13},{18,16},{19,... | collective-permute-start | bytes 393224 | tf_op jit(solution)/shard_map/ppermute | solution.py:151
  75.8 0.8 copy-start.2
  87.7 2.7 %collective-permute-start.10 = (bf16[128,512]{1,0:T(8,128)(2,1)S(1)}, bf16[128,512]{1,0:T(8,128)(2,1)S(1)}, u32[]{:S(2)}, u32[]{:S(2)}) collective-permute-start(bf16[128,512]{1,0:T(8,128)(2,1)S(1)} %get-tuple-element.18), channel_id=1, source_target_pairs={{0,3},{4,7},{8,11},{12,15},{16,19},{20,23},{24,27},{28,31},{32,35}... | collective-permute-start | bytes 393224 | tf_op jit(solution)/shard_map/ppermute | solution.py:151
  88.3 2.0 %collective-permute-start.9 = (bf16[128,512]{1,0:T(8,128)(2,1)S(1)}, bf16[128,512]{1,0:T(8,128)(2,1)S(1)}, u32[]{:S(2)}, u32[]{:S(2)}) collective-permute-start(bf16[128,512]{1,0:T(8,128)(2,1)S(1)} %get-tuple-element.19), channel_id=1, source_target_pairs={{0,1},{4,5},{8,9},{12,13},{16,17},{20,21},{24,25},{28,29},{32,33},... | collective-permute-start | bytes 393224 | tf_op jit(solution)/shard_map/ppermute | solution.py:151
  89.0 9.5 %collective-permute-start.8 = (bf16[128,512]{1,0:T(8,128)(2,1)S(1)}, bf16[128,512]{1,0:T(8,128)(2,1)S(1)}, u32[]{:S(2)}, u32[]{:S(2)}) collective-permute-start(bf16[128,512]{1,0:T(8,128)(2,1)S(1)} %slice_bitcast_fusion.4), channel_id=1, source_target_pairs={{0,2},{1,3},{4,6},{5,7},{8,10},{9,11},{12,14},{13,15},{16,18},{17,... | collective-permute-start | bytes 393224 | tf_op jit(solution)/shard_map/ppermute | solution.py:151
  99.4 22.3 %all-to-all-start.2 = ((bf16[8,32,512]{2,1,0:T(8,128)(2,1)}), bf16[8,32,512]{2,1,0:T(8,128)(2,1)S(1)}, u32[]{:S(2)}, u32[]{:S(2)}) async-start(bf16[8,32,512]{2,1,0:T(8,128)(2,1)} %bitcast.26), calls=%async_computation.2 | async-start | bytes 524288 | tf_op jit(solution)/shard_map/all_to_all | solution.py:155
  126.5 33.1 %all-to-all-start.3 = ((bf16[8,32,512]{2,1,0:T(8,128)(2,1)}), bf16[8,32,512]{2,1,0:T(8,128)(2,1)S(1)}, u32[]{:S(2)}, u32[]{:S(2)}) async-start(bf16[8,32,512]{2,1,0:T(8,128)(2,1)} %constant_dynamic-update-slice_fusion.8), calls=%async_computation.3 | async-start | bytes 524288 | tf_op jit(solution)/shard_map/all_to_all | solution.py:155
  136.5 24.4 %collective-permute-start.6 = (bf16[2,128,512]{2,1,0:T(8,128)(2,1)S(1)}, bf16[2,128,512]{2,1,0:T(8,128)(2,1)S(1)}, u32[]{:S(2)}, u32[]{:S(2)}) collective-permute-start(bf16[2,128,512]{2,1,0:T(8,128)(2,1)S(1)} %get-tuple-element.12), channel_id=1, source_target_pairs={{1,0},{2,1},{3,2},{5,4},{6,5},{7,6},{9,8},{10,9},{11,10},{13,12},{... | collective-permute-start | bytes 786440 | tf_op jit(solution)/shard_map/ppermute | solution.py:151
  138.4 22.5 %collective-permute-start.7 = (bf16[2,128,512]{2,1,0:T(8,128)(2,1)S(1)}, bf16[2,128,512]{2,1,0:T(8,128)(2,1)S(1)}, u32[]{:S(2)}, u32[]{:S(2)}) collective-permute-start(bf16[2,128,512]{2,1,0:T(8,128)(2,1)S(1)} %get-tuple-element.13), channel_id=1, source_target_pairs={{2,0},{3,1},{6,4},{7,5},{10,8},{11,9},{14,12},{15,13},{18,16},{19,... | collective-permute-start | bytes 786440 | tf_op jit(solution)/shard_map/ppermute | solution.py:151
  159.7 6.9 %collective-permute-start.11 = (bf16[128,512]{1,0:T(8,128)(2,1)S(1)}, bf16[128,512]{1,0:T(8,128)(2,1)S(1)}, u32[]{:S(2)}, u32[]{:S(2)}) collective-permute-start(bf16[128,512]{1,0:T(8,128)(2,1)S(1)} %bitcast.53), channel_id=1, source_target_pairs={{0,2},{1,3},{4,6},{5,7},{8,10},{9,11},{12,14},{13,15},{16,18},{17,... | collective-permute-start | bytes 393224 | tf_op jit(solution)/shard_map/ppermute | solution.py:151

commit v3 on v2

v3 whole, which is shorter than its diff:
```python
import functools
import math

import jax
import jax.numpy as jnp
from jax import lax
from jax.experimental import pallas as pl
from jax.experimental.pallas import tpu as pltpu
from jax.sharding import PartitionSpec as P

HEAD_SIZE = 128
QUERY_HEADS = 32
KEY_VALUE_HEADS = 4
GROUP = QUERY_HEADS // KEY_VALUE_HEADS
CHUNK = 128
WINDOW = 3 * CHUNK
KV_WIDTH = KEY_VALUE_HEADS * HEAD_SIZE
BLOCK_AXES = ("x", "core")
SEQ_AXES = ("z", "y")
PLANE_AXES = ("y", "b")


def usable_bias(chunk, segments_ref, bias_ref):
    query_doc = jnp.broadcast_to(segments_ref[pl.ds(chunk, 1), :], (CHUNK, CHUNK))
    for back in (2, 1, 0):
        at = chunk - back
        row = segments_ref[pl.ds(jnp.maximum(at, 0), 1), :]
        row = jnp.where(at >= 0, row, -1)
        usable = jnp.broadcast_to(row, (CHUNK, CHUNK)).T == query_doc
        if back == 0:
            usable &= lax.broadcasted_iota(jnp.int32, (CHUNK, CHUNK), 0) <= (
                lax.broadcasted_iota(jnp.int32, (CHUNK, CHUNK), 1)
            )
        tile = jnp.where(usable, 0.0, -jnp.inf).astype(jnp.float32)
        rows = pl.ds((2 - back) * CHUNK, CHUNK)
        bias_ref[rows, 0:CHUNK] = tile
        bias_ref[rows, CHUNK : 2 * CHUNK] = tile


def stacked(ref, heads):
    return jnp.concatenate(
        [ref[:, a * HEAD_SIZE : (a + 1) * HEAD_SIZE] for a in heads], axis=0
    )


LAST = (((1,), (1,)), ((), ()))
PLAIN = (((1,), (0,)), ((), ()))


def dot(left, right, dims):
    return lax.dot_general(left, right, dims, preferred_element_type=jnp.float32)


def score_kernel(
    order_ref,
    place_ref,
    segments_ref,
    query_ref,
    grad_ref,
    far_ref,
    near_ref,
    own_ref,
    weight_ref,
    dscore_ref,
    far_grad_ref,
    near_grad_ref,
    bias_ref,
):
    @pl.when(pl.program_id(0) == 0)
    def _():
        usable_bias(order_ref[place_ref[2]] * 4 + place_ref[3], segments_ref, bias_ref)

    scale = 1.0 / math.sqrt(HEAD_SIZE)
    keys = jnp.concatenate([far_ref[0], near_ref[0], own_ref[0]], axis=0)
    values = jnp.concatenate([far_ref[1], near_ref[1], own_ref[1]], axis=0)
    width = 2 * CHUNK
    for pair in range(GROUP // 2):
        heads = (2 * pair, 2 * pair + 1)
        scores = dot(keys, stacked(query_ref, heads), LAST) + bias_ref[...]
        top = jnp.max(scores, axis=0, keepdims=True)
        raised = jnp.exp2((scores - top) * (scale * math.log2(math.e)))
        weights = raised * (1.0 / jnp.sum(raised, axis=0, keepdims=True))
        product = weights * dot(values, stacked(grad_ref, heads), LAST)
        delta = jnp.sum(product, axis=0, keepdims=True)
        columns = pl.ds(pair * width, width)
        weight_ref[:, columns] = weights.astype(jnp.bfloat16)
        dscore_ref[:, columns] = ((product - weights * delta) * scale).astype(jnp.bfloat16)
    every = range(GROUP)
    halo = pl.ds(0, 2 * CHUNK)
    grad_keys = dot(dscore_ref[halo, :], stacked(query_ref, every), PLAIN).astype(jnp.bfloat16)
    grad_values = dot(weight_ref[halo, :], stacked(grad_ref, every), PLAIN).astype(jnp.bfloat16)
    for i, total in enumerate((grad_keys, grad_values)):
        far_grad_ref[i] = total[:CHUNK]
        near_grad_ref[i] = total[CHUNK:]


def output_kernel(
    query_ref,
    grad_ref,
    far_ref,
    near_ref,
    own_ref,
    weight_ref,
    dscore_ref,
    out_ref,
    grad_query_ref,
    own_grad_ref,
):
    keys_t = jnp.concatenate([far_ref[0], near_ref[0], own_ref[0]], axis=0).T
    values_t = jnp.concatenate([far_ref[1], near_ref[1], own_ref[1]], axis=0).T
    width = 2 * CHUNK
    for pair in range(GROUP // 2):
        columns = pl.ds(pair * width, width)
        output_t = dot(values_t, weight_ref[:, columns], PLAIN).astype(jnp.bfloat16)
        grad_query_t = dot(keys_t, dscore_ref[:, columns], PLAIN).astype(jnp.bfloat16)
        for i in range(2):
            columns = pl.ds(pair * width + i * CHUNK, CHUNK)
            part = slice(i * CHUNK, (i + 1) * CHUNK)
            out_ref[:, columns] = output_t[:, part].T
            grad_query_ref[:, columns] = grad_query_t[:, part].T
    every = range(GROUP)
    own = pl.ds(2 * CHUNK, CHUNK)
    own_grad_ref[0] = dot(dscore_ref[own, :], stacked(query_ref, every), PLAIN)
    own_grad_ref[1] = dot(weight_ref[own, :], stacked(grad_ref, every), PLAIN)


def attention_specs(rows):
    wide = pl.BlockSpec((rows, GROUP * HEAD_SIZE), lambda g, *_: (0, g))
    pair = pl.BlockSpec((2, rows, HEAD_SIZE), lambda g, *_: (0, 0, g))
    window = pl.BlockSpec((WINDOW, GROUP * HEAD_SIZE), lambda g, *_: (0, g))
    return wide, pair, window


def scores_and_halo(order, place, segments, queries, grads, far, near, own):
    rows = queries.shape[0]
    wide, pair, window = attention_specs(rows)
    held = jax.ShapeDtypeStruct((WINDOW, queries.shape[1]), jnp.bfloat16)
    half = jax.ShapeDtypeStruct((2, rows, KV_WIDTH), jnp.bfloat16)
    return pl.pallas_call(
        score_kernel,
        grid_spec=pltpu.PrefetchScalarGridSpec(
            num_scalar_prefetch=2,
            grid=(KEY_VALUE_HEADS,),
            in_specs=[pl.BlockSpec(segments.shape, lambda g, *_: (0, 0)), wide, wide, pair, pair, pair],
            out_specs=[window, window, pair, pair],
            scratch_shapes=[pltpu.VMEM((WINDOW, 2 * CHUNK), jnp.float32)],
        ),
        out_shape=[held, held, half, half],
        compiler_params=pltpu.CompilerParams(vmem_limit_bytes=32 * 1024 * 1024),
        cost_estimate=pl.CostEstimate(
            flops=7 * rows * QUERY_HEADS * WINDOW * HEAD_SIZE,
            bytes_accessed=16 * rows * QUERY_HEADS * HEAD_SIZE,
            transcendentals=rows * QUERY_HEADS * WINDOW,
        ),
    )(order, place, segments, queries, grads, far, near, own)


def outputs_and_own(queries, grads, far, near, own, weights, dscores):
    rows = queries.shape[0]
    wide, pair, window = attention_specs(rows)
    like = jax.ShapeDtypeStruct(queries.shape, jnp.bfloat16)
    return pl.pallas_call(
        output_kernel,
        grid=(KEY_VALUE_HEADS,),
        in_specs=[wide, wide, pair, pair, pair, window, window],
        out_specs=[wide, wide, pair],
        out_shape=[like, like, jax.ShapeDtypeStruct((2, rows, KV_WIDTH), jnp.float32)],
        compiler_params=pltpu.CompilerParams(vmem_limit_bytes=32 * 1024 * 1024),
        cost_estimate=pl.CostEstimate(
            flops=5 * rows * QUERY_HEADS * WINDOW * HEAD_SIZE,
            bytes_accessed=20 * rows * QUERY_HEADS * HEAD_SIZE,
            transcendentals=0,
        ),
    )(queries, grads, far, near, own, weights, dscores)


def route_kernel(forward, order_ref, place_ref, held_ref, out_ref, slot_ref):
    count = order_ref.shape[0]
    for j in range(count):
        slot_ref[order_ref[j]] = j
    z, block = place_ref[0], place_ref[1]
    for i in range(8):
        if forward:
            other = slot_ref[lax.rem(order_ref[8 * z + i] + count - 1, count)]
            index, mine = lax.div(other, 2), lax.rem(other, 2) == block
        else:
            other = slot_ref[lax.rem(order_ref[2 * i + block] + 1, count)]
            index, mine = lax.rem(other, 8), lax.div(other, 8) == z

        @pl.when(mine)
        def _(i=i, index=index):
            out_ref[i] = held_ref[index]

        @pl.when(jnp.logical_not(mine))
        def _(i=i):
            out_ref[i] = jnp.zeros(out_ref.shape[1:], out_ref.dtype)


def route(order, place, held, forward):
    whole = pl.BlockSpec(held.shape, lambda i, *_: (0, 0, 0))
    return pl.pallas_call(
        functools.partial(route_kernel, forward),
        grid_spec=pltpu.PrefetchScalarGridSpec(
            num_scalar_prefetch=2,
            grid=(1,),
            in_specs=[whole],
            out_specs=whole,
            scratch_shapes=[pltpu.SMEM((order.shape[0],), jnp.int32)],
        ),
        out_shape=jax.ShapeDtypeStruct(held.shape, held.dtype),
        cost_estimate=pl.CostEstimate(flops=0, bytes_accessed=4 * held.size, transcendentals=0),
    )(order, place, held)


def move(value, moves):
    return lax.ppermute(value, BLOCK_AXES, moves)


def exchange(pieces, axes):
    return lax.all_to_all(pieces, axes, 0, 0)


def local(queries, keys, values, grads, segment_ids, order):
    z = lax.axis_index("z")
    block = lax.axis_index("b")
    c = lax.axis_index(BLOCK_AXES)
    place = jnp.stack([z, block, 8 * z + 2 * lax.axis_index("y") + block, c]).astype(jnp.int32)
    part = (4, CHUNK // 4, KV_WIDTH)
    whole = (CHUNK, KV_WIDTH)

    moved = move(values, [(2, 0), (3, 1)])
    own = jnp.stack([keys, values], axis=0)
    near_in = move(own, [(0, 1), (1, 2), (2, 3)])
    far_in = move(own, [(0, 2), (1, 3)])
    quarter = jnp.where(c >= 2, keys, moved).reshape(part)
    held = exchange(jnp.concatenate([quarter, quarter], axis=0), SEQ_AXES)
    held, near_in, far_in = lax.optimization_barrier((held, near_in, far_in))
    arrived = exchange(route(order, place, held, True), PLANE_AXES).reshape(4, 2, *part[1:])
    quarter = (arrived[:, 0] + arrived[:, 1]).reshape(whole)
    straight = move(quarter, [(2, 0), (3, 1)])
    to_first = move(quarter, [(1, 0)])
    across = move(quarter, [(3, 0)])
    far = jnp.where(c < 2, jnp.stack([straight, quarter], axis=0), far_in)
    near = jnp.where(c == 0, jnp.stack([across, to_first], axis=0), near_in)

    weights, dscores, far_grad, near_grad = scores_and_halo(
        order, place, segment_ids.reshape(-1, CHUNK), queries, grads, far, near, own
    )

    straight = move(far_grad[0], [(0, 2), (1, 3)])
    to_second = move(near_grad[1], [(0, 1)])
    across = move(near_grad[0], [(0, 3)])
    quarter = jnp.where(c < 2, far_grad[1], straight).astype(jnp.float32)
    quarter = quarter + jnp.where(c == 1, to_second, jnp.where(c == 3, across, 0)).astype(jnp.float32)
    quarter = quarter.astype(jnp.bfloat16).reshape(part)
    pieces = jnp.repeat(quarter, 2, axis=0)
    pieces, weights, dscores = lax.optimization_barrier((pieces, weights, dscores))
    held = exchange(pieces, PLANE_AXES)
    attended, grad_query, own_grad = outputs_and_own(queries, grads, far, near, own, weights, dscores)
    near_back = move(near_grad, [(1, 0), (2, 1), (3, 2)])
    far_back = move(far_grad, [(2, 0), (3, 1)])
    arrived = exchange(route(order, place, held, False), SEQ_AXES).reshape(2, *part)
    quarter = (arrived[0] + arrived[1]).reshape(whole)
    moved = move(quarter, [(0, 2), (1, 3)])

    total = own_grad + near_back.astype(jnp.float32) + far_back.astype(jnp.float32)
    key_gradient = total[0] + jnp.where(c >= 2, quarter, 0).astype(jnp.float32)
    value_gradient = total[1] + moved.astype(jnp.float32)
    return (
        attended,
        grad_query,
        key_gradient.astype(jnp.bfloat16),
        value_gradient.astype(jnp.bfloat16),
    )


def solution(mesh):
    names = ("dp", "z", "y", "b", "x", "core")
    fine = jax.sharding.Mesh(mesh.devices.reshape(-1, 2, 4, 2, 2, 2), names)
    rows = P(names, None)
    return jax.shard_map(
        local,
        mesh=fine,
        in_specs=(rows, rows, rows, rows, P("dp"), P("dp")),
        out_specs=(rows, rows, rows, rows),
        check_vma=False,
    )
```

time: 169 us -> 149 us (0.88)
  the two profiles are of different devices: /device:TPU:38 before, /device:TPU:34 now
where the time goes in v3:
time: 149 us; the launch traced here: 148 us
  starting transfers between devices  45.4 us (30%)
  waiting for transfers between devices  38.3 us (26%)
  blocking collectives  24.8 us (17%)
  Pallas kernels  17.3 us (12%)
  local copies, waits for them, and re-layouts  13.9 us (9%)
  other arithmetic  7.38 us (5%)
    all_to_all x2, blocking collectives, exchange(): return lax.all_to_all(pieces, axes, 0, 0)  24.8 us
    ppermute x12, starting transfers between devices, move(): return lax.ppermute(value, BLOCK_AXES, moves)  24.5 us
    ppermute x12, waiting for transfers between devices, move(): return lax.ppermute(value, BLOCK_AXES, moves)  21.5 us
    all_to_all x2, starting transfers between devices, exchange(): return lax.all_to_all(pieces, axes, 0, 0)  20.9 us
    all_to_all x2, waiting for transfers between devices, exchange(): return lax.all_to_all(pieces, axes, 0, 0)  16.8 us
    unnamed x34, local copies, waits for them, and re-layouts  12.5 us
    pallas_call x1, Pallas kernels, scores_and_halo(): pl.pallas_call(score_kernel, grid_spec=pltpu.PrefetchScalarGridSpec(num_s...  8.34 us
    pallas_call x2, Pallas kernels, route(): pl.pallas_call(functools.partial(route_kernel, forward), grid_spec=pltpu....  4.86 us
  transfers between devices with their start and end apart: 14, of which 8 were waited for; matrix products, arithmetic and copies ran while one was open for 3% of the time, Pallas kernels for 3%

profile of v3, /device:TPU:34, one launch (start us, length us, event | category | flops | bytes accessed | tf_op | source)
XLA Modules:
  0.0 148.0 jit_solution(2735557431876778648)
XLA Ops:
  0.7 2.6 %collective-permute-start = (bf16[128,512]{1,0:T(8,128)(2,1)}, bf16[128,512]{1,0:T(8,128)(2,1)S(1)}, u32[]{:S(2)}, u32[]{:S(2)}) collective-permute-start(bf16[128,512]{1,0:T(8,128)(2,1)} %param.8), channel_id=1, source_target_pairs={{2,0},{3,1},{6,4},{7,5},{10,8},{11,9},{14,12},{15,13},{18,16},{19,... | collective-permute-start | bytes 393224 | tf_op jit(solution)/shard_map/ppermute | solution.py:216
  3.2 3.0 %collective-permute-done = bf16[128,512]{1,0:T(8,128)(2,1)S(1)} collective-permute-done((bf16[128,512]{1,0:T(8,128)(2,1)}, bf16[128,512]{1,0:T(8,128)(2,1)S(1)}, u32[]{:S(2)}, u32[]{:S(2)}) %collective-permute-start) | collective-permute-done | bytes 131104 | tf_op jit(solution)/shard_map/ppermute | solution.py:216
  6.3 0.9 broadcast_select_fusion
  7.2 0.7 pad_maximum_fusion
  7.9 16.8 %all-to-all-start = ((bf16[8,32,512]{2,1,0:T(8,128)(2,1)}), bf16[8,32,512]{2,1,0:T(8,128)(2,1)S(1)}, u32[]{:S(2)}, u32[]{:S(2)}) async-start(bf16[8,32,512]{2,1,0:T(8,128)(2,1)} %pad_maximum_fusion), calls=%async_computation | async-start | bytes 524288 | tf_op jit(solution)/shard_map/all_to_all | solution.py:220
  24.8 1.0 pad_maximum_fusion.1.own_ref
  25.7 1.3 collective-permute-start.2
  27.0 1.9 %collective-permute-start.1 = (bf16[2,128,512]{2,1,0:T(8,128)(2,1)S(1)}, bf16[2,128,512]{2,1,0:T(8,128)(2,1)S(1)}, u32[]{:S(2)}, u32[]{:S(2)}) collective-permute-start(bf16[2,128,512]{2,1,0:T(8,128)(2,1)S(1)} %pad_maximum_fusion.1.own_ref), channel_id=1, source_target_pairs={{0,1},{1,2},{2,3},{4,5},{5,6},{6,7},{8,9},{9,10},{10,11},{12,13},{... | collective-permute-start | bytes 786440 | tf_op jit(solution)/shard_map/ppermute | solution.py:216
  29.0 0.6 pad_add_fusion.place_ref
  29.5 7.3 %collective-permute-done.2 = bf16[2,128,512]{2,1,0:T(8,128)(2,1)S(1)} collective-permute-done((bf16[2,128,512]{2,1,0:T(8,128)(2,1)S(1)}, bf16[2,128,512]{2,1,0:T(8,128)(2,1)S(1)}, u32[]{:S(2)}, u32[]{:S(2)}) %collective-permute-start.2) | collective-permute-done | bytes 262176 | tf_op jit(solution)/shard_map/ppermute | solution.py:216
  37.3 10.9 %all-to-all-done.held_ref = bf16[8,32,512]{2,1,0:T(8,128)(2,1)S(1)} async-done(((bf16[8,32,512]{2,1,0:T(8,128)(2,1)}), bf16[8,32,512]{2,1,0:T(8,128)(2,1)S(1)}, u32[]{:S(2)}, u32[]{:S(2)}) %all-to-all-start) | async-done | bytes 262176 | tf_op jit(solution)/shard_map/all_to_all | solution.py:220
  48.2 0.7 copy-done.16
  48.9 2.4 %shard_map.93 = bf16[8,32,512]{2,1,0:T(8,128)(2,1)} custom-call(s32[16]{0:T(128)} %order_ref.5, s32[4]{0:T(128)} %pad_add_fusion.place_ref, bf16[8,32,512]{2,1,0:T(8,128)(2,1)} %copy-done.16), custom_call_target="tpu_custom_call" | custom-call | bytes 524288 | tf_op jit(solution)/shard_map/pallas_call | solution.py:201
  51.4 12.8 %all_to_all.20 = bf16[8,32,512]{2,1,0:T(8,128)(2,1)S(1)} all-to-all(bf16[8,32,512]{2,1,0:T(8,128)(2,1)} %shard_map.93), channel_id=1, replica_groups=mesh['dp'=8,'z'=2,'y'=4,'b'=2,'x'=2,'core'=2] {'y','b'}, dimensions={0} | all-to-all | bytes 524288 | tf_op jit(solution)/shard_map/all_to_all | solution.py:220
  64.2 0.7 collective-permute-start.5
  64.9 0.7 collective-permute-start.4
  65.6 5.2 %collective-permute-start.3 = (bf16[128,512]{1,0:T(8,128)(2,1)S(1)}, bf16[128,512]{1,0:T(8,128)(2,1)S(1)}, u32[]{:S(2)}, u32[]{:S(2)}) collective-permute-start(bf16[128,512]{1,0:T(8,128)(2,1)S(1)} %bitcast.54), channel_id=1, source_target_pairs={{2,0},{3,1},{6,4},{7,5},{10,8},{11,9},{14,12},{15,13},{18,16},{19,... | collective-permute-start | bytes 393224 | tf_op jit(solution)/shard_map/ppermute | solution.py:216
  70.9 3.3 %collective-permute-done.3 = bf16[128,512]{1,0:T(8,128)(2,1)S(1)} collective-permute-done((bf16[128,512]{1,0:T(8,128)(2,1)S(1)}, bf16[128,512]{1,0:T(8,128)(2,1)S(1)}, u32[]{:S(2)}, u32[]{:S(2)}) %collective-permute-start.3) | collective-permute-done | bytes 131104 | tf_op jit(solution)/shard_map/ppermute | solution.py:216
  74.3 1.3 copy-done.2
  75.6 1.2 copy-done.4
  76.8 0.6 copy-done.13
  77.4 8.3 %shard_map.94 = (bf16[384,4096]{1,0:T(8,128)(2,1)S(1)}, bf16[384,4096]{1,0:T(8,128)(2,1)S(1)}, bf16[2,128,512]{2,1,0:T(8,128)(2,1)S(1)}, bf16[2,128,512]{2,1,0:T(8,128)(2,1)S(1)}) custom-call(s32[16]{0:T(128)S(1)} %copy-done.14, s32[4]{0:T(128)S(1)} %copy-done.13, s32[64,128]{1,0:T(8,128)S(1)} %bitcast.48, bf16[128,4096]{1,0:T(8,128)(2,1)S(1)} %copy-done.2, ...), custom_call_target="tpu_custom_call" | custom-call | flops 1409286144 | bytes 8388608 | tf_op jit(solution)/shard_map/pallas_call | solution.py:139
  85.8 1.6 %copy-done = bf16[384,4096]{1,0:T(8,128)(2,1)} copy-done((bf16[384,4096]{1,0:T(8,128)(2,1)}, bf16[384,4096]{1,0:T(8,128)(2,1)S(1)}, u32[]{:S(2)}) %copy-start) | copy-done | bytes 3145752
  87.4 0.7 slice_bitcast_fusion.6
  88.1 1.3 collective-permute-start.6
  89.4 0.7 slice_bitcast_fusion.4
  90.1 1.3 collective-permute-start.8
  91.4 1.3 collective-permute-start.7
  92.7 2.8 %collective-permute-done.6 = bf16[128,512]{1,0:T(8,128)(2,1)} collective-permute-done((bf16[128,512]{1,0:T(8,128)(2,1)}, bf16[128,512]{1,0:T(8,128)(2,1)}, u32[]{:S(2)}, u32[]{:S(2)}) %collective-permute-start.6) | collective-permute-done | bytes 131104 | tf_op jit(solution)/shard_map/ppermute | solution.py:216
  95.6 1.1 add_convert_fusion
  96.7 12.0 %all_to_all.21.held_ref = bf16[8,32,512]{2,1,0:T(8,128)(2,1)} all-to-all(bf16[8,32,512]{2,1,0:T(8,128)(2,1)S(1)} %bitcast.50), channel_id=1, replica_groups=mesh['dp'=8,'z'=2,'y'=4,'b'=2,'x'=2,'core'=2] {'y','b'}, dimensions={0} | all-to-all | bytes 524288 | tf_op jit(solution)/shard_map/all_to_all | solution.py:220
  108.6 2.4 %shard_map.96 = bf16[8,32,512]{2,1,0:T(8,128)(2,1)} custom-call(s32[16]{0:T(128)} %order_ref.5, s32[4]{0:T(128)} %pad_add_fusion.place_ref, bf16[8,32,512]{2,1,0:T(8,128)(2,1)} %all_to_all.21.held_ref), custom_call_target="tpu_custom_call" | custom-call | bytes 524288 | tf_op jit(solution)/shard_map/pallas_call | solution.py:201
  111.1 4.0 %all-to-all-start.3 = ((bf16[8,32,512]{2,1,0:T(8,128)(2,1)}), bf16[8,32,512]{2,1,0:T(8,128)(2,1)}, u32[]{:S(2)}, u32[]{:S(2)}) async-start(bf16[8,32,512]{2,1,0:T(8,128)(2,1)} %shard_map.96), calls=%async_computation.3 | async-start | bytes 524288 | tf_op jit(solution)/shard_map/all_to_all | solution.py:220
  115.1 4.0 %collective-permute-start.9 = (bf16[2,128,512]{2,1,0:T(8,128)(2,1)}, bf16[2,128,512]{2,1,0:T(8,128)(2,1)}, u32[]{:S(2)}, u32[]{:S(2)}) collective-permute-start(bf16[2,128,512]{2,1,0:T(8,128)(2,1)} %copy-done.11), channel_id=1, source_target_pairs={{1,0},{2,1},{3,2},{5,4},{6,5},{7,6},{9,8},{10,9},{11,10},{13,12},{... | collective-permute-start | bytes 786440 | tf_op jit(solution)/shard_map/ppermute | solution.py:216
  119.2 2.9 %collective-permute-start.10 = (bf16[2,128,512]{2,1,0:T(8,128)(2,1)}, bf16[2,128,512]{2,1,0:T(8,128)(2,1)}, u32[]{:S(2)}, u32[]{:S(2)}) collective-permute-start(bf16[2,128,512]{2,1,0:T(8,128)(2,1)} %copy-done.12), channel_id=1, source_target_pairs={{2,0},{3,1},{6,4},{7,5},{10,8},{11,9},{14,12},{15,13},{18,16},{19,... | collective-permute-start | bytes 786440 | tf_op jit(solution)/shard_map/ppermute | solution.py:216
  122.1 1.9 %copy-done.1 = bf16[384,4096]{1,0:T(8,128)(2,1)S(1)} copy-done((bf16[384,4096]{1,0:T(8,128)(2,1)S(1)}, bf16[384,4096]{1,0:T(8,128)(2,1)}, u32[]{:S(2)}) %copy-start.1) | copy-done | bytes 3145752
  124.0 1.2 copy-done.3
  125.2 1.2 copy-done.5
  126.4 0.9 copy-done.7
  127.4 0.9 copy-done.9
  128.3 4.1 %shard_map.95 = (bf16[128,4096]{1,0:T(8,128)(2,1)}, bf16[128,4096]{1,0:T(8,128)(2,1)}, f32[2,128,512]{2,1,0:T(8,128)S(1)}) custom-call(bf16[128,4096]{1,0:T(8,128)(2,1)S(1)} %copy-done.3, bf16[128,4096]{1,0:T(8,128)(2,1)S(1)} %copy-done.5, bf16[2,128,512]{2,1,0:T(8,128)(2,1)S(1)} %copy-done.9, bf16[2,128,512]{2,1,0:T(8,128)(2,1)S(1)} %copy-done.7, ...), custom_call_target="tpu_custom_call" | custom-call | flops 1006632960 | bytes 10485760 | tf_op jit(solution)/shard_map/pallas_call | solution.py:162
  132.5 0.8 copy-done.10
  133.3 5.9 %all-to-all-done.3 = bf16[8,32,512]{2,1,0:T(8,128)(2,1)} async-done(((bf16[8,32,512]{2,1,0:T(8,128)(2,1)}), bf16[8,32,512]{2,1,0:T(8,128)(2,1)}, u32[]{:S(2)}, u32[]{:S(2)}) %all-to-all-start.3) | async-done | bytes 262176 | tf_op jit(solution)/shard_map/all_to_all | solution.py:220
  139.1 1.0 slice_add_fusion
  140.1 1.3 collective-permute-start.11
  141.4 1.3 convert_add_fusion
  142.7 4.5 %collective-permute-done.11 = bf16[128,512]{1,0:T(8,128)(2,1)S(1)} collective-permute-done((bf16[128,512]{1,0:T(8,128)(2,1)S(1)}, bf16[128,512]{1,0:T(8,128)(2,1)S(1)}, u32[]{:S(2)}, u32[]{:S(2)}) %collective-permute-start.11) | collective-permute-done | bytes 131104 | tf_op jit(solution)/shard_map/ppermute | solution.py:216
  147.2 0.8 fusion.1
  (34 shorter events, 0.6 us)
Async XLA Ops:
  0.6 73.6 %copy-start.14 = (s32[16]{0:T(128)S(1)}, s32[16]{0:T(128)}, u32[]{:S(2)}) copy-start(s32[16]{0:T(128)} %order_ref.5) | copy-start | bytes 196
  0.6 73.6 %copy-start.15 = (s32[8192]{0:T(1024)S(1)}, s32[8192]{0:T(1024)}, u32[]{:S(2)}) copy-start(s32[8192]{0:T(1024)} %param.10) | copy-start | bytes 98308
  0.7 5.6 %collective-permute-start = (bf16[128,512]{1,0:T(8,128)(2,1)}, bf16[128,512]{1,0:T(8,128)(2,1)S(1)}, u32[]{:S(2)}, u32[]{:S(2)}) collective-permute-start(bf16[128,512]{1,0:T(8,128)(2,1)} %param.8), channel_id=1, source_target_pairs={{2,0},{3,1},{6,4},{7,5},{10,8},{11,9},{14,12},{15,13},{18,16},{19,... | collective-permute-start | bytes 393224 | tf_op jit(solution)/shard_map/ppermute | solution.py:216
  7.9 40.3 %all-to-all-start = ((bf16[8,32,512]{2,1,0:T(8,128)(2,1)}), bf16[8,32,512]{2,1,0:T(8,128)(2,1)S(1)}, u32[]{:S(2)}, u32[]{:S(2)}) async-start(bf16[8,32,512]{2,1,0:T(8,128)(2,1)} %pad_maximum_fusion), calls=%async_computation | async-start | bytes 524288 | tf_op jit(solution)/shard_map/all_to_all | solution.py:220
  25.7 11.1 %collective-permute-start.2 = (bf16[2,128,512]{2,1,0:T(8,128)(2,1)S(1)}, bf16[2,128,512]{2,1,0:T(8,128)(2,1)S(1)}, u32[]{:S(2)}, u32[]{:S(2)}) collective-permute-start(bf16[2,128,512]{2,1,0:T(8,128)(2,1)S(1)} %pad_maximum_fusion.1.own_ref), channel_id=1, source_target_pairs={{0,2},{1,3},{4,6},{5,7},{8,10},{9,11},{12,14},{13,15},{16,18},{17,... | collective-permute-start | bytes 786440 | tf_op jit(solution)/shard_map/ppermute | solution.py:216
  27.0 10.3 %collective-permute-start.1 = (bf16[2,128,512]{2,1,0:T(8,128)(2,1)S(1)}, bf16[2,128,512]{2,1,0:T(8,128)(2,1)S(1)}, u32[]{:S(2)}, u32[]{:S(2)}) collective-permute-start(bf16[2,128,512]{2,1,0:T(8,128)(2,1)S(1)} %pad_maximum_fusion.1.own_ref), channel_id=1, source_target_pairs={{0,1},{1,2},{2,3},{4,5},{5,6},{6,7},{8,9},{9,10},{10,11},{12,13},{... | collective-permute-start | bytes 786440 | tf_op jit(solution)/shard_map/ppermute | solution.py:216
  48.2 0.7 copy-start.16
  64.2 6.6 %collective-permute-start.5 = (bf16[128,512]{1,0:T(8,128)(2,1)S(1)}, bf16[128,512]{1,0:T(8,128)(2,1)S(1)}, u32[]{:S(2)}, u32[]{:S(2)}) collective-permute-start(bf16[128,512]{1,0:T(8,128)(2,1)S(1)} %bitcast.52), channel_id=1, source_target_pairs={{1,0},{5,4},{9,8},{13,12},{17,16},{21,20},{25,24},{29,28},{33,32},... | collective-permute-start | bytes 393224 | tf_op jit(solution)/shard_map/ppermute | solution.py:216
  64.9 5.9 %collective-permute-start.4 = (bf16[128,512]{1,0:T(8,128)(2,1)S(1)}, bf16[128,512]{1,0:T(8,128)(2,1)S(1)}, u32[]{:S(2)}, u32[]{:S(2)}) collective-permute-start(bf16[128,512]{1,0:T(8,128)(2,1)S(1)} %bitcast.53), channel_id=1, source_target_pairs={{3,0},{7,4},{11,8},{15,12},{19,16},{23,20},{27,24},{31,28},{35,32}... | collective-permute-start | bytes 393224 | tf_op jit(solution)/shard_map/ppermute | solution.py:216
  65.6 8.6 %collective-permute-start.3 = (bf16[128,512]{1,0:T(8,128)(2,1)S(1)}, bf16[128,512]{1,0:T(8,128)(2,1)S(1)}, u32[]{:S(2)}, u32[]{:S(2)}) collective-permute-start(bf16[128,512]{1,0:T(8,128)(2,1)S(1)} %bitcast.54), channel_id=1, source_target_pairs={{2,0},{3,1},{6,4},{7,5},{10,8},{11,9},{14,12},{15,13},{18,16},{19,... | collective-permute-start | bytes 393224 | tf_op jit(solution)/shard_map/ppermute | solution.py:216
  70.9 19.2 %copy-start.6 = (bf16[2,128,512]{2,1,0:T(8,128)(2,1)}, bf16[2,128,512]{2,1,0:T(8,128)(2,1)S(1)}, u32[]{:S(2)}) copy-start(bf16[2,128,512]{2,1,0:T(8,128)(2,1)S(1)} %maximum_select_fusion.1.near_ref) | copy-start | bytes 786436
  74.3 15.9 %copy-start.8 = (bf16[2,128,512]{2,1,0:T(8,128)(2,1)}, bf16[2,128,512]{2,1,0:T(8,128)(2,1)S(1)}, u32[]{:S(2)}) copy-start(bf16[2,128,512]{2,1,0:T(8,128)(2,1)S(1)} %maximum_select_fusion.far_ref) | copy-start | bytes 786436
  74.3 1.3 copy-start.2
  75.6 1.2 copy-start.4
  76.8 0.6 copy-start.13
  85.7 1.6 %copy-start = (bf16[384,4096]{1,0:T(8,128)(2,1)}, bf16[384,4096]{1,0:T(8,128)(2,1)S(1)}, u32[]{:S(2)}) copy-start(bf16[384,4096]{1,0:T(8,128)(2,1)S(1)} %get-tuple-element.25.dscore_ref) | copy-start | bytes 9437188
  87.4 4.1 %copy-start.11 = (bf16[2,128,512]{2,1,0:T(8,128)(2,1)}, bf16[2,128,512]{2,1,0:T(8,128)(2,1)S(1)}, u32[]{:S(2)}) copy-start(bf16[2,128,512]{2,1,0:T(8,128)(2,1)S(1)} %get-tuple-element.21) | copy-start | bytes 786436
  87.4 4.1 %copy-start.12 = (bf16[2,128,512]{2,1,0:T(8,128)(2,1)}, bf16[2,128,512]{2,1,0:T(8,128)(2,1)S(1)}, u32[]{:S(2)}) copy-start(bf16[2,128,512]{2,1,0:T(8,128)(2,1)S(1)} %get-tuple-element.20) | copy-start | bytes 786436
  88.1 7.5 %collective-permute-start.6 = (bf16[128,512]{1,0:T(8,128)(2,1)}, bf16[128,512]{1,0:T(8,128)(2,1)}, u32[]{:S(2)}, u32[]{:S(2)}) collective-permute-start(bf16[128,512]{1,0:T(8,128)(2,1)} %slice_bitcast_fusion.6), channel_id=1, source_target_pairs={{0,2},{1,3},{4,6},{5,7},{8,10},{9,11},{12,14},{13,15},{16,18},{17,... | collective-permute-start | bytes 393224 | tf_op jit(solution)/shard_map/ppermute | solution.py:216
  90.1 5.5 %collective-permute-start.8 = (bf16[128,512]{1,0:T(8,128)(2,1)}, bf16[128,512]{1,0:T(8,128)(2,1)}, u32[]{:S(2)}, u32[]{:S(2)}) collective-permute-start(bf16[128,512]{1,0:T(8,128)(2,1)} %get-tuple-element.32), channel_id=1, source_target_pairs={{0,3},{4,7},{8,11},{12,15},{16,19},{20,23},{24,27},{28,31},{32,35}... | collective-permute-start | bytes 393224 | tf_op jit(solution)/shard_map/ppermute | solution.py:216
  91.4 4.1 %collective-permute-start.7 = (bf16[128,512]{1,0:T(8,128)(2,1)}, bf16[128,512]{1,0:T(8,128)(2,1)}, u32[]{:S(2)}, u32[]{:S(2)}) collective-permute-start(bf16[128,512]{1,0:T(8,128)(2,1)} %get-tuple-element.33), channel_id=1, source_target_pairs={{0,1},{4,5},{8,9},{12,13},{16,17},{20,21},{24,25},{28,29},{32,33},... | collective-permute-start | bytes 393224 | tf_op jit(solution)/shard_map/ppermute | solution.py:216
  111.1 28.0 %all-to-all-start.3 = ((bf16[8,32,512]{2,1,0:T(8,128)(2,1)}), bf16[8,32,512]{2,1,0:T(8,128)(2,1)}, u32[]{:S(2)}, u32[]{:S(2)}) async-start(bf16[8,32,512]{2,1,0:T(8,128)(2,1)} %shard_map.96), calls=%async_computation.3 | async-start | bytes 524288 | tf_op jit(solution)/shard_map/all_to_all | solution.py:220
  115.1 26.3 %collective-permute-start.9 = (bf16[2,128,512]{2,1,0:T(8,128)(2,1)}, bf16[2,128,512]{2,1,0:T(8,128)(2,1)}, u32[]{:S(2)}, u32[]{:S(2)}) collective-permute-start(bf16[2,128,512]{2,1,0:T(8,128)(2,1)} %copy-done.11), channel_id=1, source_target_pairs={{1,0},{2,1},{3,2},{5,4},{6,5},{7,6},{9,8},{10,9},{11,10},{13,12},{... | collective-permute-start | bytes 786440 | tf_op jit(solution)/shard_map/ppermute | solution.py:216
  119.2 22.3 %collective-permute-start.10 = (bf16[2,128,512]{2,1,0:T(8,128)(2,1)}, bf16[2,128,512]{2,1,0:T(8,128)(2,1)}, u32[]{:S(2)}, u32[]{:S(2)}) collective-permute-start(bf16[2,128,512]{2,1,0:T(8,128)(2,1)} %copy-done.12), channel_id=1, source_target_pairs={{2,0},{3,1},{6,4},{7,5},{10,8},{11,9},{14,12},{15,13},{18,16},{19,... | collective-permute-start | bytes 786440 | tf_op jit(solution)/shard_map/ppermute | solution.py:216
  122.1 1.9 %copy-start.1 = (bf16[384,4096]{1,0:T(8,128)(2,1)S(1)}, bf16[384,4096]{1,0:T(8,128)(2,1)}, u32[]{:S(2)}) copy-start(bf16[384,4096]{1,0:T(8,128)(2,1)} %copy-done) | copy-start | bytes 9437188
  124.0 1.2 copy-start.3
  125.2 1.2 copy-start.5
  126.4 0.9 copy-start.7
  127.4 0.9 copy-start.9
  132.5 0.8 copy-start.10
  140.1 7.1 %collective-permute-start.11 = (bf16[128,512]{1,0:T(8,128)(2,1)S(1)}, bf16[128,512]{1,0:T(8,128)(2,1)S(1)}, u32[]{:S(2)}, u32[]{:S(2)}) collective-permute-start(bf16[128,512]{1,0:T(8,128)(2,1)S(1)} %bitcast.58), channel_id=1, source_target_pairs={{0,2},{1,3},{4,6},{5,7},{8,10},{9,11},{12,14},{13,15},{16,18},{17,... | collective-permute-start | bytes 393224 | tf_op jit(solution)/shard_map/ppermute | solution.py:216

commit v4 on v3

--- a/solution.py
+++ b/solution.py
@@ -17,7 +17,7 @@
 KV_WIDTH = KEY_VALUE_HEADS * HEAD_SIZE
 BLOCK_AXES = ("x", "core")
 SEQ_AXES = ("z", "y")
-PLANE_AXES = ("y", "b")
+PLANE_AXES = ("y", "b", "x")
 
 
 def usable_bias(chunk, segments_ref, bias_ref):
@@ -71,8 +71,8 @@
         usable_bias(order_ref[place_ref[2]] * 4 + place_ref[3], segments_ref, bias_ref)
 
     scale = 1.0 / math.sqrt(HEAD_SIZE)
-    keys = jnp.concatenate([far_ref[0], near_ref[0], own_ref[0]], axis=0)
-    values = jnp.concatenate([far_ref[1], near_ref[1], own_ref[1]], axis=0)
+    values = jnp.concatenate([far_ref[0], near_ref[0], own_ref[0]], axis=0)
+    keys = jnp.concatenate([far_ref[1], near_ref[1], own_ref[1]], axis=0)
     width = 2 * CHUNK
     for pair in range(GROUP // 2):
         heads = (2 * pair, 2 * pair + 1)
@@ -89,7 +89,7 @@
     halo = pl.ds(0, 2 * CHUNK)
     grad_keys = dot(dscore_ref[halo, :], stacked(query_ref, every), PLAIN).astype(jnp.bfloat16)
     grad_values = dot(weight_ref[halo, :], stacked(grad_ref, every), PLAIN).astype(jnp.bfloat16)
-    for i, total in enumerate((grad_keys, grad_values)):
+    for i, total in enumerate((grad_values, grad_keys)):
         far_grad_ref[i] = total[:CHUNK]
         near_grad_ref[i] = total[CHUNK:]
 
@@ -106,8 +106,8 @@
     grad_query_ref,
     own_grad_ref,
 ):
-    keys_t = jnp.concatenate([far_ref[0], near_ref[0], own_ref[0]], axis=0).T
-    values_t = jnp.concatenate([far_ref[1], near_ref[1], own_ref[1]], axis=0).T
+    values_t = jnp.concatenate([far_ref[0], near_ref[0], own_ref[0]], axis=0).T
+    keys_t = jnp.concatenate([far_ref[1], near_ref[1], own_ref[1]], axis=0).T
     width = 2 * CHUNK
     for pair in range(GROUP // 2):
         columns = pl.ds(pair * width, width)
@@ -120,8 +120,8 @@
             grad_query_ref[:, columns] = grad_query_t[:, part].T
     every = range(GROUP)
     own = pl.ds(2 * CHUNK, CHUNK)
-    own_grad_ref[0] = dot(dscore_ref[own, :], stacked(query_ref, every), PLAIN)
-    own_grad_ref[1] = dot(weight_ref[own, :], stacked(grad_ref, every), PLAIN)
+    own_grad_ref[0] = dot(weight_ref[own, :], stacked(grad_ref, every), PLAIN)
+    own_grad_ref[1] = dot(dscore_ref[own, :], stacked(query_ref, every), PLAIN)
 
 
 def attention_specs(rows):
@@ -146,7 +146,7 @@
             scratch_shapes=[pltpu.VMEM((WINDOW, 2 * CHUNK), jnp.float32)],
         ),
         out_shape=[held, held, half, half],
-        compiler_params=pltpu.CompilerParams(vmem_limit_bytes=32 * 1024 * 1024),
+        compiler_params=pltpu.CompilerParams(vmem_limit_bytes=58 * 1024 * 1024),
         cost_estimate=pl.CostEstimate(
             flops=7 * rows * QUERY_HEADS * WINDOW * HEAD_SIZE,
             bytes_accessed=16 * rows * QUERY_HEADS * HEAD_SIZE,
@@ -165,7 +165,7 @@
         in_specs=[wide, wide, pair, pair, pair, window, window],
         out_specs=[wide, wide, pair],
         out_shape=[like, like, jax.ShapeDtypeStruct((2, rows, KV_WIDTH), jnp.float32)],
-        compiler_params=pltpu.CompilerParams(vmem_limit_bytes=32 * 1024 * 1024),
+        compiler_params=pltpu.CompilerParams(vmem_limit_bytes=58 * 1024 * 1024),
         cost_estimate=pl.CostEstimate(
             flops=5 * rows * QUERY_HEADS * WINDOW * HEAD_SIZE,
             bytes_accessed=20 * rows * QUERY_HEADS * HEAD_SIZE,
@@ -179,35 +179,38 @@
     for j in range(count):
         slot_ref[order_ref[j]] = j
     z, block = place_ref[0], place_ref[1]
+    empty = jnp.zeros(out_ref.shape[1:], out_ref.dtype)
     for i in range(8):
         if forward:
             other = slot_ref[lax.rem(order_ref[8 * z + i] + count - 1, count)]
-            index, mine = lax.div(other, 2), lax.rem(other, 2) == block
+            index, mine, to = lax.div(other, 2), lax.rem(other, 2) == block, 2 * i
+            out_ref[to + 1] = empty
         else:
             other = slot_ref[lax.rem(order_ref[2 * i + block] + 1, count)]
-            index, mine = lax.rem(other, 8), lax.div(other, 8) == z
+            index, mine, to = 2 * lax.rem(other, 8), lax.div(other, 8) == z, i
 
         @pl.when(mine)
-        def _(i=i, index=index):
-            out_ref[i] = held_ref[index]
+        def _(to=to, index=index):
+            out_ref[to] = held_ref[index]
 
         @pl.when(jnp.logical_not(mine))
-        def _(i=i):
-            out_ref[i] = jnp.zeros(out_ref.shape[1:], out_ref.dtype)
+        def _(to=to):
+            out_ref[to] = empty
 
 
 def route(order, place, held, forward):
-    whole = pl.BlockSpec(held.shape, lambda i, *_: (0, 0, 0))
+    pieces = 16 if forward else 8
+    whole = lambda n: pl.BlockSpec((n, *held.shape[1:]), lambda i, *_: (0, 0, 0))
     return pl.pallas_call(
         functools.partial(route_kernel, forward),
         grid_spec=pltpu.PrefetchScalarGridSpec(
             num_scalar_prefetch=2,
             grid=(1,),
-            in_specs=[whole],
-            out_specs=whole,
+            in_specs=[whole(held.shape[0])],
+            out_specs=whole(pieces),
             scratch_shapes=[pltpu.SMEM((order.shape[0],), jnp.int32)],
         ),
-        out_shape=jax.ShapeDtypeStruct(held.shape, held.dtype),
+        out_shape=jax.ShapeDtypeStruct((pieces, *held.shape[1:]), held.dtype),
         cost_estimate=pl.CostEstimate(flops=0, bytes_accessed=4 * held.size, transcendentals=0),
     )(order, place, held)
 
@@ -229,31 +232,26 @@
     whole = (CHUNK, KV_WIDTH)
 
     moved = move(values, [(2, 0), (3, 1)])
-    own = jnp.stack([keys, values], axis=0)
+    own = jnp.stack([values, keys], axis=0)
     near_in = move(own, [(0, 1), (1, 2), (2, 3)])
     far_in = move(own, [(0, 2), (1, 3)])
     quarter = jnp.where(c >= 2, keys, moved).reshape(part)
     held = exchange(jnp.concatenate([quarter, quarter], axis=0), SEQ_AXES)
     held, near_in, far_in = lax.optimization_barrier((held, near_in, far_in))
-    arrived = exchange(route(order, place, held, True), PLANE_AXES).reshape(4, 2, *part[1:])
-    quarter = (arrived[:, 0] + arrived[:, 1]).reshape(whole)
-    straight = move(quarter, [(2, 0), (3, 1)])
-    to_first = move(quarter, [(1, 0)])
-    across = move(quarter, [(3, 0)])
-    far = jnp.where(c < 2, jnp.stack([straight, quarter], axis=0), far_in)
-    near = jnp.where(c == 0, jnp.stack([across, to_first], axis=0), near_in)
+    arrived = exchange(route(order, place, held, True), PLANE_AXES).reshape(4, 2, 2, *part[1:])
+    arrived = (arrived[:, 0] + arrived[:, 1]).transpose(1, 0, 2, 3).reshape(2, *whole)
+    before = move(arrived, [(1, 0)])
+    far = jnp.where(c < 2, arrived, far_in)
+    near = jnp.where(c == 0, before, near_in)
 
     weights, dscores, far_grad, near_grad = scores_and_halo(
         order, place, segment_ids.reshape(-1, CHUNK), queries, grads, far, near, own
     )
 
-    straight = move(far_grad[0], [(0, 2), (1, 3)])
-    to_second = move(near_grad[1], [(0, 1)])
-    across = move(near_grad[0], [(0, 3)])
-    quarter = jnp.where(c < 2, far_grad[1], straight).astype(jnp.float32)
-    quarter = quarter + jnp.where(c == 1, to_second, jnp.where(c == 3, across, 0)).astype(jnp.float32)
-    quarter = quarter.astype(jnp.bfloat16).reshape(part)
-    pieces = jnp.repeat(quarter, 2, axis=0)
+    before = move(near_grad, [(0, 1)])
+    halo = (far_grad.astype(jnp.float32) + before.astype(jnp.float32)).astype(jnp.bfloat16)
+    pieces = halo.reshape(2, *part).transpose(1, 0, 2, 3)
+    pieces = jnp.broadcast_to(pieces[:, None], (4, 2, 2, *part[1:])).reshape(16, *part[1:])
     pieces, weights, dscores = lax.optimization_barrier((pieces, weights, dscores))
     held = exchange(pieces, PLANE_AXES)
     attended, grad_query, own_grad = outputs_and_own(queries, grads, far, near, own, weights, dscores)
@@ -264,8 +262,8 @@
     moved = move(quarter, [(0, 2), (1, 3)])
 
     total = own_grad + near_back.astype(jnp.float32) + far_back.astype(jnp.float32)
-    key_gradient = total[0] + jnp.where(c >= 2, quarter, 0).astype(jnp.float32)
-    value_gradient = total[1] + moved.astype(jnp.float32)
+    key_gradient = total[1] + jnp.where(c >= 2, quarter, 0).astype(jnp.float32)
+    value_gradient = total[0] + moved.astype(jnp.float32)
     return (
         attended,
         grad_query,

time: 149 us -> 139 us (0.933)
  local copies, waits for them, and re-layouts: 13.9 us -> 0.82 us
  starting transfers between devices: 45.4 us -> 34 us
  blocking collectives: 24.8 us -> 35.9 us
  Pallas kernels: 17.3 us -> 21.5 us
    unnamed x34 -> x8, local copies, waits for them, and re-layouts: 12.5 us -> 0.72 us
    all_to_all x2, blocking collectives: 24.8 us -> 35.9 us  [exchange(): return lax.all_to_all(pieces, axes, 0, 0)]
    ppermute x12 -> x8, starting transfers between devices: 24.5 us -> 13.7 us  [move(): return lax.ppermute(value, BLOCK_AXES, moves)]
    ppermute x12 -> x8, waiting for transfers between devices: 21.5 us -> 15.4 us  [move(): return lax.ppermute(value, BLOCK_AXES, moves)]
    all_to_all x2, waiting for transfers between devices: 16.8 us -> 22.2 us  [exchange(): return lax.all_to_all(pieces, axes, 0, 0)]
    pallas_call x1, Pallas kernels: 4.12 us -> 6.64 us  [outputs_and_own(): pl.pallas_call(output_kernel, grid=(KEY_VALUE_HEADS,), in_specs=[wide, wi...]
  transfers between devices with their start and end apart: 14 -> 10, of which waited for: 8 -> 6; matrix products, arithmetic and copies ran while one was open for 3% -> 3% of each run, Pallas kernels for 3% -> 5%
where the time goes in v4:
time: 139 us; the launch traced here: 138 us
  waiting for transfers between devices  37.5 us (27%)
  blocking collectives  35.9 us (26%)
  starting transfers between devices  34 us (24%)
  Pallas kernels  21.5 us (15%)
  other arithmetic  7.67 us (6%)
    all_to_all x2, blocking collectives, exchange(): return lax.all_to_all(pieces, axes, 0, 0)  35.9 us
    all_to_all x2, waiting for transfers between devices, exchange(): return lax.all_to_all(pieces, axes, 0, 0)  22.2 us
    all_to_all x2, starting transfers between devices, exchange(): return lax.all_to_all(pieces, axes, 0, 0)  20.2 us
    ppermute x8, waiting for transfers between devices, move(): return lax.ppermute(value, BLOCK_AXES, moves)  15.4 us
    ppermute x8, starting transfers between devices, move(): return lax.ppermute(value, BLOCK_AXES, moves)  13.7 us
    pallas_call x1, Pallas kernels, scores_and_halo(): pl.pallas_call(score_kernel, grid_spec=pltpu.PrefetchScalarGridSpec(num_s...  9.77 us
    pallas_call x1, Pallas kernels, outputs_and_own(): pl.pallas_call(output_kernel, grid=(KEY_VALUE_HEADS,), in_specs=[wide, wi...  6.64 us
    pallas_call x2, Pallas kernels, route(): pl.pallas_call(functools.partial(route_kernel, forward), grid_spec=pltpu....  5.07 us
  transfers between devices with their start and end apart: 10, of which 6 were waited for; matrix products, arithmetic and copies ran while one was open for 3% of the time, Pallas kernels for 5%

profile of v4, /device:TPU:34, one launch (start us, length us, event | category | flops | bytes accessed | tf_op | source)
XLA Modules:
  0.0 138.2 jit_solution(5742317749813743686)
XLA Ops:
  0.6 2.4 %collective-permute-start = (bf16[128,512]{1,0:T(8,128)(2,1)}, bf16[128,512]{1,0:T(8,128)(2,1)S(1)}, u32[]{:S(2)}, u32[]{:S(2)}) collective-permute-start(bf16[128,512]{1,0:T(8,128)(2,1)} %param.8), channel_id=1, source_target_pairs={{2,0},{3,1},{6,4},{7,5},{10,8},{11,9},{14,12},{15,13},{18,16},{19,... | collective-permute-start | bytes 393224 | tf_op jit(solution)/shard_map/ppermute | solution.py:219
  3.1 3.0 %collective-permute-done = bf16[128,512]{1,0:T(8,128)(2,1)S(1)} collective-permute-done((bf16[128,512]{1,0:T(8,128)(2,1)}, bf16[128,512]{1,0:T(8,128)(2,1)S(1)}, u32[]{:S(2)}, u32[]{:S(2)}) %collective-permute-start) | collective-permute-done | bytes 131104 | tf_op jit(solution)/shard_map/ppermute | solution.py:219
  6.1 0.9 broadcast_select_fusion.2
  7.1 0.7 pad_maximum_fusion
  7.8 16.8 %all-to-all-start = ((bf16[8,32,512]{2,1,0:T(8,128)(2,1)}), bf16[8,32,512]{2,1,0:T(8,128)(2,1)S(1)}, u32[]{:S(2)}, u32[]{:S(2)}) async-start(bf16[8,32,512]{2,1,0:T(8,128)(2,1)} %pad_maximum_fusion), calls=%async_computation | async-start | bytes 524288 | tf_op jit(solution)/shard_map/all_to_all | solution.py:223
  24.6 1.0 pad_maximum_fusion.1.own_ref
  25.6 0.0 copy-start
  25.6 1.3 collective-permute-start.2
  26.9 1.9 %collective-permute-start.1 = (bf16[2,128,512]{2,1,0:T(8,128)(2,1)S(1)}, bf16[2,128,512]{2,1,0:T(8,128)(2,1)S(1)}, u32[]{:S(2)}, u32[]{:S(2)}) collective-permute-start(bf16[2,128,512]{2,1,0:T(8,128)(2,1)S(1)} %pad_maximum_fusion.1.own_ref), channel_id=1, source_target_pairs={{0,1},{1,2},{2,3},{4,5},{5,6},{6,7},{8,9},{9,10},{10,11},{12,13},{... | collective-permute-start | bytes 786440 | tf_op jit(solution)/shard_map/ppermute | solution.py:219
  28.8 0.6 pad_add_fusion.place_ref
  29.4 7.3 %collective-permute-done.2 = bf16[2,128,512]{2,1,0:T(8,128)(2,1)S(1)} collective-permute-done((bf16[2,128,512]{2,1,0:T(8,128)(2,1)S(1)}, bf16[2,128,512]{2,1,0:T(8,128)(2,1)S(1)}, u32[]{:S(2)}, u32[]{:S(2)}) %collective-permute-start.2) | collective-permute-done | bytes 262176 | tf_op jit(solution)/shard_map/ppermute | solution.py:219
  36.7 0.5 collective-permute-done.1
  37.2 10.9 %all-to-all-done.held_ref = bf16[8,32,512]{2,1,0:T(8,128)(2,1)S(1)} async-done(((bf16[8,32,512]{2,1,0:T(8,128)(2,1)}), bf16[8,32,512]{2,1,0:T(8,128)(2,1)S(1)}, u32[]{:S(2)}, u32[]{:S(2)}) %all-to-all-start) | async-done | bytes 262176 | tf_op jit(solution)/shard_map/all_to_all | solution.py:223
  48.1 0.0 copy-start.1
  48.1 0.7 copy-done.1
  48.8 2.6 %shard_map.93 = bf16[16,32,512]{2,1,0:T(8,128)(2,1)} custom-call(s32[16]{0:T(128)} %order_ref.5, s32[4]{0:T(128)} %pad_add_fusion.place_ref, bf16[8,32,512]{2,1,0:T(8,128)(2,1)} %copy-done.1), custom_call_target="tpu_custom_call" | custom-call | bytes 524288 | tf_op jit(solution)/shard_map/pallas_call | solution.py:204
  51.3 15.6 %all_to_all.20 = bf16[16,32,512]{2,1,0:T(8,128)(2,1)S(1)} all-to-all(bf16[16,32,512]{2,1,0:T(8,128)(2,1)} %shard_map.93), channel_id=1, replica_groups=mesh['dp'=8,'z'=2,'y'=4,'b'=2,'x'=2,'core'=2] {'y','b','x'}, dimensions={0} | all-to-all | bytes 1048576 | tf_op jit(solution)/shard_map/all_to_all | solution.py:223
  67.0 0.7 collective-permute-start.3
  67.7 0.7 broadcast_select_fusion.1.far_ref
  68.4 0.0 collective-permute-done.3
  68.4 0.7 broadcast_select_fusion.near_ref
  69.1 0.0 copy-done
  69.1 9.8 %shard_map.94 = (bf16[384,4096]{1,0:T(8,128)(2,1)}, bf16[384,4096]{1,0:T(8,128)(2,1)}, bf16[2,128,512]{2,1,0:T(8,128)(2,1)}, bf16[2,128,512]{2,1,0:T(8,128)(2,1)}) custom-call(s32[16]{0:T(128)} %order_ref.5, s32[4]{0:T(128)} %pad_add_fusion.place_ref, s32[64,128]{1,0:T(8,128)} %bitcast.41, bf16[128,4096]{1,0:T(8,128)(2,1)} %query_ref.3, ...), custom_call_target="tpu_custom_call" | custom-call | flops 1409286144 | bytes 8388608 | tf_op jit(solution)/shard_map/pallas_call | solution.py:139
  78.9 0.0 copy-start.2
  78.9 0.0 copy-start.3
  78.9 0.8 collective-permute-start.4
  79.7 0.0 collective-permute-done.4
  79.7 1.0 add_convert_fusion
  80.8 20.3 %all_to_all.21.held_ref = bf16[16,32,512]{2,1,0:T(8,128)(2,1)} all-to-all(bf16[16,32,512]{2,1,0:T(8,128)(2,1)S(1)} %bitcast.33), channel_id=1, replica_groups=mesh['dp'=8,'z'=2,'y'=4,'b'=2,'x'=2,'core'=2] {'y','b','x'}, dimensions={0} | all-to-all | bytes 1048576 | tf_op jit(solution)/shard_map/all_to_all | solution.py:223
  101.2 2.5 %shard_map.96 = bf16[8,32,512]{2,1,0:T(8,128)(2,1)} custom-call(s32[16]{0:T(128)} %order_ref.5, s32[4]{0:T(128)} %pad_add_fusion.place_ref, bf16[16,32,512]{2,1,0:T(8,128)(2,1)} %all_to_all.21.held_ref), custom_call_target="tpu_custom_call" | custom-call | bytes 1048576 | tf_op jit(solution)/shard_map/pallas_call | solution.py:204
  103.7 3.4 %all-to-all-start.3 = ((bf16[8,32,512]{2,1,0:T(8,128)(2,1)}), bf16[8,32,512]{2,1,0:T(8,128)(2,1)S(1)}, u32[]{:S(2)}, u32[]{:S(2)}) async-start(bf16[8,32,512]{2,1,0:T(8,128)(2,1)} %shard_map.96), calls=%async_computation.3 | async-start | bytes 524288 | tf_op jit(solution)/shard_map/all_to_all | solution.py:223
  107.1 0.0 copy-done.2
  107.1 3.4 %collective-permute-start.6 = (bf16[2,128,512]{2,1,0:T(8,128)(2,1)S(1)}, bf16[2,128,512]{2,1,0:T(8,128)(2,1)S(1)}, u32[]{:S(2)}, u32[]{:S(2)}) collective-permute-start(bf16[2,128,512]{2,1,0:T(8,128)(2,1)S(1)} %copy-done.2), channel_id=1, source_target_pairs={{2,0},{3,1},{6,4},{7,5},{10,8},{11,9},{14,12},{15,13},{18,16},{19,... | collective-permute-start | bytes 786440 | tf_op jit(solution)/shard_map/ppermute | solution.py:219
  110.5 0.0 copy-done.3
  110.5 1.9 %collective-permute-start.5 = (bf16[2,128,512]{2,1,0:T(8,128)(2,1)S(1)}, bf16[2,128,512]{2,1,0:T(8,128)(2,1)S(1)}, u32[]{:S(2)}, u32[]{:S(2)}) collective-permute-start(bf16[2,128,512]{2,1,0:T(8,128)(2,1)S(1)} %copy-done.3), channel_id=1, source_target_pairs={{1,0},{2,1},{3,2},{5,4},{6,5},{7,6},{9,8},{10,9},{11,10},{13,12},{... | collective-permute-start | bytes 786440 | tf_op jit(solution)/shard_map/ppermute | solution.py:219
  112.5 6.6 %shard_map.95 = (bf16[128,4096]{1,0:T(8,128)(2,1)}, bf16[128,4096]{1,0:T(8,128)(2,1)}, f32[2,128,512]{2,1,0:T(8,128)}) custom-call(bf16[128,4096]{1,0:T(8,128)(2,1)} %query_ref.3, bf16[128,4096]{1,0:T(8,128)(2,1)} %grad_ref.3, bf16[2,128,512]{2,1,0:T(8,128)(2,1)} %broadcast_select_fusion.1.far_ref, bf16[2,128,512]{2,1,0:T(8,128)(2,1)} %broadcast_select_fusion.near_ref, ...), custom_call_target="tpu_custom_call" | custom-call | flops 1006632960 | bytes 10485760 | tf_op jit(solution)/shard_map/pallas_call | solution.py:162
  119.1 11.3 %all-to-all-done.3 = bf16[8,32,512]{2,1,0:T(8,128)(2,1)S(1)} async-done(((bf16[8,32,512]{2,1,0:T(8,128)(2,1)}), bf16[8,32,512]{2,1,0:T(8,128)(2,1)S(1)}, u32[]{:S(2)}, u32[]{:S(2)}) %all-to-all-start.3) | async-done | bytes 262176 | tf_op jit(solution)/shard_map/all_to_all | solution.py:223
  130.4 1.3 collective-permute-start.7
  131.7 0.0 collective-permute-done.6
  131.7 0.0 collective-permute-done.5
  131.7 1.1 convert_add_fusion
  132.9 4.6 %collective-permute-done.7 = bf16[128,512]{1,0:T(8,128)(2,1)S(1)} collective-permute-done((bf16[128,512]{1,0:T(8,128)(2,1)S(1)}, bf16[128,512]{1,0:T(8,128)(2,1)S(1)}, u32[]{:S(2)}, u32[]{:S(2)}) %collective-permute-start.7) | collective-permute-done | bytes 131104 | tf_op jit(solution)/shard_map/ppermute | solution.py:219
  137.4 0.8 fusion.1
  (5 shorter events, 0.1 us)
Async XLA Ops:
  0.6 5.5 %collective-permute-start = (bf16[128,512]{1,0:T(8,128)(2,1)}, bf16[128,512]{1,0:T(8,128)(2,1)S(1)}, u32[]{:S(2)}, u32[]{:S(2)}) collective-permute-start(bf16[128,512]{1,0:T(8,128)(2,1)} %param.8), channel_id=1, source_target_pairs={{2,0},{3,1},{6,4},{7,5},{10,8},{11,9},{14,12},{15,13},{18,16},{19,... | collective-permute-start | bytes 393224 | tf_op jit(solution)/shard_map/ppermute | solution.py:219
  7.8 40.3 %all-to-all-start = ((bf16[8,32,512]{2,1,0:T(8,128)(2,1)}), bf16[8,32,512]{2,1,0:T(8,128)(2,1)S(1)}, u32[]{:S(2)}, u32[]{:S(2)}) async-start(bf16[8,32,512]{2,1,0:T(8,128)(2,1)} %pad_maximum_fusion), calls=%async_computation | async-start | bytes 524288 | tf_op jit(solution)/shard_map/all_to_all | solution.py:223
  25.6 43.5 %copy-start = (bf16[2,128,512]{2,1,0:T(8,128)(2,1)}, bf16[2,128,512]{2,1,0:T(8,128)(2,1)S(1)}, u32[]{:S(2)}) copy-start(bf16[2,128,512]{2,1,0:T(8,128)(2,1)S(1)} %pad_maximum_fusion.1.own_ref) | copy-start | bytes 786436
  25.6 11.1 %collective-permute-start.2 = (bf16[2,128,512]{2,1,0:T(8,128)(2,1)S(1)}, bf16[2,128,512]{2,1,0:T(8,128)(2,1)S(1)}, u32[]{:S(2)}, u32[]{:S(2)}) collective-permute-start(bf16[2,128,512]{2,1,0:T(8,128)(2,1)S(1)} %pad_maximum_fusion.1.own_ref), channel_id=1, source_target_pairs={{0,2},{1,3},{4,6},{5,7},{8,10},{9,11},{12,14},{13,15},{16,18},{17,... | collective-permute-start | bytes 786440 | tf_op jit(solution)/shard_map/ppermute | solution.py:219
  26.9 10.3 %collective-permute-start.1 = (bf16[2,128,512]{2,1,0:T(8,128)(2,1)S(1)}, bf16[2,128,512]{2,1,0:T(8,128)(2,1)S(1)}, u32[]{:S(2)}, u32[]{:S(2)}) collective-permute-start(bf16[2,128,512]{2,1,0:T(8,128)(2,1)S(1)} %pad_maximum_fusion.1.own_ref), channel_id=1, source_target_pairs={{0,1},{1,2},{2,3},{4,5},{5,6},{6,7},{8,9},{9,10},{10,11},{12,13},{... | collective-permute-start | bytes 786440 | tf_op jit(solution)/shard_map/ppermute | solution.py:219
  48.1 0.7 copy-start.1
  67.0 1.4 %collective-permute-start.3 = (bf16[2,128,512]{2,1,0:T(8,128)(2,1)S(1)}, bf16[2,128,512]{2,1,0:T(8,128)(2,1)S(1)}, u32[]{:S(2)}, u32[]{:S(2)}) collective-permute-start(bf16[2,128,512]{2,1,0:T(8,128)(2,1)S(1)} %bitcast.35), channel_id=1, source_target_pairs={{1,0},{5,4},{9,8},{13,12},{17,16},{21,20},{25,24},{29,28},{33,32},... | collective-permute-start | bytes 786440 | tf_op jit(solution)/shard_map/ppermute | solution.py:219
  78.9 28.2 %copy-start.2 = (bf16[2,128,512]{2,1,0:T(8,128)(2,1)S(1)}, bf16[2,128,512]{2,1,0:T(8,128)(2,1)}, u32[]{:S(2)}) copy-start(bf16[2,128,512]{2,1,0:T(8,128)(2,1)} %get-tuple-element.20) | copy-start | bytes 786436
  78.9 31.6 %copy-start.3 = (bf16[2,128,512]{2,1,0:T(8,128)(2,1)S(1)}, bf16[2,128,512]{2,1,0:T(8,128)(2,1)}, u32[]{:S(2)}) copy-start(bf16[2,128,512]{2,1,0:T(8,128)(2,1)} %get-tuple-element.21) | copy-start | bytes 786436
  78.9 0.8 collective-permute-start.4
  103.7 26.7 %all-to-all-start.3 = ((bf16[8,32,512]{2,1,0:T(8,128)(2,1)}), bf16[8,32,512]{2,1,0:T(8,128)(2,1)S(1)}, u32[]{:S(2)}, u32[]{:S(2)}) async-start(bf16[8,32,512]{2,1,0:T(8,128)(2,1)} %shard_map.96), calls=%async_computation.3 | async-start | bytes 524288 | tf_op jit(solution)/shard_map/all_to_all | solution.py:223
  107.1 24.6 %collective-permute-start.6 = (bf16[2,128,512]{2,1,0:T(8,128)(2,1)S(1)}, bf16[2,128,512]{2,1,0:T(8,128)(2,1)S(1)}, u32[]{:S(2)}, u32[]{:S(2)}) collective-permute-start(bf16[2,128,512]{2,1,0:T(8,128)(2,1)S(1)} %copy-done.2), channel_id=1, source_target_pairs={{2,0},{3,1},{6,4},{7,5},{10,8},{11,9},{14,12},{15,13},{18,16},{19,... | collective-permute-start | bytes 786440 | tf_op jit(solution)/shard_map/ppermute | solution.py:219
  110.5 21.2 %collective-permute-start.5 = (bf16[2,128,512]{2,1,0:T(8,128)(2,1)S(1)}, bf16[2,128,512]{2,1,0:T(8,128)(2,1)S(1)}, u32[]{:S(2)}, u32[]{:S(2)}) collective-permute-start(bf16[2,128,512]{2,1,0:T(8,128)(2,1)S(1)} %copy-done.3), channel_id=1, source_target_pairs={{1,0},{2,1},{3,2},{5,4},{6,5},{7,6},{9,8},{10,9},{11,10},{13,12},{... | collective-permute-start | bytes 786440 | tf_op jit(solution)/shard_map/ppermute | solution.py:219
  130.4 7.0 %collective-permute-start.7 = (bf16[128,512]{1,0:T(8,128)(2,1)S(1)}, bf16[128,512]{1,0:T(8,128)(2,1)S(1)}, u32[]{:S(2)}, u32[]{:S(2)}) collective-permute-start(bf16[128,512]{1,0:T(8,128)(2,1)S(1)} %bitcast.39), channel_id=1, source_target_pairs={{0,2},{1,3},{4,6},{5,7},{8,10},{9,11},{12,14},{13,15},{16,18},{17,... | collective-permute-start | bytes 393224 | tf_op jit(solution)/shard_map/ppermute | solution.py:219

commit v5 on v4

v5 whole, which is shorter than its diff:
```python
import functools
import math

import jax
import jax.numpy as jnp
from jax import lax
from jax.experimental import pallas as pl
from jax.experimental.pallas import tpu as pltpu
from jax.sharding import PartitionSpec as P

HEAD_SIZE = 128
QUERY_HEADS = 32
KEY_VALUE_HEADS = 4
GROUP = QUERY_HEADS // KEY_VALUE_HEADS
CHUNK = 128
WINDOW = 3 * CHUNK
KV_WIDTH = KEY_VALUE_HEADS * HEAD_SIZE
BLOCK_AXES = ("x", "core")
SPREAD_AXES = ("y", "x")
PLANE_AXES = ("y", "b", "x")
COUNT = 16


def usable_bias(chunk, segments_ref, bias_ref):
    query_doc = jnp.broadcast_to(segments_ref[pl.ds(chunk, 1), :], (CHUNK, CHUNK))
    for back in (2, 1, 0):
        at = chunk - back
        row = segments_ref[pl.ds(jnp.maximum(at, 0), 1), :]
        row = jnp.where(at >= 0, row, -1)
        usable = jnp.broadcast_to(row, (CHUNK, CHUNK)).T == query_doc
        if back == 0:
            usable &= lax.broadcasted_iota(jnp.int32, (CHUNK, CHUNK), 0) <= (
                lax.broadcasted_iota(jnp.int32, (CHUNK, CHUNK), 1)
            )
        tile = jnp.where(usable, 0.0, -jnp.inf).astype(jnp.float32)
        rows = pl.ds((2 - back) * CHUNK, CHUNK)
        bias_ref[rows, 0:CHUNK] = tile
        bias_ref[rows, CHUNK : 2 * CHUNK] = tile


def stacked(ref, heads):
    return jnp.concatenate(
        [ref[:, a * HEAD_SIZE : (a + 1) * HEAD_SIZE] for a in heads], axis=0
    )


LAST = (((1,), (1,)), ((), ()))
PLAIN = (((1,), (0,)), ((), ()))


def dot(left, right, dims):
    return lax.dot_general(left, right, dims, preferred_element_type=jnp.float32)


def window(info_ref, cross_ref, before_ref, far_ref, near_ref, own_ref):
    chunk = info_ref[COUNT + 3]
    far = jnp.where(chunk < 2, cross_ref[...], far_ref[...])
    near = jnp.where(chunk == 0, before_ref[...], near_ref[...])
    return tuple(jnp.concatenate([far[i], near[i], own_ref[i]], axis=0) for i in range(2))


def score_kernel(
    info_ref,
    segments_ref,
    query_ref,
    grad_ref,
    cross_ref,
    before_ref,
    far_ref,
    near_ref,
    own_ref,
    weight_ref,
    dscore_ref,
    far_grad_ref,
    near_grad_ref,
    bias_ref,
):
    @pl.when(pl.program_id(0) == 0)
    def _():
        usable_bias(info_ref[info_ref[COUNT + 2]] * 4 + info_ref[COUNT + 3], segments_ref, bias_ref)

    scale = 1.0 / math.sqrt(HEAD_SIZE)
    values, keys = window(info_ref, cross_ref, before_ref, far_ref, near_ref, own_ref)
    width = 2 * CHUNK
    pairs = GROUP // 2

    def products(pair):
        heads = (2 * pair, 2 * pair + 1)
        return (
            dot(keys, stacked(query_ref, heads), LAST),
            dot(values, stacked(grad_ref, heads), LAST),
        )

    ahead = products(0)
    for pair in range(pairs):
        scores, dprob = ahead
        if pair + 1 < pairs:
            ahead = products(pair + 1)
        scores = scores + bias_ref[...]
        top = jnp.max(scores, axis=0, keepdims=True)
        raised = jnp.exp2((scores - top) * (scale * math.log2(math.e)))
        share = 1.0 / jnp.sum(raised, axis=0, keepdims=True)
        delta = jnp.sum(raised * dprob, axis=0, keepdims=True) * share
        columns = pl.ds(pair * width, width)
        weight_ref[:, columns] = (raised * share).astype(jnp.bfloat16)
        dscore_ref[:, columns] = (raised * (share * scale) * (dprob - delta)).astype(jnp.bfloat16)
    every = range(GROUP)
    halo = pl.ds(0, 2 * CHUNK)
    grad_keys = dot(dscore_ref[halo, :], stacked(query_ref, every), PLAIN).astype(jnp.bfloat16)
    grad_values = dot(weight_ref[halo, :], stacked(grad_ref, every), PLAIN).astype(jnp.bfloat16)
    for i, total in enumerate((grad_values, grad_keys)):
        far_grad_ref[i] = total[:CHUNK]
        near_grad_ref[i] = total[CHUNK:]


def output_kernel(
    info_ref,
    query_ref,
    grad_ref,
    cross_ref,
    before_ref,
    far_ref,
    near_ref,
    own_ref,
    weight_ref,
    dscore_ref,
    out_ref,
    grad_query_ref,
    own_grad_ref,
):
    values, keys = window(info_ref, cross_ref, before_ref, far_ref, near_ref, own_ref)
    values_t, keys_t = values.T, keys.T
    width = 2 * CHUNK
    for pair in range(GROUP // 2):
        columns = pl.ds(pair * width, width)
        output_t = dot(values_t, weight_ref[:, columns], PLAIN).astype(jnp.bfloat16)
        grad_query_t = dot(keys_t, dscore_ref[:, columns], PLAIN).astype(jnp.bfloat16)
        for i in range(2):
            columns = pl.ds(pair * width + i * CHUNK, CHUNK)
            part = slice(i * CHUNK, (i + 1) * CHUNK)
            out_ref[:, columns] = output_t[:, part].T
            grad_query_ref[:, columns] = grad_query_t[:, part].T
    every = range(GROUP)
    own = pl.ds(2 * CHUNK, CHUNK)
    own_grad_ref[0] = dot(weight_ref[own, :], stacked(grad_ref, every), PLAIN)
    own_grad_ref[1] = dot(dscore_ref[own, :], stacked(query_ref, every), PLAIN)


def attention_specs(rows):
    wide = pl.BlockSpec((rows, GROUP * HEAD_SIZE), lambda g, *_: (0, g))
    pair = pl.BlockSpec((2, rows, HEAD_SIZE), lambda g, *_: (0, 0, g))
    tall = pl.BlockSpec((WINDOW, GROUP * HEAD_SIZE), lambda g, *_: (0, g))
    return wide, pair, tall


def scores_and_halo(info, segments, queries, grads, pairs):
    rows = queries.shape[0]
    wide, pair, tall = attention_specs(rows)
    held = jax.ShapeDtypeStruct((WINDOW, queries.shape[1]), jnp.bfloat16)
    half = jax.ShapeDtypeStruct((2, rows, KV_WIDTH), jnp.bfloat16)
    return pl.pallas_call(
        score_kernel,
        grid_spec=pltpu.PrefetchScalarGridSpec(
            num_scalar_prefetch=1,
            grid=(KEY_VALUE_HEADS,),
            in_specs=[pl.BlockSpec(segments.shape, lambda g, *_: (0, 0)), wide, wide] + [pair] * 5,
            out_specs=[tall, tall, pair, pair],
            scratch_shapes=[pltpu.VMEM((WINDOW, 2 * CHUNK), jnp.float32)],
        ),
        out_shape=[held, held, half, half],
        compiler_params=pltpu.CompilerParams(vmem_limit_bytes=58 * 1024 * 1024),
        cost_estimate=pl.CostEstimate(
            flops=7 * rows * QUERY_HEADS * WINDOW * HEAD_SIZE,
            bytes_accessed=16 * rows * QUERY_HEADS * HEAD_SIZE,
            transcendentals=rows * QUERY_HEADS * WINDOW,
        ),
    )(info, segments, queries, grads, *pairs)


def outputs_and_own(info, queries, grads, pairs, weights, dscores):
    rows = queries.shape[0]
    wide, pair, tall = attention_specs(rows)
    like = jax.ShapeDtypeStruct(queries.shape, jnp.bfloat16)
    return pl.pallas_call(
        output_kernel,
        grid_spec=pltpu.PrefetchScalarGridSpec(
            num_scalar_prefetch=1,
            grid=(KEY_VALUE_HEADS,),
            in_specs=[wide, wide] + [pair] * 5 + [tall, tall],
            out_specs=[wide, wide, pair],
        ),
        out_shape=[like, like, jax.ShapeDtypeStruct((2, rows, KV_WIDTH), jnp.float32)],
        compiler_params=pltpu.CompilerParams(vmem_limit_bytes=58 * 1024 * 1024),
        cost_estimate=pl.CostEstimate(
            flops=5 * rows * QUERY_HEADS * WINDOW * HEAD_SIZE,
            bytes_accessed=20 * rows * QUERY_HEADS * HEAD_SIZE,
            transcendentals=0,
        ),
    )(info, queries, grads, *pairs, weights, dscores)


def slots_in_order(info_ref, slot_ref):
    for j in range(COUNT):
        slot_ref[info_ref[j]] = j


def route_forward_kernel(info_ref, here_ref, there_ref, out_ref, slot_ref):
    slots_in_order(info_ref, slot_ref)
    z, block = info_ref[COUNT], info_ref[COUNT + 1]
    empty = jnp.zeros(out_ref.shape[1:], out_ref.dtype)
    for i in range(8):
        source = slot_ref[lax.rem(info_ref[8 * z + i] + COUNT - 1, COUNT)]
        mine = lax.rem(source, 2) == block
        near = lax.div(source, 8) == z
        y = lax.rem(lax.div(source, 2), 4)
        out_ref[2 * i + 1] = empty

        @pl.when(jnp.logical_and(mine, near))
        def _(i=i, y=y):
            out_ref[2 * i] = here_ref[y]

        @pl.when(jnp.logical_and(mine, jnp.logical_not(near)))
        def _(i=i, y=y):
            out_ref[2 * i] = there_ref[y]

        @pl.when(jnp.logical_not(mine))
        def _(i=i):
            out_ref[2 * i] = empty


def route_back_kernel(info_ref, held_ref, here_ref, there_ref, slot_ref):
    slots_in_order(info_ref, slot_ref)
    z, block = info_ref[COUNT], info_ref[COUNT + 1]
    empty = jnp.zeros(here_ref.shape[1:], here_ref.dtype)
    for half, out_ref in ((z, here_ref), (1 - z, there_ref)):
        for y in range(4):
            after = slot_ref[lax.rem(info_ref[8 * half + 2 * y + block] + 1, COUNT)]
            mine = lax.div(after, 8) == z

            @pl.when(mine)
            def _(out_ref=out_ref, y=y, after=after):
                out_ref[y] = held_ref[2 * lax.rem(after, 8)]

            @pl.when(jnp.logical_not(mine))
            def _(out_ref=out_ref, y=y):
                out_ref[y] = empty


def route(kernel, info, operands, counts):
    shape = operands[0].shape[1:]
    whole = lambda n: pl.BlockSpec((n, *shape), lambda i, *_: (0, 0, 0))
    return pl.pallas_call(
        kernel,
        grid_spec=pltpu.PrefetchScalarGridSpec(
            num_scalar_prefetch=1,
            grid=(1,),
            in_specs=[whole(t.shape[0]) for t in operands],
            out_specs=[whole(n) for n in counts],
            scratch_shapes=[pltpu.SMEM((COUNT,), jnp.int32)],
        ),
        out_shape=[jax.ShapeDtypeStruct((n, *shape), jnp.bfloat16) for n in counts],
        cost_estimate=pl.CostEstimate(flops=0, bytes_accessed=1 << 20, transcendentals=0),
    )(info, *operands)


def move(value, moves):
    return lax.ppermute(value, BLOCK_AXES, moves)


def exchange(pieces, axes):
    return lax.all_to_all(pieces, axes, 0, 0)


def across(value):
    return lax.ppermute(value, "z", [(0, 1), (1, 0)])


def local(queries, keys, values, grads, segment_ids, order):
    z = lax.axis_index("z")
    block = lax.axis_index("b")
    c = lax.axis_index(BLOCK_AXES)
    place = [z, block, 8 * z + 2 * lax.axis_index("y") + block, c]
    info = jnp.concatenate([order, jnp.stack(place).astype(jnp.int32)])
    part = (4, CHUNK // 4, KV_WIDTH)
    whole = (CHUNK, KV_WIDTH)
    own = jnp.stack([values, keys], axis=0)

    pieces = own.reshape(2, *part).transpose(1, 0, 2, 3).reshape(8, *part[1:])
    here = exchange(pieces, SPREAD_AXES).reshape(4, 2, *part[1:])[:, 1]
    there = across(here)
    near_in = move(own, [(0, 1), (1, 2), (2, 3)])
    far_in = move(own, [(0, 2), (1, 3)])
    there, near_in, far_in = lax.optimization_barrier((there, near_in, far_in))
    (pieces,) = route(route_forward_kernel, info, (here, there), (16,))
    arrived = exchange(pieces, PLANE_AXES).reshape(4, 2, 2, *part[1:])
    cross = (arrived[:, 0] + arrived[:, 1]).transpose(1, 0, 2, 3).reshape(2, *whole)
    pairs = (cross, move(cross, [(1, 0)]), far_in, near_in, own)

    weights, dscores, far_grad, near_grad = scores_and_halo(
        info, segment_ids.reshape(-1, CHUNK), queries, grads, pairs
    )

    before = move(near_grad, [(0, 1)])
    halo = (far_grad.astype(jnp.float32) + before.astype(jnp.float32)).astype(jnp.bfloat16)
    pieces = halo.reshape(2, *part).transpose(1, 0, 2, 3)
    pieces = jnp.broadcast_to(pieces[:, None], (4, 2, 2, *part[1:])).reshape(16, *part[1:])
    held = exchange(pieces, PLANE_AXES)
    here, there = route(route_back_kernel, info, (held,), (4, 4))
    there, weights, dscores = lax.optimization_barrier((there, weights, dscores))
    there = across(there)
    attended, grad_query, own_grad = outputs_and_own(info, queries, grads, pairs, weights, dscores)
    near_back = move(near_grad, [(1, 0), (2, 1), (3, 2)])
    far_back = move(far_grad, [(2, 0), (3, 1)])
    pieces = jnp.broadcast_to((here + there)[:, None], (4, 2, *part[1:])).reshape(8, *part[1:])
    late = exchange(pieces, SPREAD_AXES).reshape(4, 2, *part[1:]).transpose(1, 0, 2, 3)
    late = jnp.where(c >= 2, late.reshape(2, *whole), 0)

    total = own_grad + near_back.astype(jnp.float32) + far_back.astype(jnp.float32)
    value_gradient = total[0] + late[0].astype(jnp.float32)
    key_gradient = total[1] + late[1].astype(jnp.float32)
    return (
        attended,
        grad_query,
        key_gradient.astype(jnp.bfloat16),
        value_gradient.astype(jnp.bfloat16),
    )


def solution(mesh):
    names = ("dp", "z", "y", "b", "x", "core")
    fine = jax.sharding.Mesh(mesh.devices.reshape(-1, 2, 4, 2, 2, 2), names)
    rows = P(names, None)
    return jax.shard_map(
        local,
        mesh=fine,
        in_specs=(rows, rows, rows, rows, P("dp"), P("dp")),
        out_specs=(rows, rows, rows, rows),
        check_vma=False,
    )
```

time: 139 us -> 136 us (0.978)
  the two profiles are of different devices: /device:TPU:34 before, /device:TPU:32 now
where the time goes in v5:
time: 136 us; the launch traced here: 135 us
  starting transfers between devices  50.5 us (37%)
  waiting for transfers between devices  32.9 us (24%)
  Pallas kernels  22 us (16%)
  blocking collectives  17.8 us (13%)
  other arithmetic  5.71 us (4%)
  local copies, waits for them, and re-layouts  5.07 us (4%)
    ppermute x2, starting transfers between devices, across(): return lax.ppermute(value, 'z', [(0, 1), (1, 0)])  26.8 us
    all_to_all x1, blocking collectives, exchange(): return lax.all_to_all(pieces, axes, 0, 0)  17.8 us
    all_to_all x3, waiting for transfers between devices, exchange(): return lax.all_to_all(pieces, axes, 0, 0)  17.2 us
    all_to_all x3, starting transfers between devices, exchange(): return lax.all_to_all(pieces, axes, 0, 0)  12.4 us
    ppermute x2, waiting for transfers between devices, across(): return lax.ppermute(value, 'z', [(0, 1), (1, 0)])  12.3 us
    ppermute x6, starting transfers between devices, move(): return lax.ppermute(value, BLOCK_AXES, moves)  11.3 us
    pallas_call x1, Pallas kernels, scores_and_halo(): pl.pallas_call(score_kernel, grid_spec=pltpu.PrefetchScalarGridSpec(num_s...  9.28 us
    pallas_call x1, Pallas kernels, outputs_and_own(): pl.pallas_call(output_kernel, grid_spec=pltpu.PrefetchScalarGridSpec(num_...  7.57 us
  transfers between devices with their start and end apart: 11, of which 7 were waited for; matrix products, arithmetic and copies ran while one was open for 3% of the time, Pallas kernels for 7%

profile of v5, /device:TPU:32, one launch (start us, length us, event | category | flops | bytes accessed | tf_op | source)
XLA Modules:
  0.0 134.8 jit_solution(4468324050510080248)
XLA Ops:
  0.6 1.7 %pad_maximum_fusion = bf16[2,4,32,512]{3,2,0,1:T(8,128)(2,1)} fusion(bf16[1,4,32,512]{3,2,0,1:T(8,128)(2,1)} %bitcast.46, bf16[1,4,32,512]{3,2,0,1:T(8,128)(2,1)} %bitcast.48), kind=kLoop, calls=%fused_computation.6 | loop fusion | flops 131072 | bytes 524288 | tf_op jit(solution)/shard_map/stack | solution.py:286
  2.3 5.4 %all-to-all-start = ((bf16[8,32,512]{2,1,0:T(8,128)(2,1)}), bf16[8,32,512]{2,1,0:T(8,128)(2,1)S(1)}, u32[]{:S(2)}, u32[]{:S(2)}) async-start(bf16[8,32,512]{2,1,0:T(8,128)(2,1)} %bitcast.7), calls=%async_computation | async-start | bytes 524288 | tf_op jit(solution)/shard_map/all_to_all | solution.py:271
  7.7 1.0 pad_maximum_fusion.1.own_ref
  8.7 0.0 copy-start.2
  8.7 3.9 %collective-permute-start.2 = (bf16[2,128,512]{2,1,0:T(8,128)(2,1)S(1)}, bf16[2,128,512]{2,1,0:T(8,128)(2,1)S(1)}, u32[]{:S(2)}, u32[]{:S(2)}) collective-permute-start(bf16[2,128,512]{2,1,0:T(8,128)(2,1)S(1)} %pad_maximum_fusion.1.own_ref), channel_id=1, source_target_pairs={{0,2},{1,3},{4,6},{5,7},{8,10},{9,11},{12,14},{13,15},{16,18},{17,... | collective-permute-start | bytes 786440 | tf_op jit(solution)/shard_map/ppermute | solution.py:267
  12.7 1.3 collective-permute-start.1
  14.0 1.0 all-to-all-done
  15.0 0.0 copy-start.3
  15.0 14.8 %collective-permute-start = (bf16[4,32,512]{2,1,0:T(8,128)(2,1)S(1)}, bf16[4,32,512]{2,1,0:T(8,128)(2,1)S(1)}, u32[]{:S(2)}, u32[]{:S(2)}) collective-permute-start(bf16[4,32,512]{2,1,0:T(8,128)(2,1)S(1)} %slice_bitcast_fusion.here_ref), channel_id=1, source_target_pairs={{0,32},{32,0},{1,33},{33,1},{2,34},{34,2},{3,35},{35,3},{4,36},{36... | collective-permute-start | bytes 393224 | tf_op jit(solution)/shard_map/ppermute | solution.py:275
  29.9 1.2 concatenate.4.info_ref
  31.1 0.0 collective-permute-done.2.far_ref
  31.1 0.0 collective-permute-done.1.near_ref
  31.1 0.0 copy-start.5
  31.1 9.9 %collective-permute-done.there_ref = bf16[4,32,512]{2,1,0:T(8,128)(2,1)S(1)} collective-permute-done((bf16[4,32,512]{2,1,0:T(8,128)(2,1)S(1)}, bf16[4,32,512]{2,1,0:T(8,128)(2,1)S(1)}, u32[]{:S(2)}, u32[]{:S(2)}) %collective-permute-start) | collective-permute-done | bytes 131104 | tf_op jit(solution)/shard_map/ppermute | solution.py:275
  41.0 0.0 copy-done.3
  41.0 0.7 copy-done.9
  41.7 2.6 %shard_map.93 = bf16[16,32,512]{2,1,0:T(8,128)(2,1)} custom-call(s32[20]{0:T(128)} %concatenate.4.info_ref, bf16[4,32,512]{2,1,0:T(8,128)(2,1)} %copy-done.3, bf16[4,32,512]{2,1,0:T(8,128)(2,1)} %copy-done.9), custom_call_target="tpu_custom_call" | custom-call | bytes 1048576 | tf_op jit(solution)/shard_map/pallas_call | solution.py:252
  44.3 17.8 %all_to_all.20 = bf16[16,32,512]{2,1,0:T(8,128)(2,1)S(1)} all-to-all(bf16[16,32,512]{2,1,0:T(8,128)(2,1)} %shard_map.93), channel_id=1, replica_groups=mesh['dp'=8,'z'=2,'y'=4,'b'=2,'x'=2,'core'=2] {'y','b','x'}, dimensions={0} | all-to-all | bytes 1048576 | tf_op jit(solution)/shard_map/all_to_all | solution.py:271
  62.2 0.0 copy-start.1
  62.2 1.3 collective-permute-start.3
  63.5 2.1 %collective-permute-done.3.before_ref = bf16[2,128,512]{2,1,0:T(8,128)(2,1)S(1)} collective-permute-done((bf16[2,128,512]{2,1,0:T(8,128)(2,1)S(1)}, bf16[2,128,512]{2,1,0:T(8,128)(2,1)S(1)}, u32[]{:S(2)}, u32[]{:S(2)}) %collective-permute-start.3) | collective-permute-done | bytes 262176 | tf_op jit(solution)/shard_map/ppermute | solution.py:267
  65.6 0.0 copy-done.4
  65.6 0.0 copy-done.1
  65.6 0.7 copy-done.7
  66.3 9.3 %shard_map.94 = (bf16[384,4096]{1,0:T(8,128)(2,1)}, bf16[384,4096]{1,0:T(8,128)(2,1)}, bf16[2,128,512]{2,1,0:T(8,128)(2,1)}, bf16[2,128,512]{2,1,0:T(8,128)(2,1)}) custom-call(s32[20]{0:T(128)} %concatenate.4.info_ref, s32[64,128]{1,0:T(8,128)} %bitcast.52, bf16[128,4096]{1,0:T(8,128)(2,1)} %query_ref.3, bf16[128,4096]{1,0:T(8,128)(2,1)} %grad_ref.3, ...), custom_call_target="tpu_custom_call" | custom-call | flops 1409286144 | bytes 8388608 | tf_op jit(solution)/shard_map/pallas_call | solution.py:161
  75.6 2.2 %collective-permute-start.4 = (bf16[2,128,512]{2,1,0:T(8,128)(2,1)}, bf16[2,128,512]{2,1,0:T(8,128)(2,1)S(1)}, u32[]{:S(2)}, u32[]{:S(2)}) collective-permute-start(bf16[2,128,512]{2,1,0:T(8,128)(2,1)} %get-tuple-element.23), channel_id=1, source_target_pairs={{0,1},{4,5},{8,9},{12,13},{16,17},{20,21},{24,25},{28,29},{32,33},... | collective-permute-start | bytes 786440 | tf_op jit(solution)/shard_map/ppermute | solution.py:267
  77.8 1.3 collective-permute-done.4
  79.1 1.0 add_convert_fusion
  80.2 0.8 broadcast_in_dim.7
  81.0 3.6 %all-to-all-start.2 = ((bf16[16,32,512]{2,1,0:T(8,128)(2,1)}), bf16[16,32,512]{2,1,0:T(8,128)(2,1)S(1)}, u32[]{:S(2)}, u32[]{:S(2)}) async-start(bf16[16,32,512]{2,1,0:T(8,128)(2,1)} %bitcast.21), calls=%async_computation.2 | async-start | bytes 1048576 | tf_op jit(solution)/shard_map/all_to_all | solution.py:271
  84.6 0.0 copy-done.6
  84.6 1.3 collective-permute-start.6
  85.9 0.0 copy-done.10
  85.9 1.3 collective-permute-start.5
  87.2 9.7 %all-to-all-done.2.held_ref = bf16[16,32,512]{2,1,0:T(8,128)(2,1)S(1)} async-done(((bf16[16,32,512]{2,1,0:T(8,128)(2,1)}), bf16[16,32,512]{2,1,0:T(8,128)(2,1)S(1)}, u32[]{:S(2)}, u32[]{:S(2)}) %all-to-all-start.2) | async-done | bytes 524320 | tf_op jit(solution)/shard_map/all_to_all | solution.py:271
  96.9 0.8 copy-done
  97.7 2.5 %shard_map.95 = (bf16[4,32,512]{2,1,0:T(8,128)(2,1)}, bf16[4,32,512]{2,1,0:T(8,128)(2,1)}) custom-call(s32[20]{0:T(128)} %concatenate.4.info_ref, bf16[16,32,512]{2,1,0:T(8,128)(2,1)} %copy-done), custom_call_target="tpu_custom_call" | custom-call | bytes 1048576 | tf_op jit(solution)/shard_map/pallas_call | solution.py:252
  100.2 12.0 %collective-permute-start.7 = (bf16[4,32,512]{2,1,0:T(8,128)(2,1)}, bf16[4,32,512]{2,1,0:T(8,128)(2,1)S(1)}, u32[]{:S(2)}, u32[]{:S(2)}) collective-permute-start(bf16[4,32,512]{2,1,0:T(8,128)(2,1)} %get-tuple-element.33), channel_id=1, source_target_pairs={{0,32},{32,0},{1,33},{33,1},{2,34},{34,2},{3,35},{35,3},{4,36},{36... | collective-permute-start | bytes 393224 | tf_op jit(solution)/shard_map/ppermute | solution.py:275
  112.2 0.0 copy-start.8
  112.2 7.6 %shard_map.96 = (bf16[128,4096]{1,0:T(8,128)(2,1)}, bf16[128,4096]{1,0:T(8,128)(2,1)}, f32[2,128,512]{2,1,0:T(8,128)}) custom-call(s32[20]{0:T(128)} %concatenate.4.info_ref, bf16[128,4096]{1,0:T(8,128)(2,1)} %query_ref.3, bf16[128,4096]{1,0:T(8,128)(2,1)} %grad_ref.3, bf16[2,128,512]{2,1,0:T(8,128)(2,1)} %bitcast.42, bf16[2,128,512]{2,1,0:T(8,128)(2,1)} %copy-done.7, ...), custom_call_target="tpu_custom_call" | custom-call | flops 1006632960 | bytes 10485760 | tf_op jit(solution)/shard_map/pallas_call | solution.py:184
  119.8 2.4 %collective-permute-done.7 = bf16[4,32,512]{2,1,0:T(8,128)(2,1)S(1)} collective-permute-done((bf16[4,32,512]{2,1,0:T(8,128)(2,1)}, bf16[4,32,512]{2,1,0:T(8,128)(2,1)S(1)}, u32[]{:S(2)}, u32[]{:S(2)}) %collective-permute-start.7) | collective-permute-done | bytes 131104 | tf_op jit(solution)/shard_map/ppermute | solution.py:275
  122.2 0.7 broadcast_in_dim.8
  123.0 3.4 %all-to-all-start.3 = ((bf16[8,32,512]{2,1,0:T(8,128)(2,1)}), bf16[8,32,512]{2,1,0:T(8,128)(2,1)S(1)}, u32[]{:S(2)}, u32[]{:S(2)}) async-start(bf16[8,32,512]{2,1,0:T(8,128)(2,1)} %bitcast.22), calls=%async_computation.3 | async-start | bytes 524288 | tf_op jit(solution)/shard_map/all_to_all | solution.py:271
  126.4 0.0 collective-permute-done.6
  126.4 0.0 collective-permute-done.5
  126.4 1.1 convert_add_fusion
  127.5 6.5 %all-to-all-done.3 = bf16[8,32,512]{2,1,0:T(8,128)(2,1)S(1)} async-done(((bf16[8,32,512]{2,1,0:T(8,128)(2,1)}), bf16[8,32,512]{2,1,0:T(8,128)(2,1)S(1)}, u32[]{:S(2)}, u32[]{:S(2)}) %all-to-all-start.3) | async-done | bytes 262176 | tf_op jit(solution)/shard_map/all_to_all | solution.py:271
  134.1 0.8 fusion.3
  (16 shorter events, 0.2 us)
Async XLA Ops:
  2.3 12.7 %all-to-all-start = ((bf16[8,32,512]{2,1,0:T(8,128)(2,1)}), bf16[8,32,512]{2,1,0:T(8,128)(2,1)S(1)}, u32[]{:S(2)}, u32[]{:S(2)}) async-start(bf16[8,32,512]{2,1,0:T(8,128)(2,1)} %bitcast.7), calls=%async_computation | async-start | bytes 524288 | tf_op jit(solution)/shard_map/all_to_all | solution.py:271
  8.7 56.9 %copy-start.2 = (bf16[2,128,512]{2,1,0:T(8,128)(2,1)}, bf16[2,128,512]{2,1,0:T(8,128)(2,1)S(1)}, u32[]{:S(2)}) copy-start(bf16[2,128,512]{2,1,0:T(8,128)(2,1)S(1)} %pad_maximum_fusion.1.own_ref) | copy-start | bytes 786436
  8.7 22.4 %collective-permute-start.2 = (bf16[2,128,512]{2,1,0:T(8,128)(2,1)S(1)}, bf16[2,128,512]{2,1,0:T(8,128)(2,1)S(1)}, u32[]{:S(2)}, u32[]{:S(2)}) collective-permute-start(bf16[2,128,512]{2,1,0:T(8,128)(2,1)S(1)} %pad_maximum_fusion.1.own_ref), channel_id=1, source_target_pairs={{0,2},{1,3},{4,6},{5,7},{8,10},{9,11},{12,14},{13,15},{16,18},{17,... | collective-permute-start | bytes 786440 | tf_op jit(solution)/shard_map/ppermute | solution.py:267
  12.7 18.4 %collective-permute-start.1 = (bf16[2,128,512]{2,1,0:T(8,128)(2,1)S(1)}, bf16[2,128,512]{2,1,0:T(8,128)(2,1)S(1)}, u32[]{:S(2)}, u32[]{:S(2)}) collective-permute-start(bf16[2,128,512]{2,1,0:T(8,128)(2,1)S(1)} %pad_maximum_fusion.1.own_ref), channel_id=1, source_target_pairs={{0,1},{1,2},{2,3},{4,5},{5,6},{6,7},{8,9},{9,10},{10,11},{12,13},{... | collective-permute-start | bytes 786440 | tf_op jit(solution)/shard_map/ppermute | solution.py:267
  15.0 26.0 %copy-start.3 = (bf16[4,32,512]{2,1,0:T(8,128)(2,1)}, bf16[4,32,512]{2,1,0:T(8,128)(2,1)S(1)}, u32[]{:S(2)}) copy-start(bf16[4,32,512]{2,1,0:T(8,128)(2,1)S(1)} %slice_bitcast_fusion.here_ref) | copy-start | bytes 393220
  15.0 26.0 %collective-permute-start = (bf16[4,32,512]{2,1,0:T(8,128)(2,1)S(1)}, bf16[4,32,512]{2,1,0:T(8,128)(2,1)S(1)}, u32[]{:S(2)}, u32[]{:S(2)}) collective-permute-start(bf16[4,32,512]{2,1,0:T(8,128)(2,1)S(1)} %slice_bitcast_fusion.here_ref), channel_id=1, source_target_pairs={{0,32},{32,0},{1,33},{33,1},{2,34},{34,2},{3,35},{35,3},{4,36},{36... | collective-permute-start | bytes 393224 | tf_op jit(solution)/shard_map/ppermute | solution.py:275
  31.1 34.5 %copy-start.4 = (bf16[2,128,512]{2,1,0:T(8,128)(2,1)}, bf16[2,128,512]{2,1,0:T(8,128)(2,1)S(1)}, u32[]{:S(2)}) copy-start(bf16[2,128,512]{2,1,0:T(8,128)(2,1)S(1)} %collective-permute-done.2.far_ref) | copy-start | bytes 786436
  31.1 34.5 %copy-start.5 = (bf16[2,128,512]{2,1,0:T(8,128)(2,1)}, bf16[2,128,512]{2,1,0:T(8,128)(2,1)S(1)}, u32[]{:S(2)}) copy-start(bf16[2,128,512]{2,1,0:T(8,128)(2,1)S(1)} %collective-permute-done.1.near_ref) | copy-start | bytes 786436
  41.0 0.7 copy-start.9
  62.2 3.5 %copy-start.1 = (bf16[4,1,2,32,512]{4,3,0,2,1:T(8,128)(2,1)}, bf16[4,1,2,32,512]{4,3,0,2,1:T(8,128)(2,1)S(1)}, u32[]{:S(2)}) copy-start(bf16[4,1,2,32,512]{4,3,0,2,1:T(8,128)(2,1)S(1)} %copy_add_fusion) | copy-start | bytes 786436
  62.2 3.4 %collective-permute-start.3 = (bf16[2,128,512]{2,1,0:T(8,128)(2,1)S(1)}, bf16[2,128,512]{2,1,0:T(8,128)(2,1)S(1)}, u32[]{:S(2)}, u32[]{:S(2)}) collective-permute-start(bf16[2,128,512]{2,1,0:T(8,128)(2,1)S(1)} %bitcast.40), channel_id=1, source_target_pairs={{1,0},{5,4},{9,8},{13,12},{17,16},{21,20},{25,24},{29,28},{33,32},... | collective-permute-start | bytes 786440 | tf_op jit(solution)/shard_map/ppermute | solution.py:267
  65.6 0.7 copy-start.7
  75.6 9.0 %copy-start.6 = (bf16[2,128,512]{2,1,0:T(8,128)(2,1)S(1)}, bf16[2,128,512]{2,1,0:T(8,128)(2,1)}, u32[]{:S(2)}) copy-start(bf16[2,128,512]{2,1,0:T(8,128)(2,1)} %get-tuple-element.22) | copy-start | bytes 786436
  75.6 10.3 %copy-start.10 = (bf16[2,128,512]{2,1,0:T(8,128)(2,1)S(1)}, bf16[2,128,512]{2,1,0:T(8,128)(2,1)}, u32[]{:S(2)}) copy-start(bf16[2,128,512]{2,1,0:T(8,128)(2,1)} %get-tuple-element.23) | copy-start | bytes 786436
  75.6 3.5 %collective-permute-start.4 = (bf16[2,128,512]{2,1,0:T(8,128)(2,1)}, bf16[2,128,512]{2,1,0:T(8,128)(2,1)S(1)}, u32[]{:S(2)}, u32[]{:S(2)}) collective-permute-start(bf16[2,128,512]{2,1,0:T(8,128)(2,1)} %get-tuple-element.23), channel_id=1, source_target_pairs={{0,1},{4,5},{8,9},{12,13},{16,17},{20,21},{24,25},{28,29},{32,33},... | collective-permute-start | bytes 786440 | tf_op jit(solution)/shard_map/ppermute | solution.py:267
  81.0 15.9 %all-to-all-start.2 = ((bf16[16,32,512]{2,1,0:T(8,128)(2,1)}), bf16[16,32,512]{2,1,0:T(8,128)(2,1)S(1)}, u32[]{:S(2)}, u32[]{:S(2)}) async-start(bf16[16,32,512]{2,1,0:T(8,128)(2,1)} %bitcast.21), calls=%async_computation.2 | async-start | bytes 1048576 | tf_op jit(solution)/shard_map/all_to_all | solution.py:271
  84.6 41.8 %collective-permute-start.6 = (bf16[2,128,512]{2,1,0:T(8,128)(2,1)S(1)}, bf16[2,128,512]{2,1,0:T(8,128)(2,1)S(1)}, u32[]{:S(2)}, u32[]{:S(2)}) collective-permute-start(bf16[2,128,512]{2,1,0:T(8,128)(2,1)S(1)} %copy-done.6), channel_id=1, source_target_pairs={{2,0},{3,1},{6,4},{7,5},{10,8},{11,9},{14,12},{15,13},{18,16},{19,... | collective-permute-start | bytes 786440 | tf_op jit(solution)/shard_map/ppermute | solution.py:267
  85.9 40.5 %collective-permute-start.5 = (bf16[2,128,512]{2,1,0:T(8,128)(2,1)S(1)}, bf16[2,128,512]{2,1,0:T(8,128)(2,1)S(1)}, u32[]{:S(2)}, u32[]{:S(2)}) collective-permute-start(bf16[2,128,512]{2,1,0:T(8,128)(2,1)S(1)} %copy-done.10), channel_id=1, source_target_pairs={{1,0},{2,1},{3,2},{5,4},{6,5},{7,6},{9,8},{10,9},{11,10},{13,12},{... | collective-permute-start | bytes 786440 | tf_op jit(solution)/shard_map/ppermute | solution.py:267
  96.9 0.8 copy-start
  100.2 22.0 %collective-permute-start.7 = (bf16[4,32,512]{2,1,0:T(8,128)(2,1)}, bf16[4,32,512]{2,1,0:T(8,128)(2,1)S(1)}, u32[]{:S(2)}, u32[]{:S(2)}) collective-permute-start(bf16[4,32,512]{2,1,0:T(8,128)(2,1)} %get-tuple-element.33), channel_id=1, source_target_pairs={{0,32},{32,0},{1,33},{33,1},{2,34},{34,2},{3,35},{35,3},{4,36},{36... | collective-permute-start | bytes 393224 | tf_op jit(solution)/shard_map/ppermute | solution.py:275
  112.2 10.0 %copy-start.8 = (bf16[4,32,512]{2,1,0:T(8,128)(2,1)S(1)}, bf16[4,32,512]{2,1,0:T(8,128)(2,1)}, u32[]{:S(2)}) copy-start(bf16[4,32,512]{2,1,0:T(8,128)(2,1)} %get-tuple-element.32) | copy-start | bytes 393220
  123.0 11.0 %all-to-all-start.3 = ((bf16[8,32,512]{2,1,0:T(8,128)(2,1)}), bf16[8,32,512]{2,1,0:T(8,128)(2,1)S(1)}, u32[]{:S(2)}, u32[]{:S(2)}) async-start(bf16[8,32,512]{2,1,0:T(8,128)(2,1)} %bitcast.22), calls=%async_computation.3 | async-start | bytes 524288 | tf_op jit(solution)/shard_map/all_to_all | solution.py:271

commit v6 on v5

--- a/solution.py
+++ b/solution.py
@@ -16,8 +16,8 @@
 WINDOW = 3 * CHUNK
 KV_WIDTH = KEY_VALUE_HEADS * HEAD_SIZE
 BLOCK_AXES = ("x", "core")
-SPREAD_AXES = ("y", "x")
-PLANE_AXES = ("y", "b", "x")
+SPREAD_AXES = ("x", "y")
+PLANE_AXES = ("x", "y", "b")
 COUNT = 16
 
 
@@ -213,19 +213,19 @@
         mine = lax.rem(source, 2) == block
         near = lax.div(source, 8) == z
         y = lax.rem(lax.div(source, 2), 4)
-        out_ref[2 * i + 1] = empty
+        out_ref[8 + i] = empty
 
         @pl.when(jnp.logical_and(mine, near))
         def _(i=i, y=y):
-            out_ref[2 * i] = here_ref[y]
+            out_ref[i] = here_ref[y]
 
         @pl.when(jnp.logical_and(mine, jnp.logical_not(near)))
         def _(i=i, y=y):
-            out_ref[2 * i] = there_ref[y]
+            out_ref[i] = there_ref[y]
 
         @pl.when(jnp.logical_not(mine))
         def _(i=i):
-            out_ref[2 * i] = empty
+            out_ref[i] = empty
 
 
 def route_back_kernel(info_ref, held_ref, here_ref, there_ref, slot_ref):
@@ -239,7 +239,7 @@
 
             @pl.when(mine)
             def _(out_ref=out_ref, y=y, after=after):
-                out_ref[y] = held_ref[2 * lax.rem(after, 8)]
+                out_ref[y] = held_ref[lax.rem(after, 8)]
 
             @pl.when(jnp.logical_not(mine))
             def _(out_ref=out_ref, y=y):
@@ -248,17 +248,14 @@
 
 def route(kernel, info, operands, counts):
     shape = operands[0].shape[1:]
-    whole = lambda n: pl.BlockSpec((n, *shape), lambda i, *_: (0, 0, 0))
+    in_vmem = pl.BlockSpec(memory_space=pltpu.VMEM)
     return pl.pallas_call(
         kernel,
-        grid_spec=pltpu.PrefetchScalarGridSpec(
-            num_scalar_prefetch=1,
-            grid=(1,),
-            in_specs=[whole(t.shape[0]) for t in operands],
-            out_specs=[whole(n) for n in counts],
-            scratch_shapes=[pltpu.SMEM((COUNT,), jnp.int32)],
-        ),
+        in_specs=[pl.BlockSpec(memory_space=pltpu.SMEM)] + [in_vmem] * len(operands),
+        out_specs=[in_vmem] * len(counts),
         out_shape=[jax.ShapeDtypeStruct((n, *shape), jnp.bfloat16) for n in counts],
+        scratch_shapes=[pltpu.SMEM((COUNT,), jnp.int32)],
+        compiler_params=pltpu.CompilerParams(vmem_limit_bytes=4 * 1024 * 1024),
         cost_estimate=pl.CostEstimate(flops=0, bytes_accessed=1 << 20, transcendentals=0),
     )(info, *operands)
 
@@ -285,15 +282,14 @@
     whole = (CHUNK, KV_WIDTH)
     own = jnp.stack([values, keys], axis=0)
 
-    pieces = own.reshape(2, *part).transpose(1, 0, 2, 3).reshape(8, *part[1:])
-    here = exchange(pieces, SPREAD_AXES).reshape(4, 2, *part[1:])[:, 1]
+    here = exchange(own.reshape(8, *part[1:]), SPREAD_AXES).reshape(2, *part)[1]
     there = across(here)
     near_in = move(own, [(0, 1), (1, 2), (2, 3)])
     far_in = move(own, [(0, 2), (1, 3)])
     there, near_in, far_in = lax.optimization_barrier((there, near_in, far_in))
     (pieces,) = route(route_forward_kernel, info, (here, there), (16,))
-    arrived = exchange(pieces, PLANE_AXES).reshape(4, 2, 2, *part[1:])
-    cross = (arrived[:, 0] + arrived[:, 1]).transpose(1, 0, 2, 3).reshape(2, *whole)
+    arrived = exchange(pieces, PLANE_AXES).reshape(2, 4, 2, *part[1:])
+    cross = (arrived[:, :, 0] + arrived[:, :, 1]).reshape(2, *whole)
     pairs = (cross, move(cross, [(1, 0)]), far_in, near_in, own)
 
     weights, dscores, far_grad, near_grad = scores_and_halo(
@@ -302,18 +298,18 @@
 
     before = move(near_grad, [(0, 1)])
     halo = (far_grad.astype(jnp.float32) + before.astype(jnp.float32)).astype(jnp.bfloat16)
-    pieces = halo.reshape(2, *part).transpose(1, 0, 2, 3)
-    pieces = jnp.broadcast_to(pieces[:, None], (4, 2, 2, *part[1:])).reshape(16, *part[1:])
-    held = exchange(pieces, PLANE_AXES)
+    pieces = jnp.broadcast_to(halo.reshape(2, 4, 1, *part[1:]), (2, 4, 2, *part[1:]))
+    pieces, weights, dscores = lax.optimization_barrier((pieces, weights, dscores))
+    held = exchange(pieces.reshape(16, *part[1:]), PLANE_AXES)
+    attended, grad_query, own_grad = outputs_and_own(info, queries, grads, pairs, weights, dscores)
+    held, own_grad = lax.optimization_barrier((held, own_grad))
     here, there = route(route_back_kernel, info, (held,), (4, 4))
-    there, weights, dscores = lax.optimization_barrier((there, weights, dscores))
     there = across(there)
-    attended, grad_query, own_grad = outputs_and_own(info, queries, grads, pairs, weights, dscores)
     near_back = move(near_grad, [(1, 0), (2, 1), (3, 2)])
     far_back = move(far_grad, [(2, 0), (3, 1)])
-    pieces = jnp.broadcast_to((here + there)[:, None], (4, 2, *part[1:])).reshape(8, *part[1:])
-    late = exchange(pieces, SPREAD_AXES).reshape(4, 2, *part[1:]).transpose(1, 0, 2, 3)
-    late = jnp.where(c >= 2, late.reshape(2, *whole), 0)
+    pieces = jnp.broadcast_to(here + there, (2, *part)).reshape(8, *part[1:])
+    late = exchange(pieces, SPREAD_AXES).reshape(2, *whole)
+    late = jnp.where(c >= 2, late, 0)
 
     total = own_grad + near_back.astype(jnp.float32) + far_back.astype(jnp.float32)
     value_gradient = total[0] + late[0].astype(jnp.float32)

time: 136 us -> 132 us (0.971)
  Pallas kernels: 22 us -> 18.4 us
  starting transfers between devices: 50.5 us -> 53.7 us
  local copies, waits for them, and re-layouts: 5.07 us -> 3.06 us
    ppermute x2, waiting for transfers between devices: 12.3 us -> 19.7 us  [across(): return lax.ppermute(value, 'z', [(0, 1), (1, 0)])]
    all_to_all x3, waiting for transfers between devices: 17.2 us -> 9.79 us  [exchange(): return lax.all_to_all(pieces, axes, 0, 0)]
    pallas_call x2, Pallas kernels: 5.11 us -> 1.54 us  [route(): pl.pallas_call(kernel, in_specs=[pl.BlockSpec(memory_space=pltpu.SMEM)] +...]
    all_to_all x3, starting transfers between devices: 12.4 us -> 15.7 us  [exchange(): return lax.all_to_all(pieces, axes, 0, 0)]
    unnamed x22 -> x12, local copies, waits for them, and re-layouts: 2.17 us -> 0.71 us
  transfers between devices with their start and end apart: 11 -> 11, of which waited for: 7 -> 7; matrix products, arithmetic and copies ran while one was open for 3% -> 2% of each run, Pallas kernels for 7% -> 6%
where the time goes in v6:
time: 132 us; the launch traced here: 131 us
  starting transfers between devices  53.7 us (41%)
  waiting for transfers between devices  33 us (25%)
  Pallas kernels  18.4 us (14%)
  blocking collectives  17.4 us (13%)
  other arithmetic  4.78 us (4%)
  local copies, waits for them, and re-layouts  3.06 us (2%)
    ppermute x2, starting transfers between devices, across(): return lax.ppermute(value, 'z', [(0, 1), (1, 0)])  26.8 us
    ppermute x2, waiting for transfers between devices, across(): return lax.ppermute(value, 'z', [(0, 1), (1, 0)])  19.7 us
    all_to_all x1, blocking collectives, exchange(): return lax.all_to_all(pieces, axes, 0, 0)  17.4 us
    all_to_all x3, starting transfers between devices, exchange(): return lax.all_to_all(pieces, axes, 0, 0)  15.7 us
    ppermute x6, starting transfers between devices, move(): return lax.ppermute(value, BLOCK_AXES, moves)  11.2 us
    all_to_all x3, waiting for transfers between devices, exchange(): return lax.all_to_all(pieces, axes, 0, 0)  9.79 us
    pallas_call x1, Pallas kernels, scores_and_halo(): pl.pallas_call(score_kernel, grid_spec=pltpu.PrefetchScalarGridSpec(num_s...  9.37 us
    pallas_call x1, Pallas kernels, outputs_and_own(): pl.pallas_call(output_kernel, grid_spec=pltpu.PrefetchScalarGridSpec(num_...  7.47 us
  transfers between devices with their start and end apart: 11, of which 7 were waited for; matrix products, arithmetic and copies ran while one was open for 2% of the time, Pallas kernels for 6%

profile of v6, /device:TPU:32, one launch (start us, length us, event | category | flops | bytes accessed | tf_op | source)
XLA Modules:
  0.0 131.1 jit_solution(15292761174022123630)
XLA Ops:
  0.6 1.8 %pad_maximum_fusion.own_ref = bf16[2,128,512]{2,1,0:T(8,128)(2,1)} fusion(bf16[1,128,512]{2,1,0:T(8,128)(2,1)} %bitcast.39, bf16[1,128,512]{2,1,0:T(8,128)(2,1)} %bitcast.40), kind=kLoop, calls=%fused_computation.9 | loop fusion | flops 131072 | bytes 524288 | tf_op jit(solution)/shard_map/stack | solution.py:283
  2.4 5.4 %all-to-all-start = ((bf16[8,32,512]{2,1,0:T(8,128)(2,1)}), bf16[8,32,512]{2,1,0:T(8,128)(2,1)S(1)}, u32[]{:S(2)}, u32[]{:S(2)}) async-start(bf16[8,32,512]{2,1,0:T(8,128)(2,1)} %bitcast.6), calls=%async_computation | async-start | bytes 524288 | tf_op jit(solution)/shard_map/all_to_all | solution.py:268
  7.8 3.9 %collective-permute-start.2 = (bf16[2,128,512]{2,1,0:T(8,128)(2,1)}, bf16[2,128,512]{2,1,0:T(8,128)(2,1)S(1)}, u32[]{:S(2)}, u32[]{:S(2)}) collective-permute-start(bf16[2,128,512]{2,1,0:T(8,128)(2,1)} %pad_maximum_fusion.own_ref), channel_id=1, source_target_pairs={{0,2},{1,3},{4,6},{5,7},{8,10},{9,11},{12,14},{13,15},{16,18},{17,... | collective-permute-start | bytes 786440 | tf_op jit(solution)/shard_map/ppermute | solution.py:264
  11.7 1.3 collective-permute-start.1
  13.0 2.0 %all-to-all-done = bf16[8,32,512]{2,1,0:T(8,128)(2,1)S(1)} async-done(((bf16[8,32,512]{2,1,0:T(8,128)(2,1)}), bf16[8,32,512]{2,1,0:T(8,128)(2,1)S(1)}, u32[]{:S(2)}, u32[]{:S(2)}) %all-to-all-start) | async-done | bytes 262176 | tf_op jit(solution)/shard_map/all_to_all | solution.py:268
  15.0 14.8 %collective-permute-start = (bf16[4,32,512]{2,1,0:T(8,128)(2,1)S(1)}, bf16[4,32,512]{2,1,0:T(8,128)(2,1)S(1)}, u32[]{:S(2)}, u32[]{:S(2)}) collective-permute-start(bf16[4,32,512]{2,1,0:T(8,128)(2,1)S(1)} %slice.31.here_ref), channel_id=1, source_target_pairs={{0,32},{32,0},{1,33},{33,1},{2,34},{34,2},{3,35},{35,3},{4,36},{36... | collective-permute-start | bytes 393224 | tf_op jit(solution)/shard_map/ppermute | solution.py:272
  29.9 0.7 concatenate.3.info_ref
  30.6 0.0 copy-start
  30.6 0.0 collective-permute-done.2.far_ref
  30.6 0.0 copy-start.3
  30.6 0.0 collective-permute-done.1.near_ref
  30.6 0.0 copy-start.4
  30.6 9.1 %collective-permute-done.there_ref = bf16[4,32,512]{2,1,0:T(8,128)(2,1)S(1)} collective-permute-done((bf16[4,32,512]{2,1,0:T(8,128)(2,1)S(1)}, bf16[4,32,512]{2,1,0:T(8,128)(2,1)S(1)}, u32[]{:S(2)}, u32[]{:S(2)}) %collective-permute-start) | collective-permute-done | bytes 131104 | tf_op jit(solution)/shard_map/ppermute | solution.py:272
  39.8 0.8 shard_map.93
  40.6 17.4 %all_to_all.20 = bf16[16,32,512]{2,1,0:T(8,128)(2,1)S(1)} all-to-all(bf16[16,32,512]{2,1,0:T(8,128)(2,1)S(1)} %shard_map.93), channel_id=1, replica_groups=mesh['dp'=8,'z'=2,'y'=4,'b'=2,'x'=2,'core'=2] {'x','y','b'}, dimensions={0} | all-to-all | bytes 1048576 | tf_op jit(solution)/shard_map/all_to_all | solution.py:268
  58.0 0.0 copy-start.2
  58.0 1.3 collective-permute-start.3
  59.3 2.1 %collective-permute-done.3.before_ref = bf16[2,128,512]{2,1,0:T(8,128)(2,1)S(1)} collective-permute-done((bf16[2,128,512]{2,1,0:T(8,128)(2,1)S(1)}, bf16[2,128,512]{2,1,0:T(8,128)(2,1)S(1)}, u32[]{:S(2)}, u32[]{:S(2)}) %collective-permute-start.3) | collective-permute-done | bytes 262176 | tf_op jit(solution)/shard_map/ppermute | solution.py:264
  61.5 0.0 copy-start.5
  61.5 0.0 copy-done
  61.5 0.0 copy-done.3
  61.5 0.0 copy-done.4
  61.5 0.0 copy-done.2
  61.5 0.7 copy-done.5
  62.2 9.4 %shard_map.94 = (bf16[384,4096]{1,0:T(8,128)(2,1)}, bf16[384,4096]{1,0:T(8,128)(2,1)}, bf16[2,128,512]{2,1,0:T(8,128)(2,1)}, bf16[2,128,512]{2,1,0:T(8,128)(2,1)}) custom-call(s32[20]{0:T(128)} %copy-done, s32[64,128]{1,0:T(8,128)} %bitcast.41, bf16[128,4096]{1,0:T(8,128)(2,1)} %query_ref.3, bf16[128,4096]{1,0:T(8,128)(2,1)} %grad_ref.3, ...), custom_call_target="tpu_custom_call" | custom-call | flops 1409286144 | bytes 8388608 | tf_op jit(solution)/shard_map/pallas_call | solution.py:161
  71.5 2.0 %collective-permute-start.4 = (bf16[2,128,512]{2,1,0:T(8,128)(2,1)}, bf16[2,128,512]{2,1,0:T(8,128)(2,1)S(1)}, u32[]{:S(2)}, u32[]{:S(2)}) collective-permute-start(bf16[2,128,512]{2,1,0:T(8,128)(2,1)} %get-tuple-element.25), channel_id=1, source_target_pairs={{0,1},{4,5},{8,9},{12,13},{16,17},{20,21},{24,25},{28,29},{32,33},... | collective-permute-start | bytes 786440 | tf_op jit(solution)/shard_map/ppermute | solution.py:264
  73.6 1.3 %collective-permute-done.4 = bf16[2,128,512]{2,1,0:T(8,128)(2,1)S(1)} collective-permute-done((bf16[2,128,512]{2,1,0:T(8,128)(2,1)}, bf16[2,128,512]{2,1,0:T(8,128)(2,1)S(1)}, u32[]{:S(2)}, u32[]{:S(2)}) %collective-permute-start.4) | collective-permute-done | bytes 262176 | tf_op jit(solution)/shard_map/ppermute | solution.py:264
  74.9 1.0 add_convert_fusion
  75.9 0.8 broadcast_in_dim.15
  76.8 3.6 %all-to-all-start.2 = ((bf16[16,32,512]{2,1,0:T(8,128)(2,1)}), bf16[16,32,512]{2,1,0:T(8,128)(2,1)S(1)}, u32[]{:S(2)}, u32[]{:S(2)}) async-start(bf16[16,32,512]{2,1,0:T(8,128)(2,1)} %bitcast.11), calls=%async_computation.2 | async-start | bytes 1048576 | tf_op jit(solution)/shard_map/all_to_all | solution.py:268
  80.4 0.0 copy-start.1
  80.4 1.3 collective-permute-start.6
  81.7 1.3 collective-permute-start.5
  83.0 7.5 %shard_map.95 = (bf16[128,4096]{1,0:T(8,128)(2,1)}, bf16[128,4096]{1,0:T(8,128)(2,1)}, f32[2,128,512]{2,1,0:T(8,128)}) custom-call(s32[20]{0:T(128)} %copy-done, bf16[128,4096]{1,0:T(8,128)(2,1)} %query_ref.3, bf16[128,4096]{1,0:T(8,128)(2,1)} %grad_ref.3, bf16[2,128,512]{2,1,0:T(8,128)(2,1)} %bitcast.35, bf16[2,128,512]{2,1,0:T(8,128)(2,1)} %copy-done.5, ...), custom_call_target="tpu_custom_call" | custom-call | flops 1006632960 | bytes 10485760 | tf_op jit(solution)/shard_map/pallas_call | solution.py:184
  90.4 1.6 %all-to-all-done.2.held_ref = bf16[16,32,512]{2,1,0:T(8,128)(2,1)S(1)} async-done(((bf16[16,32,512]{2,1,0:T(8,128)(2,1)}), bf16[16,32,512]{2,1,0:T(8,128)(2,1)S(1)}, u32[]{:S(2)}, u32[]{:S(2)}) %all-to-all-start.2) | async-done | bytes 524320 | tf_op jit(solution)/shard_map/all_to_all | solution.py:268
  92.0 0.0 copy-done.1
  92.0 0.7 shard_map.96
  92.8 12.0 %collective-permute-start.7 = (bf16[4,32,512]{2,1,0:T(8,128)(2,1)S(1)}, bf16[4,32,512]{2,1,0:T(8,128)(2,1)S(1)}, u32[]{:S(2)}, u32[]{:S(2)}) collective-permute-start(bf16[4,32,512]{2,1,0:T(8,128)(2,1)S(1)} %get-tuple-element.37), channel_id=1, source_target_pairs={{0,32},{32,0},{1,33},{33,1},{2,34},{34,2},{3,35},{35,3},{4,36},{36... | collective-permute-start | bytes 393224 | tf_op jit(solution)/shard_map/ppermute | solution.py:272
  104.8 10.6 %collective-permute-done.7 = bf16[4,32,512]{2,1,0:T(8,128)(2,1)S(1)} collective-permute-done((bf16[4,32,512]{2,1,0:T(8,128)(2,1)S(1)}, bf16[4,32,512]{2,1,0:T(8,128)(2,1)S(1)}, u32[]{:S(2)}, u32[]{:S(2)}) %collective-permute-start.7) | collective-permute-done | bytes 131104 | tf_op jit(solution)/shard_map/ppermute | solution.py:272
  115.4 0.7 broadcast_in_dim.16
  116.2 6.7 %all-to-all-start.3 = ((bf16[8,32,512]{2,1,0:T(8,128)(2,1)}), bf16[8,32,512]{2,1,0:T(8,128)(2,1)S(1)}, u32[]{:S(2)}, u32[]{:S(2)}) async-start(bf16[8,32,512]{2,1,0:T(8,128)(2,1)} %bitcast.12), calls=%async_computation.3 | async-start | bytes 524288 | tf_op jit(solution)/shard_map/all_to_all | solution.py:268
  122.9 0.0 collective-permute-done.6
  122.9 0.0 collective-permute-done.5
  122.9 1.1 convert_add_fusion
  124.1 6.2 %all-to-all-done.3 = bf16[8,32,512]{2,1,0:T(8,128)(2,1)S(1)} async-done(((bf16[8,32,512]{2,1,0:T(8,128)(2,1)}), bf16[8,32,512]{2,1,0:T(8,128)(2,1)S(1)}, u32[]{:S(2)}, u32[]{:S(2)}) %all-to-all-start.3) | async-done | bytes 262176 | tf_op jit(solution)/shard_map/all_to_all | solution.py:268
  130.4 0.8 fusion.4
  (5 shorter events, 0.1 us)
Async XLA Ops:
  2.4 12.6 %all-to-all-start = ((bf16[8,32,512]{2,1,0:T(8,128)(2,1)}), bf16[8,32,512]{2,1,0:T(8,128)(2,1)S(1)}, u32[]{:S(2)}, u32[]{:S(2)}) async-start(bf16[8,32,512]{2,1,0:T(8,128)(2,1)} %bitcast.6), calls=%async_computation | async-start | bytes 524288 | tf_op jit(solution)/shard_map/all_to_all | solution.py:268
  7.8 22.8 %collective-permute-start.2 = (bf16[2,128,512]{2,1,0:T(8,128)(2,1)}, bf16[2,128,512]{2,1,0:T(8,128)(2,1)S(1)}, u32[]{:S(2)}, u32[]{:S(2)}) collective-permute-start(bf16[2,128,512]{2,1,0:T(8,128)(2,1)} %pad_maximum_fusion.own_ref), channel_id=1, source_target_pairs={{0,2},{1,3},{4,6},{5,7},{8,10},{9,11},{12,14},{13,15},{16,18},{17,... | collective-permute-start | bytes 786440 | tf_op jit(solution)/shard_map/ppermute | solution.py:264
  11.7 18.9 %collective-permute-start.1 = (bf16[2,128,512]{2,1,0:T(8,128)(2,1)}, bf16[2,128,512]{2,1,0:T(8,128)(2,1)S(1)}, u32[]{:S(2)}, u32[]{:S(2)}) collective-permute-start(bf16[2,128,512]{2,1,0:T(8,128)(2,1)} %pad_maximum_fusion.own_ref), channel_id=1, source_target_pairs={{0,1},{1,2},{2,3},{4,5},{5,6},{6,7},{8,9},{9,10},{10,11},{12,13},{... | collective-permute-start | bytes 786440 | tf_op jit(solution)/shard_map/ppermute | solution.py:264
  15.0 24.7 %collective-permute-start = (bf16[4,32,512]{2,1,0:T(8,128)(2,1)S(1)}, bf16[4,32,512]{2,1,0:T(8,128)(2,1)S(1)}, u32[]{:S(2)}, u32[]{:S(2)}) collective-permute-start(bf16[4,32,512]{2,1,0:T(8,128)(2,1)S(1)} %slice.31.here_ref), channel_id=1, source_target_pairs={{0,32},{32,0},{1,33},{33,1},{2,34},{34,2},{3,35},{35,3},{4,36},{36... | collective-permute-start | bytes 393224 | tf_op jit(solution)/shard_map/ppermute | solution.py:272
  30.6 30.9 %copy-start = (s32[20]{0:T(128)}, s32[20]{0:T(128)S(1)}, u32[]{:S(2)}) copy-start(s32[20]{0:T(128)S(1)} %concatenate.3.info_ref) | copy-start | bytes 244
  30.6 30.9 %copy-start.3 = (bf16[2,128,512]{2,1,0:T(8,128)(2,1)}, bf16[2,128,512]{2,1,0:T(8,128)(2,1)S(1)}, u32[]{:S(2)}) copy-start(bf16[2,128,512]{2,1,0:T(8,128)(2,1)S(1)} %collective-permute-done.2.far_ref) | copy-start | bytes 786436
  30.6 30.8 %copy-start.4 = (bf16[2,128,512]{2,1,0:T(8,128)(2,1)}, bf16[2,128,512]{2,1,0:T(8,128)(2,1)S(1)}, u32[]{:S(2)}) copy-start(bf16[2,128,512]{2,1,0:T(8,128)(2,1)S(1)} %collective-permute-done.1.near_ref) | copy-start | bytes 786436
  58.0 3.5 %copy-start.2 = (bf16[2,4,1,32,512]{4,3,1,0,2:T(8,128)(2,1)}, bf16[2,4,1,32,512]{4,3,1,0,2:T(8,128)(2,1)S(1)}, u32[]{:S(2)}) copy-start(bf16[2,4,1,32,512]{4,3,1,0,2:T(8,128)(2,1)S(1)} %fusion.2) | copy-start | bytes 786436
  58.0 3.4 %collective-permute-start.3 = (bf16[2,128,512]{2,1,0:T(8,128)(2,1)S(1)}, bf16[2,128,512]{2,1,0:T(8,128)(2,1)S(1)}, u32[]{:S(2)}, u32[]{:S(2)}) collective-permute-start(bf16[2,128,512]{2,1,0:T(8,128)(2,1)S(1)} %bitcast.33), channel_id=1, source_target_pairs={{1,0},{5,4},{9,8},{13,12},{17,16},{21,20},{25,24},{29,28},{33,32},... | collective-permute-start | bytes 786440 | tf_op jit(solution)/shard_map/ppermute | solution.py:264
  61.5 0.7 copy-start.5
  71.5 3.4 %collective-permute-start.4 = (bf16[2,128,512]{2,1,0:T(8,128)(2,1)}, bf16[2,128,512]{2,1,0:T(8,128)(2,1)S(1)}, u32[]{:S(2)}, u32[]{:S(2)}) collective-permute-start(bf16[2,128,512]{2,1,0:T(8,128)(2,1)} %get-tuple-element.25), channel_id=1, source_target_pairs={{0,1},{4,5},{8,9},{12,13},{16,17},{20,21},{24,25},{28,29},{32,33},... | collective-permute-start | bytes 786440 | tf_op jit(solution)/shard_map/ppermute | solution.py:264
  76.8 15.2 %all-to-all-start.2 = ((bf16[16,32,512]{2,1,0:T(8,128)(2,1)}), bf16[16,32,512]{2,1,0:T(8,128)(2,1)S(1)}, u32[]{:S(2)}, u32[]{:S(2)}) async-start(bf16[16,32,512]{2,1,0:T(8,128)(2,1)} %bitcast.11), calls=%async_computation.2 | async-start | bytes 1048576 | tf_op jit(solution)/shard_map/all_to_all | solution.py:268
  80.4 11.7 %copy-start.1 = (s32[20]{0:T(128)S(1)}, s32[20]{0:T(128)}, u32[]{:S(2)}) copy-start(s32[20]{0:T(128)} %copy-done) | copy-start | bytes 244
  80.4 42.5 %collective-permute-start.6 = (bf16[2,128,512]{2,1,0:T(8,128)(2,1)}, bf16[2,128,512]{2,1,0:T(8,128)(2,1)S(1)}, u32[]{:S(2)}, u32[]{:S(2)}) collective-permute-start(bf16[2,128,512]{2,1,0:T(8,128)(2,1)} %get-tuple-element.24), channel_id=1, source_target_pairs={{2,0},{3,1},{6,4},{7,5},{10,8},{11,9},{14,12},{15,13},{18,16},{19,... | collective-permute-start | bytes 786440 | tf_op jit(solution)/shard_map/ppermute | solution.py:264
  81.7 41.2 %collective-permute-start.5 = (bf16[2,128,512]{2,1,0:T(8,128)(2,1)}, bf16[2,128,512]{2,1,0:T(8,128)(2,1)S(1)}, u32[]{:S(2)}, u32[]{:S(2)}) collective-permute-start(bf16[2,128,512]{2,1,0:T(8,128)(2,1)} %get-tuple-element.25), channel_id=1, source_target_pairs={{1,0},{2,1},{3,2},{5,4},{6,5},{7,6},{9,8},{10,9},{11,10},{13,12},{... | collective-permute-start | bytes 786440 | tf_op jit(solution)/shard_map/ppermute | solution.py:264
  92.8 22.6 %collective-permute-start.7 = (bf16[4,32,512]{2,1,0:T(8,128)(2,1)S(1)}, bf16[4,32,512]{2,1,0:T(8,128)(2,1)S(1)}, u32[]{:S(2)}, u32[]{:S(2)}) collective-permute-start(bf16[4,32,512]{2,1,0:T(8,128)(2,1)S(1)} %get-tuple-element.37), channel_id=1, source_target_pairs={{0,32},{32,0},{1,33},{33,1},{2,34},{34,2},{3,35},{35,3},{4,36},{36... | collective-permute-start | bytes 393224 | tf_op jit(solution)/shard_map/ppermute | solution.py:272
  116.2 14.1 %all-to-all-start.3 = ((bf16[8,32,512]{2,1,0:T(8,128)(2,1)}), bf16[8,32,512]{2,1,0:T(8,128)(2,1)S(1)}, u32[]{:S(2)}, u32[]{:S(2)}) async-start(bf16[8,32,512]{2,1,0:T(8,128)(2,1)} %bitcast.12), calls=%async_computation.3 | async-start | bytes 524288 | tf_op jit(solution)/shard_map/all_to_all | solution.py:268

commit v7 on v6

--- a/solution.py
+++ b/solution.py
@@ -18,6 +18,7 @@
 BLOCK_AXES = ("x", "core")
 SPREAD_AXES = ("x", "y")
 PLANE_AXES = ("x", "y", "b")
+SCALE = 1.0 / math.sqrt(HEAD_SIZE)
 COUNT = 16
 
 
@@ -79,7 +80,6 @@
     def _():
         usable_bias(info_ref[info_ref[COUNT + 2]] * 4 + info_ref[COUNT + 3], segments_ref, bias_ref)
 
-    scale = 1.0 / math.sqrt(HEAD_SIZE)
     values, keys = window(info_ref, cross_ref, before_ref, far_ref, near_ref, own_ref)
     width = 2 * CHUNK
     pairs = GROUP // 2
@@ -98,52 +98,35 @@
             ahead = products(pair + 1)
         scores = scores + bias_ref[...]
         top = jnp.max(scores, axis=0, keepdims=True)
-        raised = jnp.exp2((scores - top) * (scale * math.log2(math.e)))
+        raised = jnp.exp2((scores - top) * (SCALE * math.log2(math.e)))
         share = 1.0 / jnp.sum(raised, axis=0, keepdims=True)
         delta = jnp.sum(raised * dprob, axis=0, keepdims=True) * share
+        weights = raised * share
         columns = pl.ds(pair * width, width)
-        weight_ref[:, columns] = (raised * share).astype(jnp.bfloat16)
-        dscore_ref[:, columns] = (raised * (share * scale) * (dprob - delta)).astype(jnp.bfloat16)
+        weight_ref[:, columns] = weights.astype(jnp.bfloat16)
+        dscore_ref[:, columns] = (weights * (dprob - delta)).astype(jnp.bfloat16)
     every = range(GROUP)
     halo = pl.ds(0, 2 * CHUNK)
-    grad_keys = dot(dscore_ref[halo, :], stacked(query_ref, every), PLAIN).astype(jnp.bfloat16)
+    grad_keys = (dot(dscore_ref[halo, :], stacked(query_ref, every), PLAIN) * SCALE).astype(jnp.bfloat16)
     grad_values = dot(weight_ref[halo, :], stacked(grad_ref, every), PLAIN).astype(jnp.bfloat16)
     for i, total in enumerate((grad_values, grad_keys)):
         far_grad_ref[i] = total[:CHUNK]
         near_grad_ref[i] = total[CHUNK:]
 
 
-def output_kernel(
-    info_ref,
-    query_ref,
-    grad_ref,
-    cross_ref,
-    before_ref,
-    far_ref,
-    near_ref,
-    own_ref,
-    weight_ref,
-    dscore_ref,
-    out_ref,
-    grad_query_ref,
-    own_grad_ref,
-):
-    values, keys = window(info_ref, cross_ref, before_ref, far_ref, near_ref, own_ref)
-    values_t, keys_t = values.T, keys.T
+def product_kernel(which, info_ref, row_ref, *refs):
+    *pair_refs, factor_ref, out_ref, own_grad_ref = refs
+    window_t = window(info_ref, *pair_refs)[which].T
+    factor = (1.0, SCALE)[which]
     width = 2 * CHUNK
     for pair in range(GROUP // 2):
         columns = pl.ds(pair * width, width)
-        output_t = dot(values_t, weight_ref[:, columns], PLAIN).astype(jnp.bfloat16)
-        grad_query_t = dot(keys_t, dscore_ref[:, columns], PLAIN).astype(jnp.bfloat16)
+        rows_t = (dot(window_t, factor_ref[:, columns], PLAIN) * factor).astype(jnp.bfloat16)
         for i in range(2):
             columns = pl.ds(pair * width + i * CHUNK, CHUNK)
-            part = slice(i * CHUNK, (i + 1) * CHUNK)
-            out_ref[:, columns] = output_t[:, part].T
-            grad_query_ref[:, columns] = grad_query_t[:, part].T
-    every = range(GROUP)
-    own = pl.ds(2 * CHUNK, CHUNK)
-    own_grad_ref[0] = dot(weight_ref[own, :], stacked(grad_ref, every), PLAIN)
-    own_grad_ref[1] = dot(dscore_ref[own, :], stacked(query_ref, every), PLAIN)
+            out_ref[:, columns] = rows_t[:, i * CHUNK : (i + 1) * CHUNK].T
+    own = factor_ref[pl.ds(2 * CHUNK, CHUNK), :]
+    own_grad_ref[...] = dot(own, stacked(row_ref, range(GROUP)), PLAIN) * factor
 
 
 def attention_specs(rows):
@@ -177,26 +160,72 @@
     )(info, segments, queries, grads, *pairs)
 
 
-def outputs_and_own(info, queries, grads, pairs, weights, dscores):
-    rows = queries.shape[0]
+def output_and_own(which, info, rows_in, pairs, factors):
+    rows = rows_in.shape[0]
     wide, pair, tall = attention_specs(rows)
-    like = jax.ShapeDtypeStruct(queries.shape, jnp.bfloat16)
-    return pl.pallas_call(
-        output_kernel,
+    narrow = pl.BlockSpec((rows, HEAD_SIZE), lambda g, *_: (0, g))
+    return pl.pallas_call(
+        functools.partial(product_kernel, which),
         grid_spec=pltpu.PrefetchScalarGridSpec(
             num_scalar_prefetch=1,
             grid=(KEY_VALUE_HEADS,),
-            in_specs=[wide, wide] + [pair] * 5 + [tall, tall],
-            out_specs=[wide, wide, pair],
+            in_specs=[wide] + [pair] * 5 + [tall],
+            out_specs=[wide, narrow],
         ),
-        out_shape=[like, like, jax.ShapeDtypeStruct((2, rows, KV_WIDTH), jnp.float32)],
+        out_shape=[
+            jax.ShapeDtypeStruct(rows_in.shape, jnp.bfloat16),
+            jax.ShapeDtypeStruct((rows, KV_WIDTH), jnp.float32),
+        ],
         compiler_params=pltpu.CompilerParams(vmem_limit_bytes=58 * 1024 * 1024),
         cost_estimate=pl.CostEstimate(
-            flops=5 * rows * QUERY_HEADS * WINDOW * HEAD_SIZE,
-            bytes_accessed=20 * rows * QUERY_HEADS * HEAD_SIZE,
+            flops=5 * rows * QUERY_HEADS * WINDOW * HEAD_SIZE // 2,
+            bytes_accessed=10 * rows * QUERY_HEADS * HEAD_SIZE,
             transcendentals=0,
         ),
-    )(info, queries, grads, *pairs, weights, dscores)
+    )(info, rows_in, *pairs, factors)
+
+
+def pair_kernel(values_ref, keys_ref, out_ref, sems):
+    copies = [
+        pltpu.make_async_copy(ref, out_ref.at[i], sems.at[i])
+        for i, ref in enumerate((values_ref, keys_ref))
+    ]
+    for copy in copies:
+        copy.start()
+    for copy in copies:
+        copy.wait()
+
+
+def paired(values, keys):
+    return pl.pallas_call(
+        pair_kernel,
+        in_specs=[pl.BlockSpec(memory_space=pl.ANY)] * 2,
+        out_specs=pl.BlockSpec(memory_space=pltpu.VMEM),
+        out_shape=jax.ShapeDtypeStruct((2, *values.shape), values.dtype),
+        scratch_shapes=[pltpu.SemaphoreType.DMA((2,))],
+        compiler_params=pltpu.CompilerParams(vmem_limit_bytes=4 * 1024 * 1024),
+    )(values, keys)
+
+
+def join_kernel(far_ref, before_ref, out_ref):
+    rows = CHUNK // 4
+    for i in range(2):
+        for y in range(4):
+            part = pl.ds(y * rows, rows)
+            total = far_ref[i, part, :].astype(jnp.float32) + before_ref[i, part, :].astype(jnp.float32)
+            for b in range(2):
+                out_ref[8 * i + 2 * y + b] = total.astype(jnp.bfloat16)
+
+
+def joined(far_grad, before):
+    in_vmem = pl.BlockSpec(memory_space=pltpu.VMEM)
+    return pl.pallas_call(
+        join_kernel,
+        in_specs=[in_vmem] * 2,
+        out_specs=in_vmem,
+        out_shape=jax.ShapeDtypeStruct((16, CHUNK // 4, KV_WIDTH), jnp.bfloat16),
+        compiler_params=pltpu.CompilerParams(vmem_limit_bytes=4 * 1024 * 1024),
+    )(far_grad, before)
 
 
 def slots_in_order(info_ref, slot_ref):
@@ -280,7 +309,7 @@
     info = jnp.concatenate([order, jnp.stack(place).astype(jnp.int32)])
     part = (4, CHUNK // 4, KV_WIDTH)
     whole = (CHUNK, KV_WIDTH)
-    own = jnp.stack([values, keys], axis=0)
+    own = paired(values, keys)
 
     here = exchange(own.reshape(8, *part[1:]), SPREAD_AXES).reshape(2, *part)[1]
     there = across(here)
@@ -297,23 +326,24 @@
     )
 
     before = move(near_grad, [(0, 1)])
-    halo = (far_grad.astype(jnp.float32) + before.astype(jnp.float32)).astype(jnp.bfloat16)
-    pieces = jnp.broadcast_to(halo.reshape(2, 4, 1, *part[1:]), (2, 4, 2, *part[1:]))
-    pieces, weights, dscores = lax.optimization_barrier((pieces, weights, dscores))
-    held = exchange(pieces.reshape(16, *part[1:]), PLANE_AXES)
-    attended, grad_query, own_grad = outputs_and_own(info, queries, grads, pairs, weights, dscores)
-    held, own_grad = lax.optimization_barrier((held, own_grad))
+    pieces = joined(far_grad, before)
+    pieces, weights = lax.optimization_barrier((pieces, weights))
+    held = exchange(pieces, PLANE_AXES)
+    attended, own_values = output_and_own(0, info, grads, pairs, weights)
+    held, own_values = lax.optimization_barrier((held, own_values))
     here, there = route(route_back_kernel, info, (held,), (4, 4))
+    there, dscores = lax.optimization_barrier((there, dscores))
     there = across(there)
+    grad_query, own_keys = output_and_own(1, info, queries, pairs, dscores)
     near_back = move(near_grad, [(1, 0), (2, 1), (3, 2)])
     far_back = move(far_grad, [(2, 0), (3, 1)])
     pieces = jnp.broadcast_to(here + there, (2, *part)).reshape(8, *part[1:])
     late = exchange(pieces, SPREAD_AXES).reshape(2, *whole)
     late = jnp.where(c >= 2, late, 0)
 
-    total = own_grad + near_back.astype(jnp.float32) + far_back.astype(jnp.float32)
-    value_gradient = total[0] + late[0].astype(jnp.float32)
-    key_gradient = total[1] + late[1].astype(jnp.float32)
+    early = near_back.astype(jnp.float32) + far_back.astype(jnp.float32)
+    value_gradient = own_values + early[0] + late[0].astype(jnp.float32)
+    key_gradient = own_keys + early[1] + late[1].astype(jnp.float32)
     return (
         attended,
         grad_query,

time: 132 us -> 133 us (level)
  Pallas kernels: 18.4 us -> 25.2 us
  waiting for transfers between devices: 33 us -> 29 us
  other arithmetic: 4.78 us -> 1.95 us
  local copies, waits for them, and re-layouts: 3.06 us -> 4.95 us
    pallas_call x1 -> x4, Pallas kernels: 7.47 us -> 13.6 us  [the longest x2 11.7 us: output_and_own(): pl.pallas_call(functools.partial(product_kernel, which), grid_spec=pltpu....]
    all_to_all x3, waiting for transfers between devices: 9.79 us -> 6.63 us  [exchange(): return lax.all_to_all(pieces, axes, 0, 0)]
    unnamed x12 -> x20, local copies, waits for them, and re-layouts: 0.71 us -> 3.46 us
    another operation x1 -> x0, other arithmetic: 1.76 us -> none  [local(): own = jnp.stack([values, keys], axis=0)]
  transfers between devices with their start and end apart: 11 -> 11, of which waited for: 7 -> 7; matrix products, arithmetic and copies ran while one was open for 2% -> 1% of each run, Pallas kernels for 6% -> 9%
where the time goes in v7:
time: 133 us; the launch traced here: 132 us
  starting transfers between devices  53 us (40%)
  waiting for transfers between devices  29 us (22%)
  Pallas kernels  25.2 us (19%)
  blocking collectives  17.4 us (13%)
  local copies, waits for them, and re-layouts  4.95 us (4%)
  other arithmetic  1.95 us (1%)
    ppermute x2, starting transfers between devices, across(): return lax.ppermute(value, 'z', [(0, 1), (1, 0)])  26.8 us
    ppermute x2, waiting for transfers between devices, across(): return lax.ppermute(value, 'z', [(0, 1), (1, 0)])  18.9 us
    all_to_all x1, blocking collectives, exchange(): return lax.all_to_all(pieces, axes, 0, 0)  17.4 us
    all_to_all x3, starting transfers between devices, exchange(): return lax.all_to_all(pieces, axes, 0, 0)  15 us
    pallas_call x2, Pallas kernels, output_and_own(): pl.pallas_call(functools.partial(product_kernel, which), grid_spec=pltpu....  11.7 us
    ppermute x6, starting transfers between devices, move(): return lax.ppermute(value, BLOCK_AXES, moves)  11.2 us
    pallas_call x1, Pallas kernels, scores_and_halo(): pl.pallas_call(score_kernel, grid_spec=pltpu.PrefetchScalarGridSpec(num_s...  10.1 us
    all_to_all x3, waiting for transfers between devices, exchange(): return lax.all_to_all(pieces, axes, 0, 0)  6.63 us
  transfers between devices with their start and end apart: 11, of which 7 were waited for; matrix products, arithmetic and copies ran while one was open for 1% of the time, Pallas kernels for 9%

profile of v7, /device:TPU:32, one launch (start us, length us, event | category | flops | bytes accessed | tf_op | source)
XLA Modules:
  0.0 132.4 jit_solution(10754003363533448602)
XLA Ops:
  0.6 0.0 copy-start.1
  0.6 0.9 copy-done.1
  1.5 0.9 copy-done.2
  2.4 1.0 shard_map.93.own_ref.refs_4_
  3.5 5.4 %all-to-all-start = ((bf16[8,32,512]{2,1,0:T(8,128)(2,1)}), bf16[8,32,512]{2,1,0:T(8,128)(2,1)S(1)}, u32[]{:S(2)}, u32[]{:S(2)}) async-start(bf16[8,32,512]{2,1,0:T(8,128)(2,1)} %bitcast.4), calls=%async_computation | async-start | bytes 524288 | tf_op jit(solution)/shard_map/all_to_all | solution.py:297
  8.9 3.9 %collective-permute-start.2 = (bf16[2,128,512]{2,1,0:T(8,128)(2,1)}, bf16[2,128,512]{2,1,0:T(8,128)(2,1)S(1)}, u32[]{:S(2)}, u32[]{:S(2)}) collective-permute-start(bf16[2,128,512]{2,1,0:T(8,128)(2,1)} %shard_map.93.own_ref.refs_4_), channel_id=1, source_target_pairs={{0,2},{1,3},{4,6},{5,7},{8,10},{9,11},{12,14},{13,15},{16,18},{17,... | collective-permute-start | bytes 786440 | tf_op jit(solution)/shard_map/ppermute | solution.py:293
  12.8 1.3 collective-permute-start.1
  14.1 2.0 %all-to-all-done = bf16[8,32,512]{2,1,0:T(8,128)(2,1)S(1)} async-done(((bf16[8,32,512]{2,1,0:T(8,128)(2,1)}), bf16[8,32,512]{2,1,0:T(8,128)(2,1)S(1)}, u32[]{:S(2)}, u32[]{:S(2)}) %all-to-all-start) | async-done | bytes 262176 | tf_op jit(solution)/shard_map/all_to_all | solution.py:297
  16.1 14.8 %collective-permute-start = (bf16[4,32,512]{2,1,0:T(8,128)(2,1)S(1)}, bf16[4,32,512]{2,1,0:T(8,128)(2,1)S(1)}, u32[]{:S(2)}, u32[]{:S(2)}) collective-permute-start(bf16[4,32,512]{2,1,0:T(8,128)(2,1)S(1)} %slice.31.here_ref), channel_id=1, source_target_pairs={{0,32},{32,0},{1,33},{33,1},{2,34},{34,2},{3,35},{35,3},{4,36},{36... | collective-permute-start | bytes 393224 | tf_op jit(solution)/shard_map/ppermute | solution.py:301
  31.0 0.7 concatenate.3.info_ref
  31.7 0.0 collective-permute-done.2.far_ref.refs_2_
  31.7 0.0 collective-permute-done.1.near_ref.refs_3_
  31.7 0.0 copy-start.7
  31.7 9.1 %collective-permute-done.there_ref = bf16[4,32,512]{2,1,0:T(8,128)(2,1)S(1)} collective-permute-done((bf16[4,32,512]{2,1,0:T(8,128)(2,1)S(1)}, bf16[4,32,512]{2,1,0:T(8,128)(2,1)S(1)}, u32[]{:S(2)}, u32[]{:S(2)}) %collective-permute-start) | collective-permute-done | bytes 131104 | tf_op jit(solution)/shard_map/ppermute | solution.py:301
  40.9 0.8 shard_map.94
  41.7 17.4 %all_to_all.20 = bf16[16,32,512]{2,1,0:T(8,128)(2,1)S(1)} all-to-all(bf16[16,32,512]{2,1,0:T(8,128)(2,1)S(1)} %shard_map.94), channel_id=1, replica_groups=mesh['dp'=8,'z'=2,'y'=4,'b'=2,'x'=2,'core'=2] {'x','y','b'}, dimensions={0} | all-to-all | bytes 1048576 | tf_op jit(solution)/shard_map/all_to_all | solution.py:297
  59.1 0.0 copy-start.5
  59.1 1.3 collective-permute-start.3
  60.4 2.1 %collective-permute-done.3.before_ref.refs_1_ = bf16[2,128,512]{2,1,0:T(8,128)(2,1)S(1)} collective-permute-done((bf16[2,128,512]{2,1,0:T(8,128)(2,1)S(1)}, bf16[2,128,512]{2,1,0:T(8,128)(2,1)S(1)}, u32[]{:S(2)}, u32[]{:S(2)}) %collective-permute-start.3) | collective-permute-done | bytes 262176 | tf_op jit(solution)/shard_map/ppermute | solution.py:293
  62.6 0.0 copy-done.3
  62.6 0.0 copy-done.6
  62.6 0.0 copy-done.7
  62.6 0.0 copy-done.5
  62.6 0.7 copy-done.8
  63.3 10.1 %shard_map.95 = (bf16[384,4096]{1,0:T(8,128)(2,1)}, bf16[384,4096]{1,0:T(8,128)(2,1)}, bf16[2,128,512]{2,1,0:T(8,128)(2,1)}, bf16[2,128,512]{2,1,0:T(8,128)(2,1)}) custom-call(s32[20]{0:T(128)} %copy-done.3, s32[64,128]{1,0:T(8,128)} %bitcast.44, bf16[128,4096]{1,0:T(8,128)(2,1)} %row_ref.3, bf16[128,4096]{1,0:T(8,128)(2,1)} %row_ref.2, ...), custom_call_target="tpu_custom_call" | custom-call | flops 1409286144 | bytes 8388608 | tf_op jit(solution)/shard_map/pallas_call | solution.py:144
  73.4 2.0 %collective-permute-start.4 = (bf16[2,128,512]{2,1,0:T(8,128)(2,1)}, bf16[2,128,512]{2,1,0:T(8,128)(2,1)S(1)}, u32[]{:S(2)}, u32[]{:S(2)}) collective-permute-start(bf16[2,128,512]{2,1,0:T(8,128)(2,1)} %get-tuple-element.27), channel_id=1, source_target_pairs={{0,1},{4,5},{8,9},{12,13},{16,17},{20,21},{24,25},{28,29},{32,33},... | collective-permute-start | bytes 786440 | tf_op jit(solution)/shard_map/ppermute | solution.py:293
  75.4 1.3 %collective-permute-done.4.before_ref = bf16[2,128,512]{2,1,0:T(8,128)(2,1)S(1)} collective-permute-done((bf16[2,128,512]{2,1,0:T(8,128)(2,1)}, bf16[2,128,512]{2,1,0:T(8,128)(2,1)S(1)}, u32[]{:S(2)}, u32[]{:S(2)}) %collective-permute-start.4) | collective-permute-done | bytes 262176 | tf_op jit(solution)/shard_map/ppermute | solution.py:293
  76.8 0.9 copy-done
  77.7 0.9 shard_map.96
  78.6 3.7 %all-to-all-start.2 = ((bf16[16,32,512]{2,1,0:T(8,128)(2,1)}), bf16[16,32,512]{2,1,0:T(8,128)(2,1)S(1)}, u32[]{:S(2)}, u32[]{:S(2)}) async-start(bf16[16,32,512]{2,1,0:T(8,128)(2,1)} %shard_map.96), calls=%async_computation.2 | async-start | bytes 1048576 | tf_op jit(solution)/shard_map/all_to_all | solution.py:297
  82.3 1.3 collective-permute-start.6
  83.6 1.3 collective-permute-start.5
  84.9 5.8 %shard_map.97 = (bf16[128,4096]{1,0:T(8,128)(2,1)}, f32[128,512]{1,0:T(8,128)}) custom-call(s32[20]{0:T(128)} %copy-done.3, bf16[128,4096]{1,0:T(8,128)(2,1)} %row_ref.2, bf16[2,128,512]{2,1,0:T(8,128)(2,1)} %bitcast.41, bf16[2,128,512]{2,1,0:T(8,128)(2,1)} %copy-done.8, bf16[2,128,512]{2,1,0:T(8,128)(2,1)} %copy-done.6, bf16[2,128,512]{2,1,0:T(8,128)(2,1)} %copy-done.7, ...), custom_call_target="tpu_custom_call" | custom-call | flops 503316480 | bytes 5242880 | tf_op jit(solution)/shard_map/pallas_call | solution.py:167
  90.7 3.3 %all-to-all-done.2.held_ref = bf16[16,32,512]{2,1,0:T(8,128)(2,1)S(1)} async-done(((bf16[16,32,512]{2,1,0:T(8,128)(2,1)}), bf16[16,32,512]{2,1,0:T(8,128)(2,1)S(1)}, u32[]{:S(2)}, u32[]{:S(2)}) %all-to-all-start.2) | async-done | bytes 524320 | tf_op jit(solution)/shard_map/all_to_all | solution.py:297
  94.0 0.0 copy-done.4
  94.0 0.7 shard_map.98
  94.7 12.0 %collective-permute-start.7 = (bf16[4,32,512]{2,1,0:T(8,128)(2,1)S(1)}, bf16[4,32,512]{2,1,0:T(8,128)(2,1)S(1)}, u32[]{:S(2)}, u32[]{:S(2)}) collective-permute-start(bf16[4,32,512]{2,1,0:T(8,128)(2,1)S(1)} %get-tuple-element.40), channel_id=1, source_target_pairs={{0,32},{32,0},{1,33},{33,1},{2,34},{34,2},{3,35},{35,3},{4,36},{36... | collective-permute-start | bytes 393224 | tf_op jit(solution)/shard_map/ppermute | solution.py:301
  106.7 9.7 %collective-permute-done.7 = bf16[4,32,512]{2,1,0:T(8,128)(2,1)S(1)} collective-permute-done((bf16[4,32,512]{2,1,0:T(8,128)(2,1)S(1)}, bf16[4,32,512]{2,1,0:T(8,128)(2,1)S(1)}, u32[]{:S(2)}, u32[]{:S(2)}) %collective-permute-start.7) | collective-permute-done | bytes 131104 | tf_op jit(solution)/shard_map/ppermute | solution.py:301
  116.5 0.7 broadcast_in_dim.7
  117.2 5.9 %all-to-all-start.3 = ((bf16[8,32,512]{2,1,0:T(8,128)(2,1)}), bf16[8,32,512]{2,1,0:T(8,128)(2,1)S(1)}, u32[]{:S(2)}, u32[]{:S(2)}) async-start(bf16[8,32,512]{2,1,0:T(8,128)(2,1)} %bitcast.9), calls=%async_computation.3 | async-start | bytes 524288 | tf_op jit(solution)/shard_map/all_to_all | solution.py:297
  123.1 0.0 collective-permute-done.6
  123.1 0.0 collective-permute-done.5
  123.1 0.1 convert_add_fusion
  123.2 0.0 copy-start.9
  123.2 5.9 %shard_map.99 = (bf16[128,4096]{1,0:T(8,128)(2,1)}, f32[128,512]{1,0:T(8,128)}) custom-call(s32[20]{0:T(128)} %copy-done.3, bf16[128,4096]{1,0:T(8,128)(2,1)} %row_ref.3, bf16[2,128,512]{2,1,0:T(8,128)(2,1)} %bitcast.42, bf16[2,128,512]{2,1,0:T(8,128)(2,1)} %copy-done.8, bf16[2,128,512]{2,1,0:T(8,128)(2,1)} %copy-done.6, bf16[2,128,512]{2,1,0:T(8,128)(2,1)} %copy-done.7, ...), custom_call_target="tpu_custom_call" | custom-call | flops 503316480 | bytes 5242880 | tf_op jit(solution)/shard_map/pallas_call | solution.py:167
  129.1 1.4 %all-to-all-done.3 = bf16[8,32,512]{2,1,0:T(8,128)(2,1)S(1)} async-done(((bf16[8,32,512]{2,1,0:T(8,128)(2,1)}), bf16[8,32,512]{2,1,0:T(8,128)(2,1)S(1)}, u32[]{:S(2)}, u32[]{:S(2)}) %all-to-all-start.3) | async-done | bytes 262176 | tf_op jit(solution)/shard_map/all_to_all | solution.py:297
  130.6 0.0 copy-done.9
  130.6 1.8 %fusion.2 = (bf16[128,512]{1,0:T(8,128)(2,1)}, bf16[128,512]{1,0:T(8,128)(2,1)}) fusion(f32[128,512]{1,0:T(8,128)S(1)} %copy-done.9, f32[2,128,512]{2,1,0:T(8,128)S(1)} %convert_add_fusion, bf16[4,32,512]{2,1,0:T(8,128)(2,1)S(1)} %get-tuple-element.44, bf16[4,32,512]{2,1,0:T(8,128)(2,1)S(1)} %get-tuple-element.45, f32[128,512]{1,0:T(8,128)} %get-tuple-element.38), kind=kLoop, calls=%fused_computation.4 | loop fusion | flops 524288 | bytes 1572864 | tf_op jit(solution)/shard_map/convert_element_type | solution.py:351
  (11 shorter events, 0.1 us)
Async XLA Ops:
  0.6 0.9 copy-start.1
  1.5 0.9 copy-start.2
  3.5 12.6 %all-to-all-start = ((bf16[8,32,512]{2,1,0:T(8,128)(2,1)}), bf16[8,32,512]{2,1,0:T(8,128)(2,1)S(1)}, u32[]{:S(2)}, u32[]{:S(2)}) async-start(bf16[8,32,512]{2,1,0:T(8,128)(2,1)} %bitcast.4), calls=%async_computation | async-start | bytes 524288 | tf_op jit(solution)/shard_map/all_to_all | solution.py:297
  8.9 22.8 %collective-permute-start.2 = (bf16[2,128,512]{2,1,0:T(8,128)(2,1)}, bf16[2,128,512]{2,1,0:T(8,128)(2,1)S(1)}, u32[]{:S(2)}, u32[]{:S(2)}) collective-permute-start(bf16[2,128,512]{2,1,0:T(8,128)(2,1)} %shard_map.93.own_ref.refs_4_), channel_id=1, source_target_pairs={{0,2},{1,3},{4,6},{5,7},{8,10},{9,11},{12,14},{13,15},{16,18},{17,... | collective-permute-start | bytes 786440 | tf_op jit(solution)/shard_map/ppermute | solution.py:293
  12.8 18.9 %collective-permute-start.1 = (bf16[2,128,512]{2,1,0:T(8,128)(2,1)}, bf16[2,128,512]{2,1,0:T(8,128)(2,1)S(1)}, u32[]{:S(2)}, u32[]{:S(2)}) collective-permute-start(bf16[2,128,512]{2,1,0:T(8,128)(2,1)} %shard_map.93.own_ref.refs_4_), channel_id=1, source_target_pairs={{0,1},{1,2},{2,3},{4,5},{5,6},{6,7},{8,9},{9,10},{10,11},{12,13},{... | collective-permute-start | bytes 786440 | tf_op jit(solution)/shard_map/ppermute | solution.py:293
  16.1 24.7 %collective-permute-start = (bf16[4,32,512]{2,1,0:T(8,128)(2,1)S(1)}, bf16[4,32,512]{2,1,0:T(8,128)(2,1)S(1)}, u32[]{:S(2)}, u32[]{:S(2)}) collective-permute-start(bf16[4,32,512]{2,1,0:T(8,128)(2,1)S(1)} %slice.31.here_ref), channel_id=1, source_target_pairs={{0,32},{32,0},{1,33},{33,1},{2,34},{34,2},{3,35},{35,3},{4,36},{36... | collective-permute-start | bytes 393224 | tf_op jit(solution)/shard_map/ppermute | solution.py:301
  31.7 30.9 %copy-start.3 = (s32[20]{0:T(128)}, s32[20]{0:T(128)S(1)}, u32[]{:S(2)}) copy-start(s32[20]{0:T(128)S(1)} %concatenate.3.info_ref) | copy-start | bytes 244
  31.7 30.9 %copy-start.6 = (bf16[2,128,512]{2,1,0:T(8,128)(2,1)}, bf16[2,128,512]{2,1,0:T(8,128)(2,1)S(1)}, u32[]{:S(2)}) copy-start(bf16[2,128,512]{2,1,0:T(8,128)(2,1)S(1)} %collective-permute-done.2.far_ref.refs_2_) | copy-start | bytes 786436
  31.7 30.8 %copy-start.7 = (bf16[2,128,512]{2,1,0:T(8,128)(2,1)}, bf16[2,128,512]{2,1,0:T(8,128)(2,1)S(1)}, u32[]{:S(2)}) copy-start(bf16[2,128,512]{2,1,0:T(8,128)(2,1)S(1)} %collective-permute-done.1.near_ref.refs_3_) | copy-start | bytes 786436
  59.1 3.5 %copy-start.5 = (bf16[2,4,1,32,512]{4,3,1,0,2:T(8,128)(2,1)}, bf16[2,4,1,32,512]{4,3,1,0,2:T(8,128)(2,1)S(1)}, u32[]{:S(2)}) copy-start(bf16[2,4,1,32,512]{4,3,1,0,2:T(8,128)(2,1)S(1)} %fusion.6) | copy-start | bytes 786436
  59.1 3.4 %collective-permute-start.3 = (bf16[2,128,512]{2,1,0:T(8,128)(2,1)S(1)}, bf16[2,128,512]{2,1,0:T(8,128)(2,1)S(1)}, u32[]{:S(2)}, u32[]{:S(2)}) collective-permute-start(bf16[2,128,512]{2,1,0:T(8,128)(2,1)S(1)} %bitcast.39), channel_id=1, source_target_pairs={{1,0},{5,4},{9,8},{13,12},{17,16},{21,20},{25,24},{29,28},{33,32},... | collective-permute-start | bytes 786440 | tf_op jit(solution)/shard_map/ppermute | solution.py:293
  62.6 0.7 copy-start.8
  73.4 3.4 %collective-permute-start.4 = (bf16[2,128,512]{2,1,0:T(8,128)(2,1)}, bf16[2,128,512]{2,1,0:T(8,128)(2,1)S(1)}, u32[]{:S(2)}, u32[]{:S(2)}) collective-permute-start(bf16[2,128,512]{2,1,0:T(8,128)(2,1)} %get-tuple-element.27), channel_id=1, source_target_pairs={{0,1},{4,5},{8,9},{12,13},{16,17},{20,21},{24,25},{28,29},{32,33},... | collective-permute-start | bytes 786440 | tf_op jit(solution)/shard_map/ppermute | solution.py:293
  76.8 0.9 copy-start
  78.6 15.4 %copy-start.4 = (s32[20]{0:T(128)S(1)}, s32[20]{0:T(128)}, u32[]{:S(2)}) copy-start(s32[20]{0:T(128)} %copy-done.3) | copy-start | bytes 244
  78.6 15.4 %all-to-all-start.2 = ((bf16[16,32,512]{2,1,0:T(8,128)(2,1)}), bf16[16,32,512]{2,1,0:T(8,128)(2,1)S(1)}, u32[]{:S(2)}, u32[]{:S(2)}) async-start(bf16[16,32,512]{2,1,0:T(8,128)(2,1)} %shard_map.96), calls=%async_computation.2 | async-start | bytes 1048576 | tf_op jit(solution)/shard_map/all_to_all | solution.py:297
  82.3 40.8 %collective-permute-start.6 = (bf16[2,128,512]{2,1,0:T(8,128)(2,1)}, bf16[2,128,512]{2,1,0:T(8,128)(2,1)S(1)}, u32[]{:S(2)}, u32[]{:S(2)}) collective-permute-start(bf16[2,128,512]{2,1,0:T(8,128)(2,1)} %get-tuple-element.26.far_ref), channel_id=1, source_target_pairs={{2,0},{3,1},{6,4},{7,5},{10,8},{11,9},{14,12},{15,13},{18,16},{19,... | collective-permute-start | bytes 786440 | tf_op jit(solution)/shard_map/ppermute | solution.py:293
  83.6 39.5 %collective-permute-start.5 = (bf16[2,128,512]{2,1,0:T(8,128)(2,1)}, bf16[2,128,512]{2,1,0:T(8,128)(2,1)S(1)}, u32[]{:S(2)}, u32[]{:S(2)}) collective-permute-start(bf16[2,128,512]{2,1,0:T(8,128)(2,1)} %get-tuple-element.27), channel_id=1, source_target_pairs={{1,0},{2,1},{3,2},{5,4},{6,5},{7,6},{9,8},{10,9},{11,10},{13,12},{... | collective-permute-start | bytes 786440 | tf_op jit(solution)/shard_map/ppermute | solution.py:293
  94.7 21.8 %collective-permute-start.7 = (bf16[4,32,512]{2,1,0:T(8,128)(2,1)S(1)}, bf16[4,32,512]{2,1,0:T(8,128)(2,1)S(1)}, u32[]{:S(2)}, u32[]{:S(2)}) collective-permute-start(bf16[4,32,512]{2,1,0:T(8,128)(2,1)S(1)} %get-tuple-element.40), channel_id=1, source_target_pairs={{0,32},{32,0},{1,33},{33,1},{2,34},{34,2},{3,35},{35,3},{4,36},{36... | collective-permute-start | bytes 393224 | tf_op jit(solution)/shard_map/ppermute | solution.py:301
  117.2 13.3 %all-to-all-start.3 = ((bf16[8,32,512]{2,1,0:T(8,128)(2,1)}), bf16[8,32,512]{2,1,0:T(8,128)(2,1)S(1)}, u32[]{:S(2)}, u32[]{:S(2)}) async-start(bf16[8,32,512]{2,1,0:T(8,128)(2,1)} %bitcast.9), calls=%async_computation.3 | async-start | bytes 524288 | tf_op jit(solution)/shard_map/all_to_all | solution.py:297
  123.2 7.4 %copy-start.9 = (f32[128,512]{1,0:T(8,128)S(1)}, f32[128,512]{1,0:T(8,128)}, u32[]{:S(2)}) copy-start(f32[128,512]{1,0:T(8,128)} %get-tuple-element.41) | copy-start | bytes 786436

commit v8 on v6

--- a/solution.py
+++ b/solution.py
@@ -297,13 +297,15 @@
     )
 
     before = move(near_grad, [(0, 1)])
-    halo = (far_grad.astype(jnp.float32) + before.astype(jnp.float32)).astype(jnp.bfloat16)
-    pieces = jnp.broadcast_to(halo.reshape(2, 4, 1, *part[1:]), (2, 4, 2, *part[1:]))
+    twice = lambda t: jnp.broadcast_to(t.reshape(2, 4, 1, *part[1:]), (2, 4, 2, *part[1:]))
+    pieces = twice(far_grad).astype(jnp.float32) + twice(before).astype(jnp.float32)
+    pieces = pieces.astype(jnp.bfloat16)
     pieces, weights, dscores = lax.optimization_barrier((pieces, weights, dscores))
     held = exchange(pieces.reshape(16, *part[1:]), PLANE_AXES)
     attended, grad_query, own_grad = outputs_and_own(info, queries, grads, pairs, weights, dscores)
     held, own_grad = lax.optimization_barrier((held, own_grad))
     here, there = route(route_back_kernel, info, (held,), (4, 4))
+    there, near_grad, far_grad = lax.optimization_barrier((there, near_grad, far_grad))
     there = across(there)
     near_back = move(near_grad, [(1, 0), (2, 1), (3, 2)])
     far_back = move(far_grad, [(2, 0), (3, 1)])

time: 132 us -> 134 us (1.015)
  waiting for transfers between devices: 33 us -> 36.9 us
  starting transfers between devices: 53.7 us -> 51.6 us
    all_to_all x3, waiting for transfers between devices: 9.79 us -> 12.3 us  [exchange(): return lax.all_to_all(pieces, axes, 0, 0)]
    all_to_all x3, starting transfers between devices: 15.7 us -> 13.6 us  [exchange(): return lax.all_to_all(pieces, axes, 0, 0)]
    ppermute x2, waiting for transfers between devices: 19.7 us -> 21.1 us  [across(): return lax.ppermute(value, 'z', [(0, 1), (1, 0)])]
where the time goes in v8:
time: 134 us; the launch traced here: 133 us
  starting transfers between devices  51.6 us (39%)
  waiting for transfers between devices  36.9 us (28%)
  Pallas kernels  18.5 us (14%)
  blocking collectives  17.4 us (13%)
  other arithmetic  4.72 us (4%)
  local copies, waits for them, and re-layouts  3.06 us (2%)
    ppermute x2, starting transfers between devices, across(): return lax.ppermute(value, 'z', [(0, 1), (1, 0)])  26.8 us
    ppermute x2, waiting for transfers between devices, across(): return lax.ppermute(value, 'z', [(0, 1), (1, 0)])  21.1 us
    all_to_all x1, blocking collectives, exchange(): return lax.all_to_all(pieces, axes, 0, 0)  17.4 us
    all_to_all x3, starting transfers between devices, exchange(): return lax.all_to_all(pieces, axes, 0, 0)  13.6 us
    all_to_all x3, waiting for transfers between devices, exchange(): return lax.all_to_all(pieces, axes, 0, 0)  12.3 us
    ppermute x6, starting transfers between devices, move(): return lax.ppermute(value, BLOCK_AXES, moves)  11.2 us
    pallas_call x1, Pallas kernels, scores_and_halo(): pl.pallas_call(score_kernel, grid_spec=pltpu.PrefetchScalarGridSpec(num_s...  9.34 us
    pallas_call x1, Pallas kernels, outputs_and_own(): pl.pallas_call(output_kernel, grid_spec=pltpu.PrefetchScalarGridSpec(num_...  7.59 us
  transfers between devices with their start and end apart: 11, of which 7 were waited for; matrix products, arithmetic and copies ran while one was open for 2% of the time, Pallas kernels for 6%

profile of v8, /device:TPU:32, one launch (start us, length us, event | category | flops | bytes accessed | tf_op | source)
XLA Modules:
  0.0 133.0 jit_solution(8219259594452029166)
XLA Ops:
  0.6 1.7 %pad_maximum_fusion.own_ref = bf16[2,128,512]{2,1,0:T(8,128)(2,1)} fusion(bf16[1,128,512]{2,1,0:T(8,128)(2,1)} %bitcast.39, bf16[1,128,512]{2,1,0:T(8,128)(2,1)} %bitcast.40), kind=kLoop, calls=%fused_computation.9 | loop fusion | flops 131072 | bytes 524288 | tf_op jit(solution)/shard_map/stack | solution.py:283
  2.3 5.4 %all-to-all-start = ((bf16[8,32,512]{2,1,0:T(8,128)(2,1)}), bf16[8,32,512]{2,1,0:T(8,128)(2,1)S(1)}, u32[]{:S(2)}, u32[]{:S(2)}) async-start(bf16[8,32,512]{2,1,0:T(8,128)(2,1)} %bitcast.6), calls=%async_computation | async-start | bytes 524288 | tf_op jit(solution)/shard_map/all_to_all | solution.py:268
  7.7 3.9 %collective-permute-start.2 = (bf16[2,128,512]{2,1,0:T(8,128)(2,1)}, bf16[2,128,512]{2,1,0:T(8,128)(2,1)S(1)}, u32[]{:S(2)}, u32[]{:S(2)}) collective-permute-start(bf16[2,128,512]{2,1,0:T(8,128)(2,1)} %pad_maximum_fusion.own_ref), channel_id=1, source_target_pairs={{0,2},{1,3},{4,6},{5,7},{8,10},{9,11},{12,14},{13,15},{16,18},{17,... | collective-permute-start | bytes 786440 | tf_op jit(solution)/shard_map/ppermute | solution.py:264
  11.7 1.3 collective-permute-start.1
  13.0 2.0 %all-to-all-done = bf16[8,32,512]{2,1,0:T(8,128)(2,1)S(1)} async-done(((bf16[8,32,512]{2,1,0:T(8,128)(2,1)}), bf16[8,32,512]{2,1,0:T(8,128)(2,1)S(1)}, u32[]{:S(2)}, u32[]{:S(2)}) %all-to-all-start) | async-done | bytes 262176 | tf_op jit(solution)/shard_map/all_to_all | solution.py:268
  15.0 14.8 %collective-permute-start = (bf16[4,32,512]{2,1,0:T(8,128)(2,1)S(1)}, bf16[4,32,512]{2,1,0:T(8,128)(2,1)S(1)}, u32[]{:S(2)}, u32[]{:S(2)}) collective-permute-start(bf16[4,32,512]{2,1,0:T(8,128)(2,1)S(1)} %slice.31.here_ref), channel_id=1, source_target_pairs={{0,32},{32,0},{1,33},{33,1},{2,34},{34,2},{3,35},{35,3},{4,36},{36... | collective-permute-start | bytes 393224 | tf_op jit(solution)/shard_map/ppermute | solution.py:272
  29.8 0.7 concatenate.3.info_ref
  30.6 0.0 copy-start
  30.6 0.0 collective-permute-done.2.far_ref
  30.6 0.0 collective-permute-done.1.near_ref
  30.6 0.0 copy-start.4
  30.6 9.1 %collective-permute-done.there_ref = bf16[4,32,512]{2,1,0:T(8,128)(2,1)S(1)} collective-permute-done((bf16[4,32,512]{2,1,0:T(8,128)(2,1)S(1)}, bf16[4,32,512]{2,1,0:T(8,128)(2,1)S(1)}, u32[]{:S(2)}, u32[]{:S(2)}) %collective-permute-start) | collective-permute-done | bytes 131104 | tf_op jit(solution)/shard_map/ppermute | solution.py:272
  39.7 0.8 shard_map.93
  40.5 17.4 %all_to_all.20 = bf16[16,32,512]{2,1,0:T(8,128)(2,1)S(1)} all-to-all(bf16[16,32,512]{2,1,0:T(8,128)(2,1)S(1)} %shard_map.93), channel_id=1, replica_groups=mesh['dp'=8,'z'=2,'y'=4,'b'=2,'x'=2,'core'=2] {'x','y','b'}, dimensions={0} | all-to-all | bytes 1048576 | tf_op jit(solution)/shard_map/all_to_all | solution.py:268
  58.0 0.0 copy-start.2
  58.0 1.3 collective-permute-start.3
  59.3 2.1 %collective-permute-done.3.before_ref = bf16[2,128,512]{2,1,0:T(8,128)(2,1)S(1)} collective-permute-done((bf16[2,128,512]{2,1,0:T(8,128)(2,1)S(1)}, bf16[2,128,512]{2,1,0:T(8,128)(2,1)S(1)}, u32[]{:S(2)}, u32[]{:S(2)}) %collective-permute-start.3) | collective-permute-done | bytes 262176 | tf_op jit(solution)/shard_map/ppermute | solution.py:264
  61.4 0.0 copy-done
  61.4 0.0 copy-done.3
  61.4 0.0 copy-done.4
  61.4 0.0 copy-done.2
  61.4 0.7 copy-done.6
  62.1 9.3 %shard_map.94 = (bf16[384,4096]{1,0:T(8,128)(2,1)}, bf16[384,4096]{1,0:T(8,128)(2,1)}, bf16[2,128,512]{2,1,0:T(8,128)(2,1)}, bf16[2,128,512]{2,1,0:T(8,128)(2,1)}) custom-call(s32[20]{0:T(128)} %copy-done, s32[64,128]{1,0:T(8,128)} %bitcast.41, bf16[128,4096]{1,0:T(8,128)(2,1)} %query_ref.3, bf16[128,4096]{1,0:T(8,128)(2,1)} %grad_ref.3, ...), custom_call_target="tpu_custom_call" | custom-call | flops 1409286144 | bytes 8388608 | tf_op jit(solution)/shard_map/pallas_call | solution.py:161
  71.5 2.0 %collective-permute-start.4 = (bf16[2,128,512]{2,1,0:T(8,128)(2,1)}, bf16[2,128,512]{2,1,0:T(8,128)(2,1)S(1)}, u32[]{:S(2)}, u32[]{:S(2)}) collective-permute-start(bf16[2,128,512]{2,1,0:T(8,128)(2,1)} %get-tuple-element.40), channel_id=1, source_target_pairs={{0,1},{4,5},{8,9},{12,13},{16,17},{20,21},{24,25},{28,29},{32,33},... | collective-permute-start | bytes 786440 | tf_op jit(solution)/shard_map/ppermute | solution.py:264
  73.5 1.3 %collective-permute-done.4 = bf16[2,128,512]{2,1,0:T(8,128)(2,1)S(1)} collective-permute-done((bf16[2,128,512]{2,1,0:T(8,128)(2,1)}, bf16[2,128,512]{2,1,0:T(8,128)(2,1)S(1)}, u32[]{:S(2)}, u32[]{:S(2)}) %collective-permute-start.4) | collective-permute-done | bytes 262176 | tf_op jit(solution)/shard_map/ppermute | solution.py:264
  74.8 1.0 add_convert_fusion
  75.9 0.8 broadcast_in_dim.7
  76.7 3.6 %all-to-all-start.2 = ((bf16[16,32,512]{2,1,0:T(8,128)(2,1)}), bf16[16,32,512]{2,1,0:T(8,128)(2,1)S(1)}, u32[]{:S(2)}, u32[]{:S(2)}) async-start(bf16[16,32,512]{2,1,0:T(8,128)(2,1)} %bitcast.11), calls=%async_computation.2 | async-start | bytes 1048576 | tf_op jit(solution)/shard_map/all_to_all | solution.py:268
  80.3 0.0 copy-start.1
  80.3 0.0 copy-start.7
  80.3 0.0 copy-start.5
  80.3 7.6 %shard_map.95 = (bf16[128,4096]{1,0:T(8,128)(2,1)}, bf16[128,4096]{1,0:T(8,128)(2,1)}, f32[2,128,512]{2,1,0:T(8,128)}) custom-call(s32[20]{0:T(128)} %copy-done, bf16[128,4096]{1,0:T(8,128)(2,1)} %query_ref.3, bf16[128,4096]{1,0:T(8,128)(2,1)} %grad_ref.3, bf16[2,128,512]{2,1,0:T(8,128)(2,1)} %bitcast.35, bf16[2,128,512]{2,1,0:T(8,128)(2,1)} %copy-done.6, ...), custom_call_target="tpu_custom_call" | custom-call | flops 1006632960 | bytes 10485760 | tf_op jit(solution)/shard_map/pallas_call | solution.py:184
  87.9 4.0 %all-to-all-done.2.held_ref = bf16[16,32,512]{2,1,0:T(8,128)(2,1)S(1)} async-done(((bf16[16,32,512]{2,1,0:T(8,128)(2,1)}), bf16[16,32,512]{2,1,0:T(8,128)(2,1)S(1)}, u32[]{:S(2)}, u32[]{:S(2)}) %all-to-all-start.2) | async-done | bytes 524320 | tf_op jit(solution)/shard_map/all_to_all | solution.py:268
  91.9 0.0 copy-done.1
  91.9 0.7 shard_map.96
  92.7 0.0 copy-done.7
  92.7 1.3 collective-permute-start.5
  94.0 0.0 copy-done.5
  94.0 1.3 collective-permute-start.6
  95.3 12.0 %collective-permute-start.7 = (bf16[4,32,512]{2,1,0:T(8,128)(2,1)S(1)}, bf16[4,32,512]{2,1,0:T(8,128)(2,1)S(1)}, u32[]{:S(2)}, u32[]{:S(2)}) collective-permute-start(bf16[4,32,512]{2,1,0:T(8,128)(2,1)S(1)} %get-tuple-element.43), channel_id=1, source_target_pairs={{0,32},{32,0},{1,33},{33,1},{2,34},{34,2},{3,35},{35,3},{4,36},{36... | collective-permute-start | bytes 393224 | tf_op jit(solution)/shard_map/ppermute | solution.py:272
  107.3 12.0 %collective-permute-done.7 = bf16[4,32,512]{2,1,0:T(8,128)(2,1)S(1)} collective-permute-done((bf16[4,32,512]{2,1,0:T(8,128)(2,1)S(1)}, bf16[4,32,512]{2,1,0:T(8,128)(2,1)S(1)}, u32[]{:S(2)}, u32[]{:S(2)}) %collective-permute-start.7) | collective-permute-done | bytes 131104 | tf_op jit(solution)/shard_map/ppermute | solution.py:272
  119.4 0.7 broadcast_in_dim.16
  120.1 4.7 %all-to-all-start.3 = ((bf16[8,32,512]{2,1,0:T(8,128)(2,1)}), bf16[8,32,512]{2,1,0:T(8,128)(2,1)S(1)}, u32[]{:S(2)}, u32[]{:S(2)}) async-start(bf16[8,32,512]{2,1,0:T(8,128)(2,1)} %bitcast.12), calls=%async_computation.3 | async-start | bytes 524288 | tf_op jit(solution)/shard_map/all_to_all | solution.py:268
  124.8 0.0 collective-permute-done.5
  124.8 0.0 collective-permute-done.6
  124.8 1.1 convert_add_fusion
  125.9 6.3 %all-to-all-done.3 = bf16[8,32,512]{2,1,0:T(8,128)(2,1)S(1)} async-done(((bf16[8,32,512]{2,1,0:T(8,128)(2,1)}), bf16[8,32,512]{2,1,0:T(8,128)(2,1)S(1)}, u32[]{:S(2)}, u32[]{:S(2)}) %all-to-all-start.3) | async-done | bytes 262176 | tf_op jit(solution)/shard_map/all_to_all | solution.py:268
  132.3 0.8 fusion.4
  (7 shorter events, 0.1 us)
Async XLA Ops:
  2.3 12.6 %all-to-all-start = ((bf16[8,32,512]{2,1,0:T(8,128)(2,1)}), bf16[8,32,512]{2,1,0:T(8,128)(2,1)S(1)}, u32[]{:S(2)}, u32[]{:S(2)}) async-start(bf16[8,32,512]{2,1,0:T(8,128)(2,1)} %bitcast.6), calls=%async_computation | async-start | bytes 524288 | tf_op jit(solution)/shard_map/all_to_all | solution.py:268
  7.7 22.8 %collective-permute-start.2 = (bf16[2,128,512]{2,1,0:T(8,128)(2,1)}, bf16[2,128,512]{2,1,0:T(8,128)(2,1)S(1)}, u32[]{:S(2)}, u32[]{:S(2)}) collective-permute-start(bf16[2,128,512]{2,1,0:T(8,128)(2,1)} %pad_maximum_fusion.own_ref), channel_id=1, source_target_pairs={{0,2},{1,3},{4,6},{5,7},{8,10},{9,11},{12,14},{13,15},{16,18},{17,... | collective-permute-start | bytes 786440 | tf_op jit(solution)/shard_map/ppermute | solution.py:264
  11.7 18.9 %collective-permute-start.1 = (bf16[2,128,512]{2,1,0:T(8,128)(2,1)}, bf16[2,128,512]{2,1,0:T(8,128)(2,1)S(1)}, u32[]{:S(2)}, u32[]{:S(2)}) collective-permute-start(bf16[2,128,512]{2,1,0:T(8,128)(2,1)} %pad_maximum_fusion.own_ref), channel_id=1, source_target_pairs={{0,1},{1,2},{2,3},{4,5},{5,6},{6,7},{8,9},{9,10},{10,11},{12,13},{... | collective-permute-start | bytes 786440 | tf_op jit(solution)/shard_map/ppermute | solution.py:264
  15.0 24.7 %collective-permute-start = (bf16[4,32,512]{2,1,0:T(8,128)(2,1)S(1)}, bf16[4,32,512]{2,1,0:T(8,128)(2,1)S(1)}, u32[]{:S(2)}, u32[]{:S(2)}) collective-permute-start(bf16[4,32,512]{2,1,0:T(8,128)(2,1)S(1)} %slice.31.here_ref), channel_id=1, source_target_pairs={{0,32},{32,0},{1,33},{33,1},{2,34},{34,2},{3,35},{35,3},{4,36},{36... | collective-permute-start | bytes 393224 | tf_op jit(solution)/shard_map/ppermute | solution.py:272
  30.6 30.9 %copy-start = (s32[20]{0:T(128)}, s32[20]{0:T(128)S(1)}, u32[]{:S(2)}) copy-start(s32[20]{0:T(128)S(1)} %concatenate.3.info_ref) | copy-start | bytes 244
  30.6 30.9 %copy-start.3 = (bf16[2,128,512]{2,1,0:T(8,128)(2,1)}, bf16[2,128,512]{2,1,0:T(8,128)(2,1)S(1)}, u32[]{:S(2)}) copy-start(bf16[2,128,512]{2,1,0:T(8,128)(2,1)S(1)} %collective-permute-done.2.far_ref) | copy-start | bytes 786436
  30.6 30.8 %copy-start.4 = (bf16[2,128,512]{2,1,0:T(8,128)(2,1)}, bf16[2,128,512]{2,1,0:T(8,128)(2,1)S(1)}, u32[]{:S(2)}) copy-start(bf16[2,128,512]{2,1,0:T(8,128)(2,1)S(1)} %collective-permute-done.1.near_ref) | copy-start | bytes 786436
  58.0 3.5 %copy-start.2 = (bf16[2,4,1,32,512]{4,3,1,0,2:T(8,128)(2,1)}, bf16[2,4,1,32,512]{4,3,1,0,2:T(8,128)(2,1)S(1)}, u32[]{:S(2)}) copy-start(bf16[2,4,1,32,512]{4,3,1,0,2:T(8,128)(2,1)S(1)} %fusion.2) | copy-start | bytes 786436
  58.0 3.4 %collective-permute-start.3 = (bf16[2,128,512]{2,1,0:T(8,128)(2,1)S(1)}, bf16[2,128,512]{2,1,0:T(8,128)(2,1)S(1)}, u32[]{:S(2)}, u32[]{:S(2)}) collective-permute-start(bf16[2,128,512]{2,1,0:T(8,128)(2,1)S(1)} %bitcast.33), channel_id=1, source_target_pairs={{1,0},{5,4},{9,8},{13,12},{17,16},{21,20},{25,24},{29,28},{33,32},... | collective-permute-start | bytes 786440 | tf_op jit(solution)/shard_map/ppermute | solution.py:264
  61.4 0.7 copy-start.6
  71.5 3.4 %collective-permute-start.4 = (bf16[2,128,512]{2,1,0:T(8,128)(2,1)}, bf16[2,128,512]{2,1,0:T(8,128)(2,1)S(1)}, u32[]{:S(2)}, u32[]{:S(2)}) collective-permute-start(bf16[2,128,512]{2,1,0:T(8,128)(2,1)} %get-tuple-element.40), channel_id=1, source_target_pairs={{0,1},{4,5},{8,9},{12,13},{16,17},{20,21},{24,25},{28,29},{32,33},... | collective-permute-start | bytes 786440 | tf_op jit(solution)/shard_map/ppermute | solution.py:264
  76.7 15.2 %all-to-all-start.2 = ((bf16[16,32,512]{2,1,0:T(8,128)(2,1)}), bf16[16,32,512]{2,1,0:T(8,128)(2,1)S(1)}, u32[]{:S(2)}, u32[]{:S(2)}) async-start(bf16[16,32,512]{2,1,0:T(8,128)(2,1)} %bitcast.11), calls=%async_computation.2 | async-start | bytes 1048576 | tf_op jit(solution)/shard_map/all_to_all | solution.py:268
  80.3 11.7 %copy-start.1 = (s32[20]{0:T(128)S(1)}, s32[20]{0:T(128)}, u32[]{:S(2)}) copy-start(s32[20]{0:T(128)} %copy-done) | copy-start | bytes 244
  80.3 12.4 %copy-start.7 = (bf16[2,128,512]{2,1,0:T(8,128)(2,1)S(1)}, bf16[2,128,512]{2,1,0:T(8,128)(2,1)}, u32[]{:S(2)}) copy-start(bf16[2,128,512]{2,1,0:T(8,128)(2,1)} %get-tuple-element.40) | copy-start | bytes 786436
  80.3 13.7 %copy-start.5 = (bf16[2,128,512]{2,1,0:T(8,128)(2,1)S(1)}, bf16[2,128,512]{2,1,0:T(8,128)(2,1)}, u32[]{:S(2)}) copy-start(bf16[2,128,512]{2,1,0:T(8,128)(2,1)} %get-tuple-element.41) | copy-start | bytes 786436
  92.7 32.1 %collective-permute-start.5 = (bf16[2,128,512]{2,1,0:T(8,128)(2,1)S(1)}, bf16[2,128,512]{2,1,0:T(8,128)(2,1)S(1)}, u32[]{:S(2)}, u32[]{:S(2)}) collective-permute-start(bf16[2,128,512]{2,1,0:T(8,128)(2,1)S(1)} %copy-done.7), channel_id=1, source_target_pairs={{1,0},{2,1},{3,2},{5,4},{6,5},{7,6},{9,8},{10,9},{11,10},{13,12},{... | collective-permute-start | bytes 786440 | tf_op jit(solution)/shard_map/ppermute | solution.py:264
  94.0 30.7 %collective-permute-start.6 = (bf16[2,128,512]{2,1,0:T(8,128)(2,1)S(1)}, bf16[2,128,512]{2,1,0:T(8,128)(2,1)S(1)}, u32[]{:S(2)}, u32[]{:S(2)}) collective-permute-start(bf16[2,128,512]{2,1,0:T(8,128)(2,1)S(1)} %copy-done.5), channel_id=1, source_target_pairs={{2,0},{3,1},{6,4},{7,5},{10,8},{11,9},{14,12},{15,13},{18,16},{19,... | collective-permute-start | bytes 786440 | tf_op jit(solution)/shard_map/ppermute | solution.py:264
  95.3 24.0 %collective-permute-start.7 = (bf16[4,32,512]{2,1,0:T(8,128)(2,1)S(1)}, bf16[4,32,512]{2,1,0:T(8,128)(2,1)S(1)}, u32[]{:S(2)}, u32[]{:S(2)}) collective-permute-start(bf16[4,32,512]{2,1,0:T(8,128)(2,1)S(1)} %get-tuple-element.43), channel_id=1, source_target_pairs={{0,32},{32,0},{1,33},{33,1},{2,34},{34,2},{3,35},{35,3},{4,36},{36... | collective-permute-start | bytes 393224 | tf_op jit(solution)/shard_map/ppermute | solution.py:272
  120.1 12.1 %all-to-all-start.3 = ((bf16[8,32,512]{2,1,0:T(8,128)(2,1)}), bf16[8,32,512]{2,1,0:T(8,128)(2,1)S(1)}, u32[]{:S(2)}, u32[]{:S(2)}) async-start(bf16[8,32,512]{2,1,0:T(8,128)(2,1)} %bitcast.12), calls=%async_computation.3 | async-start | bytes 524288 | tf_op jit(solution)/shard_map/all_to_all | solution.py:268

commit v9 on v6

--- a/solution.py
+++ b/solution.py
@@ -305,6 +305,7 @@
     held, own_grad = lax.optimization_barrier((held, own_grad))
     here, there = route(route_back_kernel, info, (held,), (4, 4))
     there = across(there)
+    there, near_grad, far_grad = lax.optimization_barrier((there, near_grad, far_grad))
     near_back = move(near_grad, [(1, 0), (2, 1), (3, 2)])
     far_back = move(far_grad, [(2, 0), (3, 1)])
     pieces = jnp.broadcast_to(here + there, (2, *part)).reshape(8, *part[1:])

time: 132 us -> 134 us (1.015)
  waiting for transfers between devices: 33 us -> 39.6 us
  starting transfers between devices: 53.7 us -> 50.5 us
    ppermute x6, waiting for transfers between devices: 3.48 us -> 9.83 us  [move(): return lax.ppermute(value, BLOCK_AXES, moves)]
    all_to_all x3, starting transfers between devices: 15.7 us -> 12.5 us  [exchange(): return lax.all_to_all(pieces, axes, 0, 0)]
  transfers between devices with their start and end apart: 11 -> 11, of which waited for: 7 -> 8; matrix products, arithmetic and copies ran while one was open for 2% -> 1% of each run, Pallas kernels for 6% -> 6%
where the time goes in v9:
time: 134 us
  starting transfers between devices  50.5 us (38%)
  waiting for transfers between devices  39.6 us (30%)
  Pallas kernels  18.4 us (14%)
  blocking collectives  17.4 us (13%)
  other arithmetic  3.7 us (3%)
  local copies, waits for them, and re-layouts  3.08 us (2%)
    ppermute x2, starting transfers between devices, across(): return lax.ppermute(value, 'z', [(0, 1), (1, 0)])  26.8 us
    ppermute x2, waiting for transfers between devices, across(): return lax.ppermute(value, 'z', [(0, 1), (1, 0)])  18.9 us
    all_to_all x1, blocking collectives, exchange(): return lax.all_to_all(pieces, axes, 0, 0)  17.4 us
    all_to_all x3, starting transfers between devices, exchange(): return lax.all_to_all(pieces, axes, 0, 0)  12.5 us
    ppermute x6, starting transfers between devices, move(): return lax.ppermute(value, BLOCK_AXES, moves)  11.2 us
    all_to_all x3, waiting for transfers between devices, exchange(): return lax.all_to_all(pieces, axes, 0, 0)  10.9 us
    ppermute x6, waiting for transfers between devices, move(): return lax.ppermute(value, BLOCK_AXES, moves)  9.83 us
    pallas_call x1, Pallas kernels, scores_and_halo(): pl.pallas_call(score_kernel, grid_spec=pltpu.PrefetchScalarGridSpec(num_s...  9.31 us
  transfers between devices with their start and end apart: 11, of which 8 were waited for; matrix products, arithmetic and copies ran while one was open for 1% of the time, Pallas kernels for 6%

profile of v9, /device:TPU:32, one launch (start us, length us, event | category | flops | bytes accessed | tf_op | source)
XLA Modules:
  0.0 133.6 jit_solution(9574144662802209153)
XLA Ops:
  0.6 1.7 %pad_maximum_fusion.own_ref = bf16[2,128,512]{2,1,0:T(8,128)(2,1)} fusion(bf16[1,128,512]{2,1,0:T(8,128)(2,1)} %bitcast.39, bf16[1,128,512]{2,1,0:T(8,128)(2,1)} %bitcast.40), kind=kLoop, calls=%fused_computation.9 | loop fusion | flops 131072 | bytes 524288 | tf_op jit(solution)/shard_map/stack | solution.py:283
  2.4 5.4 %all-to-all-start = ((bf16[8,32,512]{2,1,0:T(8,128)(2,1)}), bf16[8,32,512]{2,1,0:T(8,128)(2,1)S(1)}, u32[]{:S(2)}, u32[]{:S(2)}) async-start(bf16[8,32,512]{2,1,0:T(8,128)(2,1)} %bitcast.6), calls=%async_computation | async-start | bytes 524288 | tf_op jit(solution)/shard_map/all_to_all | solution.py:268
  7.8 3.9 %collective-permute-start.2 = (bf16[2,128,512]{2,1,0:T(8,128)(2,1)}, bf16[2,128,512]{2,1,0:T(8,128)(2,1)S(1)}, u32[]{:S(2)}, u32[]{:S(2)}) collective-permute-start(bf16[2,128,512]{2,1,0:T(8,128)(2,1)} %pad_maximum_fusion.own_ref), channel_id=1, source_target_pairs={{0,2},{1,3},{4,6},{5,7},{8,10},{9,11},{12,14},{13,15},{16,18},{17,... | collective-permute-start | bytes 786440 | tf_op jit(solution)/shard_map/ppermute | solution.py:264
  11.7 1.3 collective-permute-start.1
  13.0 2.0 %all-to-all-done = bf16[8,32,512]{2,1,0:T(8,128)(2,1)S(1)} async-done(((bf16[8,32,512]{2,1,0:T(8,128)(2,1)}), bf16[8,32,512]{2,1,0:T(8,128)(2,1)S(1)}, u32[]{:S(2)}, u32[]{:S(2)}) %all-to-all-start) | async-done | bytes 262176 | tf_op jit(solution)/shard_map/all_to_all | solution.py:268
  15.0 14.8 %collective-permute-start = (bf16[4,32,512]{2,1,0:T(8,128)(2,1)S(1)}, bf16[4,32,512]{2,1,0:T(8,128)(2,1)S(1)}, u32[]{:S(2)}, u32[]{:S(2)}) collective-permute-start(bf16[4,32,512]{2,1,0:T(8,128)(2,1)S(1)} %slice.31.here_ref), channel_id=1, source_target_pairs={{0,32},{32,0},{1,33},{33,1},{2,34},{34,2},{3,35},{35,3},{4,36},{36... | collective-permute-start | bytes 393224 | tf_op jit(solution)/shard_map/ppermute | solution.py:272
  29.8 0.7 concatenate.3.info_ref
  30.6 0.0 collective-permute-done.2.far_ref
  30.6 0.0 collective-permute-done.1.near_ref
  30.6 0.0 copy-start.5
  30.6 9.1 %collective-permute-done.there_ref = bf16[4,32,512]{2,1,0:T(8,128)(2,1)S(1)} collective-permute-done((bf16[4,32,512]{2,1,0:T(8,128)(2,1)S(1)}, bf16[4,32,512]{2,1,0:T(8,128)(2,1)S(1)}, u32[]{:S(2)}, u32[]{:S(2)}) %collective-permute-start) | collective-permute-done | bytes 131104 | tf_op jit(solution)/shard_map/ppermute | solution.py:272
  39.7 0.8 shard_map.93
  40.5 17.4 %all_to_all.20 = bf16[16,32,512]{2,1,0:T(8,128)(2,1)S(1)} all-to-all(bf16[16,32,512]{2,1,0:T(8,128)(2,1)S(1)} %shard_map.93), channel_id=1, replica_groups=mesh['dp'=8,'z'=2,'y'=4,'b'=2,'x'=2,'core'=2] {'x','y','b'}, dimensions={0} | all-to-all | bytes 1048576 | tf_op jit(solution)/shard_map/all_to_all | solution.py:268
  58.0 0.0 copy-start.2
  58.0 1.3 collective-permute-start.3
  59.3 2.1 %collective-permute-done.3.before_ref = bf16[2,128,512]{2,1,0:T(8,128)(2,1)S(1)} collective-permute-done((bf16[2,128,512]{2,1,0:T(8,128)(2,1)S(1)}, bf16[2,128,512]{2,1,0:T(8,128)(2,1)S(1)}, u32[]{:S(2)}, u32[]{:S(2)}) %collective-permute-start.3) | collective-permute-done | bytes 262176 | tf_op jit(solution)/shard_map/ppermute | solution.py:264
  61.4 0.0 copy-done
  61.4 0.0 copy-done.4
  61.4 0.0 copy-done.5
  61.5 0.0 copy-done.2
  61.5 0.7 copy-done.7
  62.2 9.3 %shard_map.94 = (bf16[384,4096]{1,0:T(8,128)(2,1)}, bf16[384,4096]{1,0:T(8,128)(2,1)}, bf16[2,128,512]{2,1,0:T(8,128)(2,1)}, bf16[2,128,512]{2,1,0:T(8,128)(2,1)}) custom-call(s32[20]{0:T(128)} %copy-done, s32[64,128]{1,0:T(8,128)} %bitcast.41, bf16[128,4096]{1,0:T(8,128)(2,1)} %query_ref.3, bf16[128,4096]{1,0:T(8,128)(2,1)} %grad_ref.3, ...), custom_call_target="tpu_custom_call" | custom-call | flops 1409286144 | bytes 8388608 | tf_op jit(solution)/shard_map/pallas_call | solution.py:161
  71.5 2.0 %collective-permute-start.4 = (bf16[2,128,512]{2,1,0:T(8,128)(2,1)}, bf16[2,128,512]{2,1,0:T(8,128)(2,1)S(1)}, u32[]{:S(2)}, u32[]{:S(2)}) collective-permute-start(bf16[2,128,512]{2,1,0:T(8,128)(2,1)} %get-tuple-element.40), channel_id=1, source_target_pairs={{0,1},{4,5},{8,9},{12,13},{16,17},{20,21},{24,25},{28,29},{32,33},... | collective-permute-start | bytes 786440 | tf_op jit(solution)/shard_map/ppermute | solution.py:264
  73.5 1.3 %collective-permute-done.4 = bf16[2,128,512]{2,1,0:T(8,128)(2,1)S(1)} collective-permute-done((bf16[2,128,512]{2,1,0:T(8,128)(2,1)}, bf16[2,128,512]{2,1,0:T(8,128)(2,1)S(1)}, u32[]{:S(2)}, u32[]{:S(2)}) %collective-permute-start.4) | collective-permute-done | bytes 262176 | tf_op jit(solution)/shard_map/ppermute | solution.py:264
  74.9 1.0 add_convert_fusion
  75.9 0.8 broadcast_in_dim.15
  76.7 3.6 %all-to-all-start.2 = ((bf16[16,32,512]{2,1,0:T(8,128)(2,1)}), bf16[16,32,512]{2,1,0:T(8,128)(2,1)S(1)}, u32[]{:S(2)}, u32[]{:S(2)}) async-start(bf16[16,32,512]{2,1,0:T(8,128)(2,1)} %bitcast.11), calls=%async_computation.2 | async-start | bytes 1048576 | tf_op jit(solution)/shard_map/all_to_all | solution.py:268
  80.3 0.0 copy-start.1
  80.3 0.0 copy-start.8
  80.3 0.0 copy-start.6
  80.3 7.6 %shard_map.95 = (bf16[128,4096]{1,0:T(8,128)(2,1)}, bf16[128,4096]{1,0:T(8,128)(2,1)}, f32[2,128,512]{2,1,0:T(8,128)}) custom-call(s32[20]{0:T(128)} %copy-done, bf16[128,4096]{1,0:T(8,128)(2,1)} %query_ref.3, bf16[128,4096]{1,0:T(8,128)(2,1)} %grad_ref.3, bf16[2,128,512]{2,1,0:T(8,128)(2,1)} %bitcast.35, bf16[2,128,512]{2,1,0:T(8,128)(2,1)} %copy-done.7, ...), custom_call_target="tpu_custom_call" | custom-call | flops 1006632960 | bytes 10485760 | tf_op jit(solution)/shard_map/pallas_call | solution.py:184
  87.9 4.0 %all-to-all-done.2.held_ref = bf16[16,32,512]{2,1,0:T(8,128)(2,1)S(1)} async-done(((bf16[16,32,512]{2,1,0:T(8,128)(2,1)}), bf16[16,32,512]{2,1,0:T(8,128)(2,1)S(1)}, u32[]{:S(2)}, u32[]{:S(2)}) %all-to-all-start.2) | async-done | bytes 524320 | tf_op jit(solution)/shard_map/all_to_all | solution.py:268
  92.0 0.0 copy-done.1
  92.0 0.7 shard_map.96
  92.7 12.0 %collective-permute-start.5 = (bf16[4,32,512]{2,1,0:T(8,128)(2,1)S(1)}, bf16[4,32,512]{2,1,0:T(8,128)(2,1)S(1)}, u32[]{:S(2)}, u32[]{:S(2)}) collective-permute-start(bf16[4,32,512]{2,1,0:T(8,128)(2,1)S(1)} %get-tuple-element.39), channel_id=1, source_target_pairs={{0,32},{32,0},{1,33},{33,1},{2,34},{34,2},{3,35},{35,3},{4,36},{36... | collective-permute-start | bytes 393224 | tf_op jit(solution)/shard_map/ppermute | solution.py:272
  104.7 9.8 %collective-permute-done.5 = bf16[4,32,512]{2,1,0:T(8,128)(2,1)S(1)} collective-permute-done((bf16[4,32,512]{2,1,0:T(8,128)(2,1)S(1)}, bf16[4,32,512]{2,1,0:T(8,128)(2,1)S(1)}, u32[]{:S(2)}, u32[]{:S(2)}) %collective-permute-start.5) | collective-permute-done | bytes 131104 | tf_op jit(solution)/shard_map/ppermute | solution.py:272
  114.6 0.7 broadcast_in_dim.16
  115.3 3.5 %all-to-all-start.3 = ((bf16[8,32,512]{2,1,0:T(8,128)(2,1)}), bf16[8,32,512]{2,1,0:T(8,128)(2,1)S(1)}, u32[]{:S(2)}, u32[]{:S(2)}) async-start(bf16[8,32,512]{2,1,0:T(8,128)(2,1)} %bitcast.12), calls=%async_computation.3 | async-start | bytes 524288 | tf_op jit(solution)/shard_map/all_to_all | solution.py:268
  118.8 0.0 copy-done.8
  118.8 1.3 collective-permute-start.6
  120.1 0.0 copy-done.6
  120.2 1.3 collective-permute-start.7
  121.5 4.8 %all-to-all-done.3 = bf16[8,32,512]{2,1,0:T(8,128)(2,1)S(1)} async-done(((bf16[8,32,512]{2,1,0:T(8,128)(2,1)}), bf16[8,32,512]{2,1,0:T(8,128)(2,1)S(1)}, u32[]{:S(2)}, u32[]{:S(2)}) %all-to-all-start.3) | async-done | bytes 262176 | tf_op jit(solution)/shard_map/all_to_all | solution.py:268
  126.4 0.0 collective-permute-done.6
  126.4 6.4 %collective-permute-done.7 = bf16[2,128,512]{2,1,0:T(8,128)(2,1)S(1)} collective-permute-done((bf16[2,128,512]{2,1,0:T(8,128)(2,1)S(1)}, bf16[2,128,512]{2,1,0:T(8,128)(2,1)S(1)}, u32[]{:S(2)}, u32[]{:S(2)}) %collective-permute-start.7) | collective-permute-done | bytes 262176 | tf_op jit(solution)/shard_map/ppermute | solution.py:264
  132.7 0.0 copy-done.3
  132.7 0.1 convert_add_fusion
  132.8 0.8 fusion.4
  (9 shorter events, 0.1 us)
Async XLA Ops:
  2.4 12.6 %all-to-all-start = ((bf16[8,32,512]{2,1,0:T(8,128)(2,1)}), bf16[8,32,512]{2,1,0:T(8,128)(2,1)S(1)}, u32[]{:S(2)}, u32[]{:S(2)}) async-start(bf16[8,32,512]{2,1,0:T(8,128)(2,1)} %bitcast.6), calls=%async_computation | async-start | bytes 524288 | tf_op jit(solution)/shard_map/all_to_all | solution.py:268
  7.8 22.8 %collective-permute-start.2 = (bf16[2,128,512]{2,1,0:T(8,128)(2,1)}, bf16[2,128,512]{2,1,0:T(8,128)(2,1)S(1)}, u32[]{:S(2)}, u32[]{:S(2)}) collective-permute-start(bf16[2,128,512]{2,1,0:T(8,128)(2,1)} %pad_maximum_fusion.own_ref), channel_id=1, source_target_pairs={{0,2},{1,3},{4,6},{5,7},{8,10},{9,11},{12,14},{13,15},{16,18},{17,... | collective-permute-start | bytes 786440 | tf_op jit(solution)/shard_map/ppermute | solution.py:264
  11.7 18.9 %collective-permute-start.1 = (bf16[2,128,512]{2,1,0:T(8,128)(2,1)}, bf16[2,128,512]{2,1,0:T(8,128)(2,1)S(1)}, u32[]{:S(2)}, u32[]{:S(2)}) collective-permute-start(bf16[2,128,512]{2,1,0:T(8,128)(2,1)} %pad_maximum_fusion.own_ref), channel_id=1, source_target_pairs={{0,1},{1,2},{2,3},{4,5},{5,6},{6,7},{8,9},{9,10},{10,11},{12,13},{... | collective-permute-start | bytes 786440 | tf_op jit(solution)/shard_map/ppermute | solution.py:264
  15.0 24.7 %collective-permute-start = (bf16[4,32,512]{2,1,0:T(8,128)(2,1)S(1)}, bf16[4,32,512]{2,1,0:T(8,128)(2,1)S(1)}, u32[]{:S(2)}, u32[]{:S(2)}) collective-permute-start(bf16[4,32,512]{2,1,0:T(8,128)(2,1)S(1)} %slice.31.here_ref), channel_id=1, source_target_pairs={{0,32},{32,0},{1,33},{33,1},{2,34},{34,2},{3,35},{35,3},{4,36},{36... | collective-permute-start | bytes 393224 | tf_op jit(solution)/shard_map/ppermute | solution.py:272
  30.6 30.9 %copy-start = (s32[20]{0:T(128)}, s32[20]{0:T(128)S(1)}, u32[]{:S(2)}) copy-start(s32[20]{0:T(128)S(1)} %concatenate.3.info_ref) | copy-start | bytes 244
  30.6 30.9 %copy-start.4 = (bf16[2,128,512]{2,1,0:T(8,128)(2,1)}, bf16[2,128,512]{2,1,0:T(8,128)(2,1)S(1)}, u32[]{:S(2)}) copy-start(bf16[2,128,512]{2,1,0:T(8,128)(2,1)S(1)} %collective-permute-done.2.far_ref) | copy-start | bytes 786436
  30.6 30.8 %copy-start.5 = (bf16[2,128,512]{2,1,0:T(8,128)(2,1)}, bf16[2,128,512]{2,1,0:T(8,128)(2,1)S(1)}, u32[]{:S(2)}) copy-start(bf16[2,128,512]{2,1,0:T(8,128)(2,1)S(1)} %collective-permute-done.1.near_ref) | copy-start | bytes 786436
  58.0 3.5 %copy-start.2 = (bf16[2,4,1,32,512]{4,3,1,0,2:T(8,128)(2,1)}, bf16[2,4,1,32,512]{4,3,1,0,2:T(8,128)(2,1)S(1)}, u32[]{:S(2)}) copy-start(bf16[2,4,1,32,512]{4,3,1,0,2:T(8,128)(2,1)S(1)} %fusion.2) | copy-start | bytes 786436
  58.0 3.4 %collective-permute-start.3 = (bf16[2,128,512]{2,1,0:T(8,128)(2,1)S(1)}, bf16[2,128,512]{2,1,0:T(8,128)(2,1)S(1)}, u32[]{:S(2)}, u32[]{:S(2)}) collective-permute-start(bf16[2,128,512]{2,1,0:T(8,128)(2,1)S(1)} %bitcast.33), channel_id=1, source_target_pairs={{1,0},{5,4},{9,8},{13,12},{17,16},{21,20},{25,24},{29,28},{33,32},... | collective-permute-start | bytes 786440 | tf_op jit(solution)/shard_map/ppermute | solution.py:264
  61.4 0.7 copy-start.7
  71.5 3.4 %collective-permute-start.4 = (bf16[2,128,512]{2,1,0:T(8,128)(2,1)}, bf16[2,128,512]{2,1,0:T(8,128)(2,1)S(1)}, u32[]{:S(2)}, u32[]{:S(2)}) collective-permute-start(bf16[2,128,512]{2,1,0:T(8,128)(2,1)} %get-tuple-element.40), channel_id=1, source_target_pairs={{0,1},{4,5},{8,9},{12,13},{16,17},{20,21},{24,25},{28,29},{32,33},... | collective-permute-start | bytes 786440 | tf_op jit(solution)/shard_map/ppermute | solution.py:264
  76.7 15.2 %all-to-all-start.2 = ((bf16[16,32,512]{2,1,0:T(8,128)(2,1)}), bf16[16,32,512]{2,1,0:T(8,128)(2,1)S(1)}, u32[]{:S(2)}, u32[]{:S(2)}) async-start(bf16[16,32,512]{2,1,0:T(8,128)(2,1)} %bitcast.11), calls=%async_computation.2 | async-start | bytes 1048576 | tf_op jit(solution)/shard_map/all_to_all | solution.py:268
  80.3 11.7 %copy-start.1 = (s32[20]{0:T(128)S(1)}, s32[20]{0:T(128)}, u32[]{:S(2)}) copy-start(s32[20]{0:T(128)} %copy-done) | copy-start | bytes 244
  80.3 38.5 %copy-start.8 = (bf16[2,128,512]{2,1,0:T(8,128)(2,1)S(1)}, bf16[2,128,512]{2,1,0:T(8,128)(2,1)}, u32[]{:S(2)}) copy-start(bf16[2,128,512]{2,1,0:T(8,128)(2,1)} %get-tuple-element.40) | copy-start | bytes 786436
  80.3 39.8 %copy-start.6 = (bf16[2,128,512]{2,1,0:T(8,128)(2,1)S(1)}, bf16[2,128,512]{2,1,0:T(8,128)(2,1)}, u32[]{:S(2)}) copy-start(bf16[2,128,512]{2,1,0:T(8,128)(2,1)} %get-tuple-element.41) | copy-start | bytes 786436
  87.9 44.8 %copy-start.3 = (f32[2,128,512]{2,1,0:T(8,128)S(1)}, f32[2,128,512]{2,1,0:T(8,128)}, u32[]{:S(2)}) copy-start(f32[2,128,512]{2,1,0:T(8,128)} %get-tuple-element.37) | copy-start | bytes 1572868
  92.7 21.8 %collective-permute-start.5 = (bf16[4,32,512]{2,1,0:T(8,128)(2,1)S(1)}, bf16[4,32,512]{2,1,0:T(8,128)(2,1)S(1)}, u32[]{:S(2)}, u32[]{:S(2)}) collective-permute-start(bf16[4,32,512]{2,1,0:T(8,128)(2,1)S(1)} %get-tuple-element.39), channel_id=1, source_target_pairs={{0,32},{32,0},{1,33},{33,1},{2,34},{34,2},{3,35},{35,3},{4,36},{36... | collective-permute-start | bytes 393224 | tf_op jit(solution)/shard_map/ppermute | solution.py:272
  115.3 11.0 %all-to-all-start.3 = ((bf16[8,32,512]{2,1,0:T(8,128)(2,1)}), bf16[8,32,512]{2,1,0:T(8,128)(2,1)S(1)}, u32[]{:S(2)}, u32[]{:S(2)}) async-start(bf16[8,32,512]{2,1,0:T(8,128)(2,1)} %bitcast.12), calls=%async_computation.3 | async-start | bytes 524288 | tf_op jit(solution)/shard_map/all_to_all | solution.py:268
  118.8 7.5 %collective-permute-start.6 = (bf16[2,128,512]{2,1,0:T(8,128)(2,1)S(1)}, bf16[2,128,512]{2,1,0:T(8,128)(2,1)S(1)}, u32[]{:S(2)}, u32[]{:S(2)}) collective-permute-start(bf16[2,128,512]{2,1,0:T(8,128)(2,1)S(1)} %copy-done.8), channel_id=1, source_target_pairs={{1,0},{2,1},{3,2},{5,4},{6,5},{7,6},{9,8},{10,9},{11,10},{13,12},{... | collective-permute-start | bytes 786440 | tf_op jit(solution)/shard_map/ppermute | solution.py:264
  120.2 12.6 %collective-permute-start.7 = (bf16[2,128,512]{2,1,0:T(8,128)(2,1)S(1)}, bf16[2,128,512]{2,1,0:T(8,128)(2,1)S(1)}, u32[]{:S(2)}, u32[]{:S(2)}) collective-permute-start(bf16[2,128,512]{2,1,0:T(8,128)(2,1)S(1)} %copy-done.6), channel_id=1, source_target_pairs={{2,0},{3,1},{6,4},{7,5},{10,8},{11,9},{14,12},{15,13},{18,16},{19,... | collective-permute-start | bytes 786440 | tf_op jit(solution)/shard_map/ppermute | solution.py:264

commit v10 on v6

--- a/solution.py
+++ b/solution.py
@@ -168,7 +168,7 @@
             scratch_shapes=[pltpu.VMEM((WINDOW, 2 * CHUNK), jnp.float32)],
         ),
         out_shape=[held, held, half, half],
-        compiler_params=pltpu.CompilerParams(vmem_limit_bytes=58 * 1024 * 1024),
+        compiler_params=pltpu.CompilerParams(vmem_limit_bytes=55 * 1024 * 1024),
         cost_estimate=pl.CostEstimate(
             flops=7 * rows * QUERY_HEADS * WINDOW * HEAD_SIZE,
             bytes_accessed=16 * rows * QUERY_HEADS * HEAD_SIZE,
@@ -190,7 +190,7 @@
             out_specs=[wide, wide, pair],
         ),
         out_shape=[like, like, jax.ShapeDtypeStruct((2, rows, KV_WIDTH), jnp.float32)],
-        compiler_params=pltpu.CompilerParams(vmem_limit_bytes=58 * 1024 * 1024),
+        compiler_params=pltpu.CompilerParams(vmem_limit_bytes=55 * 1024 * 1024),
         cost_estimate=pl.CostEstimate(
             flops=5 * rows * QUERY_HEADS * WINDOW * HEAD_SIZE,
             bytes_accessed=20 * rows * QUERY_HEADS * HEAD_SIZE,

time: 132 us -> 132 us (level)
  no operation moved by 1% of the time
where the time goes in v10:
time: 132 us; the launch traced here: 131 us
  starting transfers between devices  53.7 us (41%)
  waiting for transfers between devices  33 us (25%)
  Pallas kernels  18.4 us (14%)
  blocking collectives  17.4 us (13%)
  other arithmetic  4.78 us (4%)
  local copies, waits for them, and re-layouts  3.06 us (2%)
    ppermute x2, starting transfers between devices, across(): return lax.ppermute(value, 'z', [(0, 1), (1, 0)])  26.8 us
    ppermute x2, waiting for transfers between devices, across(): return lax.ppermute(value, 'z', [(0, 1), (1, 0)])  19.7 us
    all_to_all x1, blocking collectives, exchange(): return lax.all_to_all(pieces, axes, 0, 0)  17.4 us
    all_to_all x3, starting transfers between devices, exchange(): return lax.all_to_all(pieces, axes, 0, 0)  15.7 us
    ppermute x6, starting transfers between devices, move(): return lax.ppermute(value, BLOCK_AXES, moves)  11.2 us
    all_to_all x3, waiting for transfers between devices, exchange(): return lax.all_to_all(pieces, axes, 0, 0)  9.79 us
    pallas_call x1, Pallas kernels, scores_and_halo(): pl.pallas_call(score_kernel, grid_spec=pltpu.PrefetchScalarGridSpec(num_s...  9.37 us
    pallas_call x1, Pallas kernels, outputs_and_own(): pl.pallas_call(output_kernel, grid_spec=pltpu.PrefetchScalarGridSpec(num_...  7.47 us
  transfers between devices with their start and end apart: 11, of which 7 were waited for; matrix products, arithmetic and copies ran while one was open for 2% of the time, Pallas kernels for 6%

profile of v10, /device:TPU:32, one launch (start us, length us, event | category | flops | bytes accessed | tf_op | source)
XLA Modules:
  0.0 131.1 jit_solution(15292761174022123630)
XLA Ops:
  0.6 1.8 %pad_maximum_fusion.own_ref = bf16[2,128,512]{2,1,0:T(8,128)(2,1)} fusion(bf16[1,128,512]{2,1,0:T(8,128)(2,1)} %bitcast.39, bf16[1,128,512]{2,1,0:T(8,128)(2,1)} %bitcast.40), kind=kLoop, calls=%fused_computation.9 | loop fusion | flops 131072 | bytes 524288 | tf_op jit(solution)/shard_map/stack | solution.py:283
  2.4 5.4 %all-to-all-start = ((bf16[8,32,512]{2,1,0:T(8,128)(2,1)}), bf16[8,32,512]{2,1,0:T(8,128)(2,1)S(1)}, u32[]{:S(2)}, u32[]{:S(2)}) async-start(bf16[8,32,512]{2,1,0:T(8,128)(2,1)} %bitcast.6), calls=%async_computation | async-start | bytes 524288 | tf_op jit(solution)/shard_map/all_to_all | solution.py:268
  7.8 3.9 %collective-permute-start.2 = (bf16[2,128,512]{2,1,0:T(8,128)(2,1)}, bf16[2,128,512]{2,1,0:T(8,128)(2,1)S(1)}, u32[]{:S(2)}, u32[]{:S(2)}) collective-permute-start(bf16[2,128,512]{2,1,0:T(8,128)(2,1)} %pad_maximum_fusion.own_ref), channel_id=1, source_target_pairs={{0,2},{1,3},{4,6},{5,7},{8,10},{9,11},{12,14},{13,15},{16,18},{17,... | collective-permute-start | bytes 786440 | tf_op jit(solution)/shard_map/ppermute | solution.py:264
  11.7 1.3 collective-permute-start.1
  13.0 2.0 %all-to-all-done = bf16[8,32,512]{2,1,0:T(8,128)(2,1)S(1)} async-done(((bf16[8,32,512]{2,1,0:T(8,128)(2,1)}), bf16[8,32,512]{2,1,0:T(8,128)(2,1)S(1)}, u32[]{:S(2)}, u32[]{:S(2)}) %all-to-all-start) | async-done | bytes 262176 | tf_op jit(solution)/shard_map/all_to_all | solution.py:268
  15.0 14.8 %collective-permute-start = (bf16[4,32,512]{2,1,0:T(8,128)(2,1)S(1)}, bf16[4,32,512]{2,1,0:T(8,128)(2,1)S(1)}, u32[]{:S(2)}, u32[]{:S(2)}) collective-permute-start(bf16[4,32,512]{2,1,0:T(8,128)(2,1)S(1)} %slice.31.here_ref), channel_id=1, source_target_pairs={{0,32},{32,0},{1,33},{33,1},{2,34},{34,2},{3,35},{35,3},{4,36},{36... | collective-permute-start | bytes 393224 | tf_op jit(solution)/shard_map/ppermute | solution.py:272
  29.9 0.7 concatenate.3.info_ref
  30.6 0.0 copy-start
  30.6 0.0 collective-permute-done.2.far_ref
  30.6 0.0 copy-start.3
  30.6 0.0 collective-permute-done.1.near_ref
  30.6 0.0 copy-start.4
  30.6 9.1 %collective-permute-done.there_ref = bf16[4,32,512]{2,1,0:T(8,128)(2,1)S(1)} collective-permute-done((bf16[4,32,512]{2,1,0:T(8,128)(2,1)S(1)}, bf16[4,32,512]{2,1,0:T(8,128)(2,1)S(1)}, u32[]{:S(2)}, u32[]{:S(2)}) %collective-permute-start) | collective-permute-done | bytes 131104 | tf_op jit(solution)/shard_map/ppermute | solution.py:272
  39.8 0.8 shard_map.93
  40.6 17.4 %all_to_all.20 = bf16[16,32,512]{2,1,0:T(8,128)(2,1)S(1)} all-to-all(bf16[16,32,512]{2,1,0:T(8,128)(2,1)S(1)} %shard_map.93), channel_id=1, replica_groups=mesh['dp'=8,'z'=2,'y'=4,'b'=2,'x'=2,'core'=2] {'x','y','b'}, dimensions={0} | all-to-all | bytes 1048576 | tf_op jit(solution)/shard_map/all_to_all | solution.py:268
  58.0 0.0 copy-start.2
  58.0 1.3 collective-permute-start.3
  59.3 2.1 %collective-permute-done.3.before_ref = bf16[2,128,512]{2,1,0:T(8,128)(2,1)S(1)} collective-permute-done((bf16[2,128,512]{2,1,0:T(8,128)(2,1)S(1)}, bf16[2,128,512]{2,1,0:T(8,128)(2,1)S(1)}, u32[]{:S(2)}, u32[]{:S(2)}) %collective-permute-start.3) | collective-permute-done | bytes 262176 | tf_op jit(solution)/shard_map/ppermute | solution.py:264
  61.5 0.0 copy-start.5
  61.5 0.0 copy-done
  61.5 0.0 copy-done.3
  61.5 0.0 copy-done.4
  61.5 0.0 copy-done.2
  61.5 0.7 copy-done.5
  62.2 9.4 %shard_map.94 = (bf16[384,4096]{1,0:T(8,128)(2,1)}, bf16[384,4096]{1,0:T(8,128)(2,1)}, bf16[2,128,512]{2,1,0:T(8,128)(2,1)}, bf16[2,128,512]{2,1,0:T(8,128)(2,1)}) custom-call(s32[20]{0:T(128)} %copy-done, s32[64,128]{1,0:T(8,128)} %bitcast.41, bf16[128,4096]{1,0:T(8,128)(2,1)} %query_ref.3, bf16[128,4096]{1,0:T(8,128)(2,1)} %grad_ref.3, ...), custom_call_target="tpu_custom_call" | custom-call | flops 1409286144 | bytes 8388608 | tf_op jit(solution)/shard_map/pallas_call | solution.py:161
  71.5 2.0 %collective-permute-start.4 = (bf16[2,128,512]{2,1,0:T(8,128)(2,1)}, bf16[2,128,512]{2,1,0:T(8,128)(2,1)S(1)}, u32[]{:S(2)}, u32[]{:S(2)}) collective-permute-start(bf16[2,128,512]{2,1,0:T(8,128)(2,1)} %get-tuple-element.25), channel_id=1, source_target_pairs={{0,1},{4,5},{8,9},{12,13},{16,17},{20,21},{24,25},{28,29},{32,33},... | collective-permute-start | bytes 786440 | tf_op jit(solution)/shard_map/ppermute | solution.py:264
  73.6 1.3 %collective-permute-done.4 = bf16[2,128,512]{2,1,0:T(8,128)(2,1)S(1)} collective-permute-done((bf16[2,128,512]{2,1,0:T(8,128)(2,1)}, bf16[2,128,512]{2,1,0:T(8,128)(2,1)S(1)}, u32[]{:S(2)}, u32[]{:S(2)}) %collective-permute-start.4) | collective-permute-done | bytes 262176 | tf_op jit(solution)/shard_map/ppermute | solution.py:264
  74.9 1.0 add_convert_fusion
  76.0 0.8 broadcast_in_dim.15
  76.8 3.6 %all-to-all-start.2 = ((bf16[16,32,512]{2,1,0:T(8,128)(2,1)}), bf16[16,32,512]{2,1,0:T(8,128)(2,1)S(1)}, u32[]{:S(2)}, u32[]{:S(2)}) async-start(bf16[16,32,512]{2,1,0:T(8,128)(2,1)} %bitcast.11), calls=%async_computation.2 | async-start | bytes 1048576 | tf_op jit(solution)/shard_map/all_to_all | solution.py:268
  80.4 0.0 copy-start.1
  80.4 1.3 collective-permute-start.6
  81.7 1.3 collective-permute-start.5
  83.0 7.5 %shard_map.95 = (bf16[128,4096]{1,0:T(8,128)(2,1)}, bf16[128,4096]{1,0:T(8,128)(2,1)}, f32[2,128,512]{2,1,0:T(8,128)}) custom-call(s32[20]{0:T(128)} %copy-done, bf16[128,4096]{1,0:T(8,128)(2,1)} %query_ref.3, bf16[128,4096]{1,0:T(8,128)(2,1)} %grad_ref.3, bf16[2,128,512]{2,1,0:T(8,128)(2,1)} %bitcast.35, bf16[2,128,512]{2,1,0:T(8,128)(2,1)} %copy-done.5, ...), custom_call_target="tpu_custom_call" | custom-call | flops 1006632960 | bytes 10485760 | tf_op jit(solution)/shard_map/pallas_call | solution.py:184
  90.5 1.6 %all-to-all-done.2.held_ref = bf16[16,32,512]{2,1,0:T(8,128)(2,1)S(1)} async-done(((bf16[16,32,512]{2,1,0:T(8,128)(2,1)}), bf16[16,32,512]{2,1,0:T(8,128)(2,1)S(1)}, u32[]{:S(2)}, u32[]{:S(2)}) %all-to-all-start.2) | async-done | bytes 524320 | tf_op jit(solution)/shard_map/all_to_all | solution.py:268
  92.0 0.0 copy-done.1
  92.0 0.7 shard_map.96
  92.8 12.0 %collective-permute-start.7 = (bf16[4,32,512]{2,1,0:T(8,128)(2,1)S(1)}, bf16[4,32,512]{2,1,0:T(8,128)(2,1)S(1)}, u32[]{:S(2)}, u32[]{:S(2)}) collective-permute-start(bf16[4,32,512]{2,1,0:T(8,128)(2,1)S(1)} %get-tuple-element.37), channel_id=1, source_target_pairs={{0,32},{32,0},{1,33},{33,1},{2,34},{34,2},{3,35},{35,3},{4,36},{36... | collective-permute-start | bytes 393224 | tf_op jit(solution)/shard_map/ppermute | solution.py:272
  104.8 10.6 %collective-permute-done.7 = bf16[4,32,512]{2,1,0:T(8,128)(2,1)S(1)} collective-permute-done((bf16[4,32,512]{2,1,0:T(8,128)(2,1)S(1)}, bf16[4,32,512]{2,1,0:T(8,128)(2,1)S(1)}, u32[]{:S(2)}, u32[]{:S(2)}) %collective-permute-start.7) | collective-permute-done | bytes 131104 | tf_op jit(solution)/shard_map/ppermute | solution.py:272
  115.4 0.7 broadcast_in_dim.16
  116.2 6.7 %all-to-all-start.3 = ((bf16[8,32,512]{2,1,0:T(8,128)(2,1)}), bf16[8,32,512]{2,1,0:T(8,128)(2,1)S(1)}, u32[]{:S(2)}, u32[]{:S(2)}) async-start(bf16[8,32,512]{2,1,0:T(8,128)(2,1)} %bitcast.12), calls=%async_computation.3 | async-start | bytes 524288 | tf_op jit(solution)/shard_map/all_to_all | solution.py:268
  122.9 0.0 collective-permute-done.6
  122.9 0.0 collective-permute-done.5
  122.9 1.1 convert_add_fusion
  124.1 6.2 %all-to-all-done.3 = bf16[8,32,512]{2,1,0:T(8,128)(2,1)S(1)} async-done(((bf16[8,32,512]{2,1,0:T(8,128)(2,1)}), bf16[8,32,512]{2,1,0:T(8,128)(2,1)S(1)}, u32[]{:S(2)}, u32[]{:S(2)}) %all-to-all-start.3) | async-done | bytes 262176 | tf_op jit(solution)/shard_map/all_to_all | solution.py:268
  130.4 0.8 fusion.4
  (5 shorter events, 0.1 us)
Async XLA Ops:
  2.4 12.6 %all-to-all-start = ((bf16[8,32,512]{2,1,0:T(8,128)(2,1)}), bf16[8,32,512]{2,1,0:T(8,128)(2,1)S(1)}, u32[]{:S(2)}, u32[]{:S(2)}) async-start(bf16[8,32,512]{2,1,0:T(8,128)(2,1)} %bitcast.6), calls=%async_computation | async-start | bytes 524288 | tf_op jit(solution)/shard_map/all_to_all | solution.py:268
  7.8 22.8 %collective-permute-start.2 = (bf16[2,128,512]{2,1,0:T(8,128)(2,1)}, bf16[2,128,512]{2,1,0:T(8,128)(2,1)S(1)}, u32[]{:S(2)}, u32[]{:S(2)}) collective-permute-start(bf16[2,128,512]{2,1,0:T(8,128)(2,1)} %pad_maximum_fusion.own_ref), channel_id=1, source_target_pairs={{0,2},{1,3},{4,6},{5,7},{8,10},{9,11},{12,14},{13,15},{16,18},{17,... | collective-permute-start | bytes 786440 | tf_op jit(solution)/shard_map/ppermute | solution.py:264
  11.7 18.9 %collective-permute-start.1 = (bf16[2,128,512]{2,1,0:T(8,128)(2,1)}, bf16[2,128,512]{2,1,0:T(8,128)(2,1)S(1)}, u32[]{:S(2)}, u32[]{:S(2)}) collective-permute-start(bf16[2,128,512]{2,1,0:T(8,128)(2,1)} %pad_maximum_fusion.own_ref), channel_id=1, source_target_pairs={{0,1},{1,2},{2,3},{4,5},{5,6},{6,7},{8,9},{9,10},{10,11},{12,13},{... | collective-permute-start | bytes 786440 | tf_op jit(solution)/shard_map/ppermute | solution.py:264
  15.0 24.7 %collective-permute-start = (bf16[4,32,512]{2,1,0:T(8,128)(2,1)S(1)}, bf16[4,32,512]{2,1,0:T(8,128)(2,1)S(1)}, u32[]{:S(2)}, u32[]{:S(2)}) collective-permute-start(bf16[4,32,512]{2,1,0:T(8,128)(2,1)S(1)} %slice.31.here_ref), channel_id=1, source_target_pairs={{0,32},{32,0},{1,33},{33,1},{2,34},{34,2},{3,35},{35,3},{4,36},{36... | collective-permute-start | bytes 393224 | tf_op jit(solution)/shard_map/ppermute | solution.py:272
  30.6 30.9 %copy-start = (s32[20]{0:T(128)}, s32[20]{0:T(128)S(1)}, u32[]{:S(2)}) copy-start(s32[20]{0:T(128)S(1)} %concatenate.3.info_ref) | copy-start | bytes 244
  30.6 30.9 %copy-start.3 = (bf16[2,128,512]{2,1,0:T(8,128)(2,1)}, bf16[2,128,512]{2,1,0:T(8,128)(2,1)S(1)}, u32[]{:S(2)}) copy-start(bf16[2,128,512]{2,1,0:T(8,128)(2,1)S(1)} %collective-permute-done.2.far_ref) | copy-start | bytes 786436
  30.6 30.8 %copy-start.4 = (bf16[2,128,512]{2,1,0:T(8,128)(2,1)}, bf16[2,128,512]{2,1,0:T(8,128)(2,1)S(1)}, u32[]{:S(2)}) copy-start(bf16[2,128,512]{2,1,0:T(8,128)(2,1)S(1)} %collective-permute-done.1.near_ref) | copy-start | bytes 786436
  58.0 3.5 %copy-start.2 = (bf16[2,4,1,32,512]{4,3,1,0,2:T(8,128)(2,1)}, bf16[2,4,1,32,512]{4,3,1,0,2:T(8,128)(2,1)S(1)}, u32[]{:S(2)}) copy-start(bf16[2,4,1,32,512]{4,3,1,0,2:T(8,128)(2,1)S(1)} %fusion.2) | copy-start | bytes 786436
  58.0 3.4 %collective-permute-start.3 = (bf16[2,128,512]{2,1,0:T(8,128)(2,1)S(1)}, bf16[2,128,512]{2,1,0:T(8,128)(2,1)S(1)}, u32[]{:S(2)}, u32[]{:S(2)}) collective-permute-start(bf16[2,128,512]{2,1,0:T(8,128)(2,1)S(1)} %bitcast.33), channel_id=1, source_target_pairs={{1,0},{5,4},{9,8},{13,12},{17,16},{21,20},{25,24},{29,28},{33,32},... | collective-permute-start | bytes 786440 | tf_op jit(solution)/shard_map/ppermute | solution.py:264
  61.5 0.7 copy-start.5
  71.5 3.4 %collective-permute-start.4 = (bf16[2,128,512]{2,1,0:T(8,128)(2,1)}, bf16[2,128,512]{2,1,0:T(8,128)(2,1)S(1)}, u32[]{:S(2)}, u32[]{:S(2)}) collective-permute-start(bf16[2,128,512]{2,1,0:T(8,128)(2,1)} %get-tuple-element.25), channel_id=1, source_target_pairs={{0,1},{4,5},{8,9},{12,13},{16,17},{20,21},{24,25},{28,29},{32,33},... | collective-permute-start | bytes 786440 | tf_op jit(solution)/shard_map/ppermute | solution.py:264
  76.8 15.2 %all-to-all-start.2 = ((bf16[16,32,512]{2,1,0:T(8,128)(2,1)}), bf16[16,32,512]{2,1,0:T(8,128)(2,1)S(1)}, u32[]{:S(2)}, u32[]{:S(2)}) async-start(bf16[16,32,512]{2,1,0:T(8,128)(2,1)} %bitcast.11), calls=%async_computation.2 | async-start | bytes 1048576 | tf_op jit(solution)/shard_map/all_to_all | solution.py:268
  80.4 11.7 %copy-start.1 = (s32[20]{0:T(128)S(1)}, s32[20]{0:T(128)}, u32[]{:S(2)}) copy-start(s32[20]{0:T(128)} %copy-done) | copy-start | bytes 244
  80.4 42.5 %collective-permute-start.6 = (bf16[2,128,512]{2,1,0:T(8,128)(2,1)}, bf16[2,128,512]{2,1,0:T(8,128)(2,1)S(1)}, u32[]{:S(2)}, u32[]{:S(2)}) collective-permute-start(bf16[2,128,512]{2,1,0:T(8,128)(2,1)} %get-tuple-element.24), channel_id=1, source_target_pairs={{2,0},{3,1},{6,4},{7,5},{10,8},{11,9},{14,12},{15,13},{18,16},{19,... | collective-permute-start | bytes 786440 | tf_op jit(solution)/shard_map/ppermute | solution.py:264
  81.7 41.2 %collective-permute-start.5 = (bf16[2,128,512]{2,1,0:T(8,128)(2,1)}, bf16[2,128,512]{2,1,0:T(8,128)(2,1)S(1)}, u32[]{:S(2)}, u32[]{:S(2)}) collective-permute-start(bf16[2,128,512]{2,1,0:T(8,128)(2,1)} %get-tuple-element.25), channel_id=1, source_target_pairs={{1,0},{2,1},{3,2},{5,4},{6,5},{7,6},{9,8},{10,9},{11,10},{13,12},{... | collective-permute-start | bytes 786440 | tf_op jit(solution)/shard_map/ppermute | solution.py:264
  92.8 22.6 %collective-permute-start.7 = (bf16[4,32,512]{2,1,0:T(8,128)(2,1)S(1)}, bf16[4,32,512]{2,1,0:T(8,128)(2,1)S(1)}, u32[]{:S(2)}, u32[]{:S(2)}) collective-permute-start(bf16[4,32,512]{2,1,0:T(8,128)(2,1)S(1)} %get-tuple-element.37), channel_id=1, source_target_pairs={{0,32},{32,0},{1,33},{33,1},{2,34},{34,2},{3,35},{35,3},{4,36},{36... | collective-permute-start | bytes 393224 | tf_op jit(solution)/shard_map/ppermute | solution.py:272
  116.2 14.1 %all-to-all-start.3 = ((bf16[8,32,512]{2,1,0:T(8,128)(2,1)}), bf16[8,32,512]{2,1,0:T(8,128)(2,1)S(1)}, u32[]{:S(2)}, u32[]{:S(2)}) async-start(bf16[8,32,512]{2,1,0:T(8,128)(2,1)} %bitcast.12), calls=%async_computation.3 | async-start | bytes 524288 | tf_op jit(solution)/shard_map/all_to_all | solution.py:268
